TPU v7x, 32 devices: a whole 2x2x4 slice. The times are simulated.
32 devices in a mesh: dp: 8 (over z, y), shard: 4 (over x, core).
Axes of the slice: x: 2, y: 2, z: 4, core: 2. Of those that a mesh axis runs over, the one named last changes fastest.
Arguments:
- hidden: bfloat16 [64, 512, 768], P(('dp', 'shard')), may hold values from -6 to 6
- pair_lengths: int32 [64, 8], P(('dp', 'shard')), may hold values from 1 to 128, 512 in all within a row
- cotangent: bfloat16 [64, 512, 768], P(('dp', 'shard')), may hold values from -6 to 6
- query_weight: bfloat16 [768, 768], P(('dp', 'shard')), may hold values from -0.21875 to 0.21875
- query_bias: bfloat16 [768], P(('dp', 'shard')), may hold values from -3 to 3
- key_weight: bfloat16 [768, 768], P(('dp', 'shard')), may hold values from -0.21875 to 0.21875
- value_weight: bfloat16 [768, 768], P(('dp', 'shard')), may hold values from -0.21875 to 0.21875
- value_bias: bfloat16 [768], P(('dp', 'shard')), may hold values from -3 to 3
- out_weight: bfloat16 [768, 768], P(('dp', 'shard')), may hold values from -1.25 to 1.25
- out_bias: bfloat16 [768], P(('dp', 'shard')), may hold values from -3 to 3
- attn_gain: bfloat16 [768], P(('dp', 'shard')), may hold values from 0.099609375 to 1.8984375
- attn_shift: bfloat16 [768], P(('dp', 'shard')), may hold values from -3 to 3
- up_weight: bfloat16 [768, 3072], P(('dp', 'shard')), may hold values from -0.21875 to 0.21875
- up_bias: bfloat16 [3072], P(('dp', 'shard')), may hold values from -3 to 3
- down_weight: bfloat16 [3072, 768], P(('dp', 'shard')), may hold values from -0.109375 to 0.109375
- down_bias: bfloat16 [768], P(('dp', 'shard')), may hold values from -3 to 3
- final_gain: bfloat16 [768], P(('dp', 'shard')), may hold values from 0.099609375 to 1.8984375
- final_shift: bfloat16 [768], P(('dp', 'shard')), may hold values from -3 to 3
Outputs:
- layer_out: bfloat16 [64, 512, 768], P(('dp', 'shard'))
- grad_hidden: float32 [64, 512, 768], P(('dp', 'shard'))
- grad_query_weight: float32 [768, 768], P(('dp', 'shard'))
- grad_query_bias: float32 [768], P(('dp', 'shard'))
- grad_key_weight: float32 [768, 768], P(('dp', 'shard'))
- grad_value_weight: float32 [768, 768], P(('dp', 'shard'))
- grad_value_bias: float32 [768], P(('dp', 'shard'))
- grad_out_weight: float32 [768, 768], P(('dp', 'shard'))
- grad_out_bias: float32 [768], P(('dp', 'shard'))
- grad_attn_gain: float32 [768], P(('dp', 'shard'))
- grad_attn_shift: float32 [768], P(('dp', 'shard'))
- grad_up_weight: float32 [768, 3072], P(('dp', 'shard'))
- grad_up_bias: float32 [3072], P(('dp', 'shard'))
- grad_down_weight: float32 [3072, 768], P(('dp', 'shard'))
- grad_down_bias: float32 [768], P(('dp', 'shard'))
- grad_final_gain: float32 [768], P(('dp', 'shard'))
- grad_final_shift: float32 [768], P(('dp', 'shard'))
Inputs may be any that keep to these rules, and one draw needn't show every extreme that they name: `pair_lengths`: the 8 pair lengths of a row sum to 512, and every row has a pair of exactly 128 tokens.
All inputs are finite; a program needn't handle non-finite values.
Results may differ from a plain program's by a relative error of at most 0.013.
Values may be sent and summed in bfloat16 or wider, within the bound.
No kernel may reach another device: no remote copies, remote signals or barrier semaphores. Data moves between devices by JAX's collectives and lax.ppermute only.
A program may use at most 192 MiB of HBM per device.

v0:
```python
import jax
import jax.numpy as jnp
from jax import lax
from jax.sharding import PartitionSpec as P

HEADS = 12


EPSILON = 1e-06
SQRT_HALF = 0.7071067811865476
INV_ROOT = 0.3989422804014327
score_scale = 0.125


def matmul(left, right):
    return jnp.dot(left, right, preferred_element_type=jnp.float32)


def outer_sum(left, right):
    return jnp.einsum("ta,tb->ab", left, right, preferred_element_type=jnp.float32)


def back_product(grads, weights):
    return jnp.einsum("tb,ab->ta", grads, weights, preferred_element_type=jnp.float32)


def normalize(rows):
    centred = rows - jnp.mean(rows, -1, keepdims=True)
    inverse = lax.rsqrt(jnp.mean(centred * centred, -1, keepdims=True) + EPSILON)
    return (centred * inverse, inverse)


def norm_back(grad_rows, normed, inverse, gain):
    grad_norm = grad_rows * gain
    return inverse * (
        grad_norm
        - jnp.mean(grad_norm, -1, keepdims=True)
        - normed * jnp.mean(grad_norm * normed, -1, keepdims=True)
    )


def doc_mask(pair_lens, size):
    pair_ends = jnp.cumsum(pair_lens)
    positions = jnp.arange(size, dtype=jnp.int32)
    doc_index = jnp.sum((positions[:, None] >= pair_ends[None, :]).astype(jnp.int32), -1)
    return doc_index[:, None] == doc_index[None, :]


def split_heads(rows):
    return rows.reshape(rows.shape[0], HEADS, rows.shape[1] // HEADS)


def scores_of(query_heads, key_heads, pair_lens):
    scores = (
        jnp.einsum("qhd,khd->hqk", query_heads, key_heads, preferred_element_type=jnp.float32)
        * score_scale
    )
    return jnp.where(doc_mask(pair_lens, query_heads.shape[0])[None], scores, -1e30)


def attend(packed):
    query_rows, key_rows, value_rows, pair_lens = packed
    scores = scores_of(split_heads(query_rows), split_heads(key_rows), pair_lens)
    row_max = jnp.max(scores, -1, keepdims=True)
    exp_scores = jnp.exp(scores - row_max)
    totals = jnp.sum(exp_scores, -1, keepdims=True)
    attn_probs = exp_scores / totals
    mixed = jnp.einsum(
        "hqk,khd->qhd",
        attn_probs.astype(jnp.bfloat16),
        split_heads(value_rows),
        preferred_element_type=jnp.float32,
    )
    log_total = (row_max + jnp.log(totals))[..., 0]
    return (mixed.reshape(query_rows.shape).astype(jnp.bfloat16), log_total)


def attend_back(packed):
    query_rows, key_rows, value_rows, pair_lens, log_total, grad_rows = packed
    query_heads = split_heads(query_rows)
    key_heads = split_heads(key_rows)
    grad_heads = split_heads(grad_rows)
    scores = scores_of(query_heads, key_heads, pair_lens)
    attn_probs = jnp.exp(scores - log_total[..., None])
    grad_values = jnp.einsum(
        "hqk,qhd->khd",
        attn_probs.astype(jnp.bfloat16),
        grad_heads,
        preferred_element_type=jnp.float32,
    )
    grad_probs = jnp.einsum(
        "qhd,khd->hqk", grad_heads, split_heads(value_rows), preferred_element_type=jnp.float32
    )
    centre = jnp.sum(grad_probs * attn_probs, -1, keepdims=True)
    grad_scores = (attn_probs * (grad_probs - centre)).astype(jnp.bfloat16)
    grad_queries = (
        jnp.einsum("hqk,khd->qhd", grad_scores, key_heads, preferred_element_type=jnp.float32)
        * score_scale
    )
    grad_keys = (
        jnp.einsum("hqk,qhd->khd", grad_scores, query_heads, preferred_element_type=jnp.float32)
        * score_scale
    )
    row_shape = query_rows.shape
    return (
        grad_queries.reshape(row_shape).astype(jnp.bfloat16),
        grad_keys.reshape(row_shape).astype(jnp.bfloat16),
        grad_values.reshape(row_shape).astype(jnp.bfloat16),
    )


def per_device(
    hidden,
    pair_lengths,
    cotangent,
    query_weight,
    query_bias,
    key_weight,
    value_weight,
    value_bias,
    out_weight,
    out_bias,
    attn_gain,
    attn_shift,
    up_weight,
    up_bias,
    down_weight,
    down_bias,
    final_gain,
    final_shift,
):
    rows_here, length, width = hidden.shape
    count = rows_here * length
    attn_full = (
        lax.all_gather(query_weight, ("dp", "shard"), axis=0, tiled=True),
        lax.all_gather(query_bias, ("dp", "shard"), axis=0, tiled=True),
        lax.all_gather(key_weight, ("dp", "shard"), axis=0, tiled=True),
        lax.all_gather(value_weight, ("dp", "shard"), axis=0, tiled=True),
        lax.all_gather(value_bias, ("dp", "shard"), axis=0, tiled=True),
        lax.all_gather(out_weight, ("dp", "shard"), axis=0, tiled=True),
        lax.all_gather(out_bias, ("dp", "shard"), axis=0, tiled=True),
        lax.all_gather(attn_gain, ("dp", "shard"), axis=0, tiled=True),
        lax.all_gather(attn_shift, ("dp", "shard"), axis=0, tiled=True),
    )
    ffn_full = (
        lax.all_gather(up_weight, ("dp", "shard"), axis=0, tiled=True),
        lax.all_gather(up_bias, ("dp", "shard"), axis=0, tiled=True),
        lax.all_gather(down_weight, ("dp", "shard"), axis=0, tiled=True),
        lax.all_gather(down_bias, ("dp", "shard"), axis=0, tiled=True),
        lax.all_gather(final_gain, ("dp", "shard"), axis=0, tiled=True),
        lax.all_gather(final_shift, ("dp", "shard"), axis=0, tiled=True),
    )
    (
        query_mat,
        query_add,
        key_mat,
        value_mat,
        value_add,
        out_mat,
        out_add,
        first_gain,
        first_shift,
    ) = attn_full
    up_mat, up_add, down_mat, down_add, second_gain, second_shift = ffn_full
    tokens = hidden.reshape(count, width)
    queries = (matmul(tokens, query_mat) + query_add.astype(jnp.float32)).astype(jnp.bfloat16)
    keys_all = matmul(tokens, key_mat).astype(jnp.bfloat16)
    values_all = (matmul(tokens, value_mat) + value_add.astype(jnp.float32)).astype(jnp.bfloat16)
    query_rows = queries.reshape(rows_here, length, width)
    key_rows = keys_all.reshape(rows_here, length, width)
    value_rows = values_all.reshape(rows_here, length, width)
    mixed_rows, log_totals = lax.map(attend, (query_rows, key_rows, value_rows, pair_lengths))
    mixed = mixed_rows.reshape(count, width)
    first_sum = tokens.astype(jnp.float32) + matmul(mixed, out_mat) + out_add.astype(jnp.float32)
    first_norm, first_inverse = normalize(first_sum)
    middle = first_norm * first_gain.astype(jnp.float32) + first_shift.astype(jnp.float32)
    middle_low = middle.astype(jnp.bfloat16)
    pre_act = matmul(middle_low, up_mat) + up_add.astype(jnp.float32)
    cdf_part = 0.5 * (1.0 + lax.erf(pre_act * SQRT_HALF))
    activated = (pre_act * cdf_part).astype(jnp.bfloat16)
    second_sum = middle + matmul(activated, down_mat) + down_add.astype(jnp.float32)
    second_norm, second_inverse = normalize(second_sum)
    layer_out = (
        (second_norm * second_gain.astype(jnp.float32) + second_shift.astype(jnp.float32))
        .astype(jnp.bfloat16)
        .reshape(hidden.shape)
    )
    attn_back = (
        lax.all_gather(query_weight, ("dp", "shard"), axis=0, tiled=True),
        lax.all_gather(query_bias, ("dp", "shard"), axis=0, tiled=True),
        lax.all_gather(key_weight, ("dp", "shard"), axis=0, tiled=True),
        lax.all_gather(value_weight, ("dp", "shard"), axis=0, tiled=True),
        lax.all_gather(value_bias, ("dp", "shard"), axis=0, tiled=True),
        lax.all_gather(out_weight, ("dp", "shard"), axis=0, tiled=True),
        lax.all_gather(out_bias, ("dp", "shard"), axis=0, tiled=True),
        lax.all_gather(attn_gain, ("dp", "shard"), axis=0, tiled=True),
        lax.all_gather(attn_shift, ("dp", "shard"), axis=0, tiled=True),
    )
    ffn_back = (
        lax.all_gather(up_weight, ("dp", "shard"), axis=0, tiled=True),
        lax.all_gather(up_bias, ("dp", "shard"), axis=0, tiled=True),
        lax.all_gather(down_weight, ("dp", "shard"), axis=0, tiled=True),
        lax.all_gather(down_bias, ("dp", "shard"), axis=0, tiled=True),
        lax.all_gather(final_gain, ("dp", "shard"), axis=0, tiled=True),
        lax.all_gather(final_shift, ("dp", "shard"), axis=0, tiled=True),
    )
    back_query, back_key, back_value, back_out, back_first_gain = (
        attn_back[0],
        attn_back[2],
        attn_back[3],
        attn_back[5],
        attn_back[7],
    )
    back_up, back_down, back_second_gain = (ffn_back[0], ffn_back[2], ffn_back[4])
    grad_out = cotangent.reshape(count, width).astype(jnp.float32)
    grad_final_gain = jnp.sum(grad_out * second_norm, 0)
    grad_final_shift = jnp.sum(grad_out, 0)
    grad_second = norm_back(
        grad_out, second_norm, second_inverse, back_second_gain.astype(jnp.float32)
    )
    grad_second_low = grad_second.astype(jnp.bfloat16)
    grad_down_bias = jnp.sum(grad_second_low.astype(jnp.float32), 0)
    grad_down_weight = outer_sum(activated, grad_second_low)
    grad_act = back_product(grad_second_low, back_down)
    density = jnp.exp(-0.5 * pre_act * pre_act) * INV_ROOT
    grad_pre = (grad_act * (cdf_part + pre_act * density)).astype(jnp.bfloat16)
    grad_up_bias = jnp.sum(grad_pre.astype(jnp.float32), 0)
    grad_up_weight = outer_sum(middle_low, grad_pre)
    grad_middle = grad_second + back_product(grad_pre, back_up)
    grad_attn_gain = jnp.sum(grad_middle * first_norm, 0)
    grad_attn_shift = jnp.sum(grad_middle, 0)
    grad_first = norm_back(
        grad_middle, first_norm, first_inverse, back_first_gain.astype(jnp.float32)
    )
    ffn_grad_terms = (
        grad_up_weight,
        grad_up_bias,
        grad_down_weight,
        grad_down_bias,
        grad_final_gain,
        grad_final_shift,
    )
    grad_first_low = grad_first.astype(jnp.bfloat16)
    grad_out_bias = jnp.sum(grad_first_low.astype(jnp.float32), 0)
    grad_out_weight = outer_sum(mixed, grad_first_low)
    grad_mixed = back_product(grad_first_low, back_out).astype(jnp.bfloat16)
    grad_query_rows, grad_key_rows, grad_value_rows = lax.map(
        attend_back,
        (
            query_rows,
            key_rows,
            value_rows,
            pair_lengths,
            log_totals,
            grad_mixed.reshape(rows_here, length, width),
        ),
    )
    grad_queries = grad_query_rows.reshape(count, width)
    grad_keys = grad_key_rows.reshape(count, width)
    grad_values = grad_value_rows.reshape(count, width)
    grad_query_bias = jnp.sum(grad_queries.astype(jnp.float32), 0)
    grad_query_weight = outer_sum(tokens, grad_queries)
    grad_key_weight = outer_sum(tokens, grad_keys)
    grad_value_weight = outer_sum(tokens, grad_values)
    grad_value_bias = jnp.sum(grad_values.astype(jnp.float32), 0)
    grad_tokens = (
        grad_first
        + back_product(grad_queries, back_query)
        + back_product(grad_keys, back_key)
        + back_product(grad_values, back_value)
    )
    owned_all = (
        lax.psum_scatter(grad_query_weight, ("dp", "shard"), scatter_dimension=0, tiled=True),
        lax.psum_scatter(grad_query_bias, ("dp", "shard"), scatter_dimension=0, tiled=True),
        lax.psum_scatter(grad_key_weight, ("dp", "shard"), scatter_dimension=0, tiled=True),
        lax.psum_scatter(grad_value_weight, ("dp", "shard"), scatter_dimension=0, tiled=True),
        lax.psum_scatter(grad_value_bias, ("dp", "shard"), scatter_dimension=0, tiled=True),
        lax.psum_scatter(grad_out_weight, ("dp", "shard"), scatter_dimension=0, tiled=True),
        lax.psum_scatter(grad_out_bias, ("dp", "shard"), scatter_dimension=0, tiled=True),
        lax.psum_scatter(grad_attn_gain, ("dp", "shard"), scatter_dimension=0, tiled=True),
        lax.psum_scatter(grad_attn_shift, ("dp", "shard"), scatter_dimension=0, tiled=True),
        lax.psum_scatter(ffn_grad_terms[0], ("dp", "shard"), scatter_dimension=0, tiled=True),
        lax.psum_scatter(ffn_grad_terms[1], ("dp", "shard"), scatter_dimension=0, tiled=True),
        lax.psum_scatter(ffn_grad_terms[2], ("dp", "shard"), scatter_dimension=0, tiled=True),
        lax.psum_scatter(ffn_grad_terms[3], ("dp", "shard"), scatter_dimension=0, tiled=True),
        lax.psum_scatter(ffn_grad_terms[4], ("dp", "shard"), scatter_dimension=0, tiled=True),
        lax.psum_scatter(ffn_grad_terms[5], ("dp", "shard"), scatter_dimension=0, tiled=True),
    )
    attn_owned = owned_all[:9]
    ffn_owned = owned_all[9:]
    return (
        layer_out,
        grad_tokens.reshape(hidden.shape),
        attn_owned[0],
        attn_owned[1],
        attn_owned[2],
        attn_owned[3],
        attn_owned[4],
        attn_owned[5],
        attn_owned[6],
        attn_owned[7],
        attn_owned[8],
        ffn_owned[0],
        ffn_owned[1],
        ffn_owned[2],
        ffn_owned[3],
        ffn_owned[4],
        ffn_owned[5],
    )


def solution(mesh):
    placed = (
        P(("dp", "shard"), None, None),
        P(("dp", "shard"), None),
        P(("dp", "shard"), None, None),
        P(("dp", "shard"), None),
        P(("dp", "shard")),
        P(("dp", "shard"), None),
        P(("dp", "shard"), None),
        P(("dp", "shard")),
        P(("dp", "shard"), None),
        P(("dp", "shard")),
        P(("dp", "shard")),
        P(("dp", "shard")),
        P(("dp", "shard"), None),
        P(("dp", "shard")),
        P(("dp", "shard"), None),
        P(("dp", "shard")),
        P(("dp", "shard")),
        P(("dp", "shard")),
    )
    return jax.shard_map(
        per_device,
        mesh=mesh,
        in_specs=placed,
        out_specs=(
            P(("dp", "shard"), None, None),
            P(("dp", "shard"), None, None),
            P(("dp", "shard"), None),
            P(("dp", "shard")),
            P(("dp", "shard"), None),
            P(("dp", "shard"), None),
            P(("dp", "shard")),
            P(("dp", "shard"), None),
            P(("dp", "shard")),
            P(("dp", "shard")),
            P(("dp", "shard")),
            P(("dp", "shard"), None),
            P(("dp", "shard")),
            P(("dp", "shard"), None),
            P(("dp", "shard")),
            P(("dp", "shard")),
            P(("dp", "shard")),
        ),
        check_vma=False,
    )
```

profile of v0, /device:TPU:0, one launch (start us, length us, event | category | flops | bytes accessed | tf_op | source)
XLA Modules:
  0.0 1109.8 jit_solution(8089481676357500626)
XLA Ops:
  18.8 42.4 %all-reduce.19 = (bf16[768]{0:T(1024)(128)(2,1)S(1)}, bf16[768]{0:T(1024)(128)(2,1)S(1)}, bf16[768]{0:T(1024)(128)(2,1)S(1)}, bf16[768]{0:T(1024)(128)(2,1)S(1)}...) all-reduce(bf16[768]{0:T(1024)(128)(2,1)S(1)} %dynamic-update-slice, ...), channel_id=1, replica_groups=mesh['dp'=8,'shard'=4] {'dp','shard'}, use_global_device_ids=true, to_apply=%add | all-reduce | flops 9216 | bytes 36864
  72.0 52.0 %all-gather.9.cloned.1.call-done = bf16[768,768]{1,0:T(8,128)(2,1)} async-done(((bf16[24,768]{1,0:T(8,128)(2,1)}), bf16[768,768]{1,0:T(8,128)(2,1)}) %all-gather.9.cloned.1.call-update) | async-done | bytes 1179664 | tf_op jit(solution)/shard_map/all_gather | solution.py:135
  128.8 51.1 %all-gather.11.cloned.1.call-done = bf16[768,768]{1,0:T(8,128)(2,1)} async-done(((bf16[24,768]{1,0:T(8,128)(2,1)}), bf16[768,768]{1,0:T(8,128)(2,1)}) %all-gather.11.cloned.1.call-update) | async-done | bytes 1179664 | tf_op jit(solution)/shard_map/all_gather | solution.py:137
  184.7 23.6 %while.26 = (s32[]{:T(128)}, bf16[2,512,768]{2,1,0:T(8,128)(2,1)}, f32[2,12,512]{2,1,0:T(8,128)S(1)}, bf16[2,512,768]{1,2,0:T(8,128)(2,1)S(1)}, s32[2,8]{1,0:T(2...) while((s32[]{:T(128)}, bf16[2,512,768]{2,1,0:T(8,128)(2,1)}, ...), condition=%wide.region_5.6_spmd, body=%wide.region_0.5_spmd.sunk | while | flops 843716160 | bytes 50033424 | solution.py:172
  208.3 27.5 %all-gather.13.cloned.1.call-done = bf16[768,768]{1,0:T(8,128)(2,1)} async-done(((bf16[24,768]{1,0:T(8,128)(2,1)}), bf16[768,768]{1,0:T(8,128)(2,1)}) %all-gather.13.cloned.1.call-update) | async-done | bytes 1179664 | tf_op jit(solution)/shard_map/all_gather | solution.py:140
  241.8 59.4 %all-gather.15.cloned.1.call-done = bf16[768,3072]{1,0:T(8,128)(2,1)} async-done(((bf16[24,3072]{1,0:T(8,128)(2,1)}), bf16[768,3072]{1,0:T(8,128)(2,1)}) %all-gather.15.cloned.1.call-update) | async-done | bytes 4718608 | tf_op jit(solution)/shard_map/all_gather | solution.py:146
  301.2 12.4 %multiply_convert_fusion.3 = (bf16[1024,3072]{1,0:T(8,128)(2,1)}, f32[1024,3072]{1,0:T(8,128)}) fusion(f32[3072]{0:T(1024)S(1)} %copy-done.34, bf16[768,3072]{1,0:T(8,128)(2,1)} %all-gather.15.cloned.1.call-done, f32[1024,768]{1,0:T(8,128)} %copy-done.2, f32[768]{0:T(1024)S(1)} %copy-done.26, f32[768]{0:T(1024)S(1)} %copy-done.22, ...), kind=kOutput, calls=%fused_computation.51 | convolution fusion | flops 4854644736 | bytes 26765312 | tf_op jit(solution)/shard_map/dot_general | solution.py:16
  313.6 52.8 %all-gather.17.cloned.1.call-done = bf16[3072,768]{1,0:T(8,128)(2,1)} async-done(((bf16[96,768]{1,0:T(8,128)(2,1)}), bf16[3072,768]{1,0:T(8,128)(2,1)}) %all-gather.17.cloned.1.call-update) | async-done | bytes 4718608 | tf_op jit(solution)/shard_map/all_gather | solution.py:148
  366.3 9.5 fusion.43
  381.9 13.7 %convert_reduce_fusion.2 = (f32[3072]{0:T(1024)}, bf16[1024,3072]{1,0:T(8,128)(2,1)S(1)}) fusion(f32[1024,3072]{1,0:T(8,128)} %get-tuple-element.326, f32[3072]{0:T(1024)S(1)} %copy-done.34, bf16[3072,768]{1,0:T(8,128)(2,1)S(1)} %copy-done.39, f32[1024,768]{1,0:T(8,128)S(1)} %get-tuple-element.311), kind=kOutput, calls=%fused_computation.50 | convolution fusion | flops 4873516032 | bytes 26763264 | tf_op jit(solution)/shard_map/tb,ab->ta/dot_general | solution.py:24
  395.6 6.5 multiply_reduce_fusion.1
  413.2 81.3 %while.27 = (s32[]{:T(128)}, bf16[2,512,768]{1,2,0:T(8,128)(2,1)}, bf16[2,512,768]{1,2,0:T(8,128)(2,1)}, bf16[2,512,768]{1,2,0:T(8,128)(2,1)}, bf16[2,512,768]{1...) while((s32[]{:T(128)}, bf16[2,512,768]{1,2,0:T(8,128)(2,1)}, ...), condition=%wide.region_18.19_spmd, body=%wide.region_14.18_spmd.sunk | while | flops 2062685696 | bytes 178959856 | solution.py:247
  425.7 11.1 multiply_reduce_fusion.7
  438.6 7.0 multiply_convert_fusion.7
  466.5 11.0 multiply_reduce_fusion.7
  479.2 7.0 multiply_convert_fusion.7
  514.4 10.7 fusion.37
  527.0 10.3 fusion.34
  544.5 41.1 %all-reduce.18 = (f32[768]{0:T(1024)S(1)}, f32[768]{0:T(1024)S(1)}, f32[768]{0:T(1024)S(1)}, f32[768]{0:T(1024)S(1)}, f32[768]{0:T(1024)S(1)}, /*index=5*/f32[30...) all-reduce(f32[768]{0:T(1024)S(1)} %convert_reduce_fusion.7, ...), channel_id=3, replica_groups=mesh['dp'=8,'shard'=4] {'dp','shard'}, use_global_device_ids=true, to_apply=%region_21.22.clone | all-reduce | flops 9216 | bytes 73728
  599.5 11.8 %reduce-scatter.19.cloned.1.call-done = f32[24,768]{1,0:T(8,128)} async-done(((f32[768,768]{1,0:T(8,128)}), f32[24,768]{1,0:T(8,128)}) %reduce-scatter.19.cloned.1.call-update) | async-done | bytes 73744
  611.3 103.9 %reduce-scatter.21.cloned.1.call-done = f32[24,768]{1,0:T(8,128)} async-done(((f32[768,768]{1,0:T(8,128)}), f32[24,768]{1,0:T(8,128)}) %reduce-scatter.21.cloned.1.call-update) | async-done | bytes 73744
  715.2 104.7 %reduce-scatter.23.cloned.1.call-done = f32[24,768]{1,0:T(8,128)} async-done(((f32[768,768]{1,0:T(8,128)}), f32[24,768]{1,0:T(8,128)}) %reduce-scatter.23.cloned.1.call-update) | async-done | bytes 73744
  819.9 140.8 %reduce-scatter.15.cloned.1.call-done = f32[24,3072]{1,0:T(8,128)} async-done(((f32[768,3072]{1,0:T(8,128)}), f32[24,3072]{1,0:T(8,128)}) %reduce-scatter.15.cloned.1.call-update) | async-done | bytes 294928 | tf_op jit(solution)/shard_map/reduce_scatter | solution.py:282
  960.7 142.1 %reduce-scatter.17.cloned.1.call-done = f32[96,768]{1,0:T(8,128)} async-done(((f32[3072,768]{1,0:T(8,128)}), f32[96,768]{1,0:T(8,128)}) %reduce-scatter.17.cloned.1.call-update) | async-done | bytes 294928 | tf_op jit(solution)/shard_map/reduce_scatter | solution.py:284
  (277 shorter events, 165.3 us)
Async XLA Ops:
  7.2 61.0 %all-gather.7.cloned.1.call-start = ((), (), s32[]{:S(2)}) async-start(), calls=%async_computation.6 | async-start | bytes 1216512 | tf_op jit(solution)/shard_map/all_gather | solution.py:138
  7.9 116.1 %all-gather.9.cloned.1.call-start = ((), (), s32[]{:S(2)}) async-start(), calls=%async_computation.7 | async-start | bytes 1216512 | tf_op jit(solution)/shard_map/all_gather | solution.py:135
  8.7 171.3 %all-gather.11.cloned.1.call-start = ((), (), s32[]{:S(2)}) async-start(), calls=%async_computation.8 | async-start | bytes 1216512 | tf_op jit(solution)/shard_map/all_gather | solution.py:137
  9.4 226.4 %all-gather.13.cloned.1.call-start = ((), (), s32[]{:S(2)}) async-start(), calls=%async_computation.9 | async-start | bytes 1216512 | tf_op jit(solution)/shard_map/all_gather | solution.py:140
  10.0 291.2 %all-gather.15.cloned.1.call-start = ((), (), s32[]{:S(2)}) async-start(), calls=%async_computation.10 | async-start | bytes 4866048 | tf_op jit(solution)/shard_map/all_gather | solution.py:146
  10.6 355.8 %all-gather.17.cloned.1.call-start = ((), (), s32[]{:S(2)}) async-start(), calls=%async_computation.11 | async-start | bytes 4866048 | tf_op jit(solution)/shard_map/all_gather | solution.py:148
  11.1 588.4 %reduce-scatter.13.cloned.1.call-start = ((), (), s32[]{:S(2)}) async-start(), calls=%async_computation.12 | async-start | bytes 2433024 | tf_op jit(solution)/shard_map/reduce_scatter | solution.py:278
  239.6 61.6 %copy-start.22 = (f32[768]{0:T(1024)S(1)}, f32[768]{0:T(1024)}, u32[]{:S(2)}) copy-start(f32[768]{0:T(1024)} %convert_element_type.175) | copy-start | bytes 9220
  239.6 61.6 %copy-start.26 = (f32[768]{0:T(1024)S(1)}, f32[768]{0:T(1024)}, u32[]{:S(2)}) copy-start(f32[768]{0:T(1024)} %convert_element_type.176) | copy-start | bytes 9220
  239.6 61.6 %copy-start.34 = (f32[3072]{0:T(1024)S(1)}, f32[3072]{0:T(1024)}, u32[]{:S(2)}) copy-start(f32[3072]{0:T(1024)} %convert_element_type.178) | copy-start | bytes 36868
  239.6 162.5 %copy-start.18 = (f32[1024]{0:T(1024)}, f32[1024]{0:T(1024)S(1)}, u32[]{:S(2)}) copy-start(f32[1024]{0:T(1024)S(1)} %broadcast_multiply_fusion.4) | copy-start | bytes 12292
  241.8 160.4 %copy-start.20 = (f32[1024]{0:T(1024)}, f32[1024]{0:T(1024)S(1)}, u32[]{:S(2)}) copy-start(f32[1024]{0:T(1024)S(1)} %add_rsqrt_fusion.1) | copy-start | bytes 12292
  241.8 124.5 %copy-start.36 = (f32[768]{0:T(1024)S(1)}, f32[768]{0:T(1024)}, u32[]{:S(2)}) copy-start(f32[768]{0:T(1024)} %convert_element_type.180) | copy-start | bytes 9220
  379.0 16.6 %slice-start.3 = ((s8[4718592]{0:T(1024)(128)(4,1)}), s8[4194304]{0:T(1024)(128)(4,1)S(1)}, s32[]{:S(2)}) async-start(s8[4718592]{0:T(1024)(128)(4,1)} %bitcast.202), calls=%async_computation.21 | async-start | bytes 8388608
  381.9 13.7 %copy-start.13 = (f32[1024,768]{1,0:T(8,128)}, f32[1024,768]{1,0:T(8,128)S(1)}, u32[]{:S(2)}) copy-start(f32[1024,768]{1,0:T(8,128)S(1)} %get-tuple-element.311) | copy-start | bytes 9437188
  381.9 13.7 %copy-start.3 = (f32[1024,768]{1,0:T(8,128)S(1)}, f32[1024,768]{1,0:T(8,128)}, u32[]{:S(2)}) copy-start(f32[1024,768]{1,0:T(8,128)} %copy-done.2) | copy-start | bytes 9437188
  381.9 13.7 %slice-start.4 = ((s8[4718592]{0:T(1024)(128)(4,1)}), s8[524288]{0:T(1024)(128)(4,1)S(1)}, s32[]{:S(2)}) async-start(s8[4718592]{0:T(1024)(128)(4,1)} %bitcast.202), calls=%async_computation.22 | async-start | bytes 1048576
  408.4 202.9 %reduce-scatter.19.cloned.1.call-start = ((), (), s32[]{:S(2)}) async-start(), calls=%async_computation.15 | async-start | bytes 2433024
  425.7 12.9 %slice-start.2 = ((s8[12582912]{0:T(1024)(128)(4,1)}), s8[4194304]{0:T(1024)(128)(4,1)S(1)}, s32[]{:S(2)}) async-start(s8[12582912]{0:T(1024)(128)(4,1)} %bitcast.174), calls=%async_computation.20 | async-start | bytes 8388608 | tf_op jit(solution)/shard_map/while
  466.5 12.7 %slice-start.2 = ((s8[12582912]{0:T(1024)(128)(4,1)}), s8[4194304]{0:T(1024)(128)(4,1)S(1)}, s32[]{:S(2)}) async-start(s8[12582912]{0:T(1024)(128)(4,1)} %bitcast.174), calls=%async_computation.20 | async-start | bytes 8388608 | tf_op jit(solution)/shard_map/while
  499.7 215.5 %reduce-scatter.21.cloned.1.call-start = ((), (), s32[]{:S(2)}) async-start(), calls=%async_computation.16 | async-start | bytes 2433024
  508.1 311.8 %reduce-scatter.23.cloned.1.call-start = ((), (), s32[]{:S(2)}) async-start(), calls=%async_computation.17 | async-start | bytes 2433024
  514.3 446.4 %reduce-scatter.15.cloned.1.call-start = ((), (), s32[]{:S(2)}) async-start(), calls=%async_computation.13 | async-start | bytes 9732096 | tf_op jit(solution)/shard_map/reduce_scatter | solution.py:282
  525.1 577.7 %reduce-scatter.17.cloned.1.call-start = ((), (), s32[]{:S(2)}) async-start(), calls=%async_computation.14 | async-start | bytes 9732096 | tf_op jit(solution)/shard_map/reduce_scatter | solution.py:284
  (45 other events, 168.4 us)
Sparse Core Ops, SparseCore 0:
  10.9 56.9 all-gather.6
  70.9 53.1 all-gather.8
  126.9 52.9 all-gather.10
  182.7 53.0 all-gather.12
  238.5 62.5 all-gather.14
  303.9 62.3 all-gather.16
  408.5 97.8 reduce-scatter.12
  513.2 98.0 reduce-scatter.18
  617.1 98.0 reduce-scatter.20
  721.8 98.0 reduce-scatter.22
  826.4 134.2 reduce-scatter.14
  968.1 134.6 reduce-scatter.16
where the time goes:
time: 1120 us; the launch traced here: 1110 us
  waiting for transfers between devices  750 us (67%)
  matrix products  161 us (14%)
  blocking collectives  83.5 us (7%)
  local copies, waits for them, and re-layouts  62.7 us (6%)
  other arithmetic  36.3 us (3%)
  between operations  15 us (1%)
    unnamed x15, waiting for transfers between devices  224 us
    reduce_scatter x1, waiting for transfers between devices, per_device(): lax.psum_scatter(ffn_grad_terms[2], ('dp', 'shard'), scatter_dimension=0,...  142 us
    reduce_scatter x1, waiting for transfers between devices, per_device(): lax.psum_scatter(ffn_grad_terms[0], ('dp', 'shard'), scatter_dimension=0,...  141 us
    unnamed x2, blocking collectives  83.5 us
    all_gather x1, waiting for transfers between devices, per_device(): lax.all_gather(up_weight, ('dp', 'shard'), axis=0, tiled=True)  59.4 us
    all_gather x1, waiting for transfers between devices, per_device(): lax.all_gather(down_weight, ('dp', 'shard'), axis=0, tiled=True)  52.8 us
    all_gather x1, waiting for transfers between devices, per_device(): lax.all_gather(query_weight, ('dp', 'shard'), axis=0, tiled=True)  52 us
    all_gather x1, waiting for transfers between devices, per_device(): lax.all_gather(key_weight, ('dp', 'shard'), axis=0, tiled=True)  51.1 us
  transfers between devices with their start and end apart: 12, of which 10 were waited for; matrix products, arithmetic and copies ran while one was open for 19% of the time, Pallas kernels for 0%

commit v1 on v0

v1 whole, which is shorter than its diff:
```python
import jax
import jax.numpy as jnp
from jax import lax
from jax.sharding import PartitionSpec as P

HEADS = 12


EPSILON = 1e-06
SQRT_HALF = 0.7071067811865476
INV_ROOT = 0.3989422804014327
score_scale = 0.125

AXES = ("dp", "shard")
f32 = jnp.float32
bf16 = jnp.bfloat16
cat = jnp.concatenate


def moves(move):
    pairs = []
    for index in range(32):
        z, y, x, core = index // 8, (index // 4) % 2, (index // 2) % 2, index % 2
        z, y, x, core = move(z, y, x, core)
        pairs.append((index, z * 8 + y * 4 + x * 2 + core))
    return pairs


MOVES = {
    "core": moves(lambda z, y, x, core: (z, y, x, 1 - core)),
    "x": moves(lambda z, y, x, core: (z, y, 1 - x, core)),
    "y": moves(lambda z, y, x, core: (z, 1 - y, x, core)),
    "z1": moves(lambda z, y, x, core: ((z + 1) % 4, y, x, core)),
    "z2": moves(lambda z, y, x, core: ((z + 2) % 4, y, x, core)),
    "z3": moves(lambda z, y, x, core: ((z + 3) % 4, y, x, core)),
}


def send(values, move):
    return lax.ppermute(values, AXES, MOVES[move])


def place():
    major, minor = lax.axis_index("dp"), lax.axis_index("shard")
    return major // 2, major % 2, minor // 2, minor % 2


def phase(*values):
    return lax.optimization_barrier(values)


def add(*terms):
    total = terms[0].astype(f32)
    for term in terms[1:]:
        total = total + term.astype(f32)
    return total


def gather_blocks(block, split):
    z, y, x, core = place()
    one, two, three = send(block, "z1"), send(block, "z2"), send(block, "z3")
    one, two, three = phase(one, two, three)
    line = jnp.stack([block, one, two, three])
    first, second = line[:, :split], line[:, split:]
    first_x, second_y = send(first, "x"), send(second, "y")
    first_x, second_y, first, second = phase(first_x, second_y, first, second)
    first, second = cat([first, first_x]), cat([second, second_y])
    first_y, second_x = send(first, "y"), send(second, "x")
    other_first, other_second = send(first, "core"), send(second, "core")
    first, first_y, second, second_x, other_first, other_second = phase(
        first, first_y, second, second_x, other_first, other_second
    )
    other_first_y, other_second_x = send(first_y, "core"), send(second_x, "core")
    halves = []
    for a, b, c, d in (
        (first, first_y, second, second_x),
        (other_first, other_first_y, other_second, other_second_x),
    ):
        first_all = cat([a, b]).reshape(2, 2, 4, *first.shape[1:])
        second_all = cat([c, d]).reshape(2, 2, 4, *second.shape[1:]).swapaxes(0, 1)
        halves.append(cat([first_all, second_all], 3).reshape(16, *block.shape))
    chips = jnp.arange(16)
    source = ((chips // 2 % 2) ^ y) * 8 + ((chips % 2) ^ x) * 4 + (z - chips // 4) % 4
    return halves[0][source], halves[1][source]


def scatter_blocks(blocks, split):
    z, y, x, core = place()
    half = blocks.shape[2] // 2
    keep = lax.dynamic_slice_in_dim(blocks, core * half, half, 2)
    away = lax.dynamic_slice_in_dim(blocks, (1 - core) * half, half, 2).astype(bf16)
    (got,) = phase(send(away, "core"))
    summed = add(keep, got).astype(bf16).reshape(4, 2, 2, *blocks.shape[1:2], half)
    pick = lax.dynamic_index_in_dim
    first, second = summed[:, :, :, :split], summed[:, :, :, split:]
    got_first = send(pick(first, 1 - y, 1, False), "y")
    got_second = send(pick(second, 1 - x, 2, False), "x")
    got_first, got_second, first, second = phase(got_first, got_second, first, second)
    first = add(pick(first, y, 1, False), got_first).astype(bf16)
    second = add(pick(second, x, 2, False), got_second).astype(bf16)
    got_first = send(pick(first, 1 - x, 1, False), "x")
    got_second = send(pick(second, 1 - y, 1, False), "y")
    got_first, got_second, first, second = phase(got_first, got_second, first, second)
    first = add(pick(first, x, 1, False), got_first)
    second = add(pick(second, y, 1, False), got_second)
    line = cat([first, second], 1)
    low = line.astype(bf16)
    one = send(pick(low, (z + 1) % 4, 0, False), "z1")
    two = send(pick(low, (z + 2) % 4, 0, False), "z2")
    three = send(pick(low, (z + 3) % 4, 0, False), "z3")
    one, two, three, line = phase(one, two, three, line)
    return add(pick(line, z, 0, False), one, two, three)


def gather_attention(matrices, vector):
    z, y, x, core = place()
    count, rows, width = matrices.shape
    half = width // 2
    mine = lax.dynamic_slice_in_dim(matrices, core * half, half, 2)
    got = send(lax.dynamic_slice_in_dim(matrices, (1 - core) * half, half, 2), "core")
    pair = jnp.where(core == 0, cat([mine, got], 1), cat([got, mine], 1))
    vector_rows = jnp.pad(vector[None], ((0, 15), (0, half - vector.shape[0])))
    block = cat([pair.reshape(count * 2 * rows, half), vector_rows])
    (block,) = phase(block)
    own, other = gather_blocks(block, count * rows)
    full = jnp.where(core == 0, cat([own, other], 2), cat([other, own], 2))
    size = count * 2 * rows
    mats = full[:, :size].reshape(16, count, 2 * rows, width).swapaxes(0, 1).reshape(count, 16 * 2 * rows, width)
    entries = vector.shape[0]
    vectors = full[:, size].reshape(32, half)[:, :entries]
    return mats, vectors


def scatter_attention(matrices, vectors):
    z, y, x, core = place()
    count, full_rows, width = matrices.shape
    half = width // 2
    rows = full_rows // 32
    blocks = matrices.reshape(count, 16, 2 * rows, width).swapaxes(0, 1).reshape(16, count * 2 * rows, width)
    entries = vectors.shape[1]
    vector_rows = jnp.pad(vectors, ((0, 0), (0, half - entries))).reshape(16, 1, width)
    vector_rows = jnp.pad(vector_rows, ((0, 0), (0, 15), (0, 0)))
    line = scatter_blocks(cat([blocks, vector_rows], 1), count * rows)
    size = count * 2 * rows
    mine = line[:size].reshape(count, 2, rows, half)
    keep = lax.dynamic_index_in_dim(mine, core, 1, False)
    got = send(lax.dynamic_index_in_dim(mine, 1 - core, 1, False).astype(bf16), "core").astype(f32)
    whole = jnp.where(core == 0, cat([keep, got], 2), cat([got, keep], 2))
    return whole, line[size, :entries]


def gather_attention_any(matrices, vector):
    mats = lax.all_gather(matrices, AXES, axis=1, tiled=True)
    return mats, lax.all_gather(vector, AXES, axis=0, tiled=False)


def scatter_attention_any(matrices, vectors):
    mats = lax.psum_scatter(matrices.astype(bf16), AXES, scatter_dimension=1, tiled=True)
    return mats.astype(f32), lax.psum_scatter(vectors, AXES, scatter_dimension=0, tiled=False)


def matmul(left, right):
    return jnp.dot(left, right, preferred_element_type=jnp.float32)


def outer_sum(left, right):
    return jnp.einsum("ta,tb->ab", left, right, preferred_element_type=jnp.float32)


def back_product(grads, weights):
    return jnp.einsum("tb,ab->ta", grads, weights, preferred_element_type=jnp.float32)


def normalize(rows):
    centred = rows - jnp.mean(rows, -1, keepdims=True)
    inverse = lax.rsqrt(jnp.mean(centred * centred, -1, keepdims=True) + EPSILON)
    return (centred * inverse, inverse)


def norm_back(grad_rows, normed, inverse, gain):
    grad_norm = grad_rows * gain
    return inverse * (
        grad_norm
        - jnp.mean(grad_norm, -1, keepdims=True)
        - normed * jnp.mean(grad_norm * normed, -1, keepdims=True)
    )


def doc_mask(pair_lens, size):
    pair_ends = jnp.cumsum(pair_lens)
    positions = jnp.arange(size, dtype=jnp.int32)
    doc_index = jnp.sum((positions[:, None] >= pair_ends[None, :]).astype(jnp.int32), -1)
    return doc_index[:, None] == doc_index[None, :]


def split_heads(rows):
    return rows.reshape(rows.shape[0], HEADS, rows.shape[1] // HEADS)


def scores_of(query_heads, key_heads, pair_lens):
    scores = (
        jnp.einsum("qhd,khd->hqk", query_heads, key_heads, preferred_element_type=jnp.float32)
        * score_scale
    )
    return jnp.where(doc_mask(pair_lens, query_heads.shape[0])[None], scores, -1e30)


def attend(packed):
    query_rows, key_rows, value_rows, pair_lens = packed
    scores = scores_of(split_heads(query_rows), split_heads(key_rows), pair_lens)
    row_max = jnp.max(scores, -1, keepdims=True)
    exp_scores = jnp.exp(scores - row_max)
    totals = jnp.sum(exp_scores, -1, keepdims=True)
    attn_probs = exp_scores / totals
    mixed = jnp.einsum(
        "hqk,khd->qhd",
        attn_probs.astype(jnp.bfloat16),
        split_heads(value_rows),
        preferred_element_type=jnp.float32,
    )
    log_total = (row_max + jnp.log(totals))[..., 0]
    return (mixed.reshape(query_rows.shape).astype(jnp.bfloat16), log_total)


def attend_back(packed):
    query_rows, key_rows, value_rows, pair_lens, log_total, grad_rows = packed
    query_heads = split_heads(query_rows)
    key_heads = split_heads(key_rows)
    grad_heads = split_heads(grad_rows)
    scores = scores_of(query_heads, key_heads, pair_lens)
    attn_probs = jnp.exp(scores - log_total[..., None])
    grad_values = jnp.einsum(
        "hqk,qhd->khd",
        attn_probs.astype(jnp.bfloat16),
        grad_heads,
        preferred_element_type=jnp.float32,
    )
    grad_probs = jnp.einsum(
        "qhd,khd->hqk", grad_heads, split_heads(value_rows), preferred_element_type=jnp.float32
    )
    centre = jnp.sum(grad_probs * attn_probs, -1, keepdims=True)
    grad_scores = (attn_probs * (grad_probs - centre)).astype(jnp.bfloat16)
    grad_queries = (
        jnp.einsum("hqk,khd->qhd", grad_scores, key_heads, preferred_element_type=jnp.float32)
        * score_scale
    )
    grad_keys = (
        jnp.einsum("hqk,qhd->khd", grad_scores, query_heads, preferred_element_type=jnp.float32)
        * score_scale
    )
    row_shape = query_rows.shape
    return (
        grad_queries.reshape(row_shape).astype(jnp.bfloat16),
        grad_keys.reshape(row_shape).astype(jnp.bfloat16),
        grad_values.reshape(row_shape).astype(jnp.bfloat16),
    )


def per_device(
    known,
    hidden,
    pair_lengths,
    cotangent,
    query_weight,
    query_bias,
    key_weight,
    value_weight,
    value_bias,
    out_weight,
    out_bias,
    attn_gain,
    attn_shift,
    up_weight,
    up_bias,
    down_weight,
    down_bias,
    final_gain,
    final_shift,
):
    rows_here, length, width = hidden.shape
    count = rows_here * length
    share = query_weight.shape[0]
    devices = width // share
    chunks = up_weight.shape[1] // width
    up_mine = (
        up_weight.reshape(share, devices, chunks, share).swapaxes(1, 2).reshape(share, chunks * width)
    )
    down_mine = down_weight.reshape(chunks, share, width).swapaxes(0, 1).reshape(share, chunks * width)
    ffn_mine = cat([up_mine, down_mine], 1)
    ffn_full = lax.all_gather(ffn_mine, AXES, axis=0, tiled=True)
    vector = cat(
        [
            query_bias,
            value_bias,
            out_bias,
            attn_gain,
            attn_shift,
            down_bias,
            final_gain,
            final_shift,
            up_bias,
        ]
    )
    matrices = jnp.stack([query_weight, key_weight, value_weight, out_weight])
    mats, vectors = (gather_attention if known else gather_attention_any)(matrices, vector)
    query_mat, key_mat, value_mat, out_mat = mats[0], mats[1], mats[2], mats[3]
    vectors = (
        vectors.reshape(devices, 8 + chunks, share).swapaxes(0, 1).reshape(8 + chunks, width).astype(f32)
    )
    query_add, value_add, out_add, first_gain, first_shift, down_add, second_gain, second_shift = (
        vectors[i] for i in range(8)
    )
    up_add = vectors[8:].reshape(chunks * width)
    up_mat = ffn_full[:, : chunks * width]
    down_mat = ffn_full[:, chunks * width :].reshape(width, chunks, width)
    tokens = hidden.reshape(count, width)
    queries = (matmul(tokens, query_mat) + query_add).astype(jnp.bfloat16)
    keys_all = matmul(tokens, key_mat).astype(jnp.bfloat16)
    values_all = (matmul(tokens, value_mat) + value_add).astype(jnp.bfloat16)
    query_rows = queries.reshape(rows_here, length, width)
    key_rows = keys_all.reshape(rows_here, length, width)
    value_rows = values_all.reshape(rows_here, length, width)
    mixed_rows, log_totals = lax.map(attend, (query_rows, key_rows, value_rows, pair_lengths))
    mixed = mixed_rows.reshape(count, width)
    first_sum = tokens.astype(jnp.float32) + matmul(mixed, out_mat) + out_add
    first_norm, first_inverse = normalize(first_sum)
    middle = first_norm * first_gain + first_shift
    middle_low = middle.astype(jnp.bfloat16)
    pre_act = matmul(middle_low, up_mat) + up_add
    cdf_part = 0.5 * (1.0 + lax.erf(pre_act * SQRT_HALF))
    activated = (pre_act * cdf_part).astype(jnp.bfloat16)
    act_parts = activated.reshape(count, chunks, width)
    second_sum = (
        middle
        + jnp.einsum("tgi,ign->tn", act_parts, down_mat, preferred_element_type=jnp.float32)
        + down_add
    )
    second_norm, second_inverse = normalize(second_sum)
    layer_out = (second_norm * second_gain + second_shift).astype(jnp.bfloat16).reshape(hidden.shape)
    grad_out = cotangent.reshape(count, width).astype(jnp.float32)
    grad_final_gain = jnp.sum(grad_out * second_norm, 0)
    grad_final_shift = jnp.sum(grad_out, 0)
    grad_second = norm_back(grad_out, second_norm, second_inverse, second_gain)
    grad_second_low = grad_second.astype(jnp.bfloat16)
    grad_down_bias = jnp.sum(grad_second_low.astype(jnp.float32), 0)
    grad_down = jnp.einsum("tgi,tn->ign", act_parts, grad_second_low, preferred_element_type=f32)
    grad_act = jnp.einsum("tn,ign->tgi", grad_second_low, down_mat, preferred_element_type=f32)
    density = jnp.exp(-0.5 * pre_act * pre_act) * INV_ROOT
    grad_pre = (grad_act.reshape(pre_act.shape) * (cdf_part + pre_act * density)).astype(jnp.bfloat16)
    grad_up_bias = jnp.sum(grad_pre.astype(jnp.float32), 0)
    grad_up = outer_sum(middle_low, grad_pre)
    ffn_grads = cat([grad_up.astype(bf16), grad_down.astype(bf16).reshape(width, chunks * width)], 1)
    ffn_owned = lax.psum_scatter(ffn_grads, AXES, scatter_dimension=0, tiled=True).astype(f32)
    grad_middle = grad_second + back_product(grad_pre, up_mat)
    grad_attn_gain = jnp.sum(grad_middle * first_norm, 0)
    grad_attn_shift = jnp.sum(grad_middle, 0)
    grad_first = norm_back(grad_middle, first_norm, first_inverse, first_gain)
    grad_first_low = grad_first.astype(jnp.bfloat16)
    grad_out_bias = jnp.sum(grad_first_low.astype(jnp.float32), 0)
    grad_out_weight = outer_sum(mixed, grad_first_low)
    grad_mixed = back_product(grad_first_low, out_mat).astype(jnp.bfloat16)
    grad_query_rows, grad_key_rows, grad_value_rows = lax.map(
        attend_back,
        (
            query_rows,
            key_rows,
            value_rows,
            pair_lengths,
            log_totals,
            grad_mixed.reshape(rows_here, length, width),
        ),
    )
    grad_queries = grad_query_rows.reshape(count, width)
    grad_keys = grad_key_rows.reshape(count, width)
    grad_values = grad_value_rows.reshape(count, width)
    grad_query_bias = jnp.sum(grad_queries.astype(jnp.float32), 0)
    grad_value_bias = jnp.sum(grad_values.astype(jnp.float32), 0)
    mat_grads = jnp.stack(
        [
            outer_sum(tokens, grad_queries),
            outer_sum(tokens, grad_keys),
            outer_sum(tokens, grad_values),
            grad_out_weight,
        ]
    )
    grad_tokens = (
        grad_first
        + back_product(grad_queries, query_mat)
        + back_product(grad_keys, key_mat)
        + back_product(grad_values, value_mat)
    )
    vector_grads = jnp.stack(
        [
            grad_query_bias,
            grad_value_bias,
            grad_out_bias,
            grad_attn_gain,
            grad_attn_shift,
            grad_down_bias,
            grad_final_gain,
            grad_final_shift,
        ]
    )
    vector_grads = cat([vector_grads, grad_up_bias.reshape(chunks, width)])
    vector_grads = (
        vector_grads.reshape(8 + chunks, devices, share).swapaxes(0, 1).reshape(devices, (8 + chunks) * share)
    )
    mats_owned, vectors_owned = (scatter_attention if known else scatter_attention_any)(
        mat_grads, vector_grads
    )
    own = vectors_owned.reshape(8 + chunks, share)
    up_owned = (
        ffn_owned[:, : chunks * width]
        .reshape(share, chunks, devices, share)
        .swapaxes(1, 2)
        .reshape(share, chunks * width)
    )
    down_owned = (
        ffn_owned[:, chunks * width :].reshape(share, chunks, width).swapaxes(0, 1).reshape(chunks * share, width)
    )
    return (
        layer_out,
        grad_tokens.reshape(hidden.shape),
        mats_owned[0],
        own[0],
        mats_owned[1],
        mats_owned[2],
        own[1],
        mats_owned[3],
        own[2],
        own[3],
        own[4],
        up_owned,
        own[8:].reshape(chunks * share),
        down_owned,
        own[5],
        own[6],
        own[7],
    )


def solution(mesh):
    known = dict(mesh.shape) == {"dp": 8, "shard": 4}
    cube, flat, line = P(AXES, None, None), P(AXES, None), P(AXES)
    return jax.shard_map(
        lambda *args: per_device(known, *args),
        mesh=mesh,
        in_specs=(
            cube, flat, cube, flat, line, flat, flat, line, flat, line, line, line, flat, line, flat, line, line, line,
        ),
        out_specs=(
            cube, cube, flat, line, flat, flat, line, flat, line, line, line, flat, line, flat, line, line, line,
        ),
        check_vma=False,
    )
```

time: 1120 us -> 445 us (0.40)
  waiting for transfers between devices: 750 us -> 58.1 us
  blocking collectives: 83.5 us -> 0 us
  local copies, waits for them, and re-layouts: 62.7 us -> 118 us
  other arithmetic: 36.3 us -> 76.8 us
  starting transfers between devices: 1.09 us -> 28.6 us
  matrix products: 161 us -> 140 us
    reduce_scatter x3 -> x1, waiting for transfers between devices: 283 us -> 0.01 us  [per_device(): lax.psum_scatter(ffn_grads, AXES, scatter_dimension=0, tiled=True)]
    all_gather x6 -> x1, waiting for transfers between devices: 243 us -> 0.02 us  [per_device(): ffn_full = lax.all_gather(ffn_mine, AXES, axis=0, tiled=True)]
    unnamed x15 -> x2, waiting for transfers between devices: 224 us -> 0.03 us
    unnamed x2 -> x0, blocking collectives: 83.5 us -> none
    ppermute x0 -> x21, waiting for transfers between devices: none -> 58 us  [send(): return lax.ppermute(values, AXES, MOVES[move])]
    ppermute x0 -> x21, starting transfers between devices: none -> 28.5 us  [send(): return lax.ppermute(values, AXES, MOVES[move])]
    reshape x0 -> x13, local copies, waits for them, and re-layouts: none -> 27.7 us  [the longest x1 12.6 us: per_device(): grad_act.reshape(pre_act.shape) * (cdf_part + pre_act * density)]
    concatenate x0 -> x9, other arithmetic: none -> 22.9 us  [the longest x1 9 us: per_device(): cat([grad_up.astype(bf16), grad_down.astype(bf16).reshape(width, chunks *...]
  transfers between devices with their start and end apart: 12 -> 23, of which waited for: 10 -> 11; matrix products, arithmetic and copies ran while one was open for 19% -> 49% of each run, Pallas kernels for 0% -> 0%
where the time goes in v1:
time: 445 us; the launch traced here: 439 us
  matrix products  140 us (31%)
  local copies, waits for them, and re-layouts  118 us (27%)
  other arithmetic  76.8 us (17%)
  waiting for transfers between devices  58.1 us (13%)
  starting transfers between devices  28.6 us (6%)
  between operations  15.7 us (4%)
    ppermute x21, waiting for transfers between devices, send(): return lax.ppermute(values, AXES, MOVES[move])  58 us
    ppermute x21, starting transfers between devices, send(): return lax.ppermute(values, AXES, MOVES[move])  28.5 us
    dot_general x2, matrix products, attend_back(): jnp.einsum('qhd,khd->hqk', grad_heads, split_heads(value_rows), preferred...  22.7 us
    dot_general x5, matrix products, matmul(): return jnp.dot(left, right, preferred_element_type=jnp.float32)  22.1 us
    dot_general x5, matrix products, back_product(): jnp.einsum('tb,ab->ta', grads, weights, preferred_element_type=jnp.float32)  21.8 us
    dot_general x4, matrix products, scores_of(): jnp.einsum('qhd,khd->hqk', query_heads, key_heads, preferred_element_type...  17.2 us
    dot_general x5, matrix products, outer_sum(): jnp.einsum('ta,tb->ab', left, right, preferred_element_type=jnp.float32)  16.1 us
    dynamic_slice x14, local copies, waits for them, and re-layouts, per_device(): lax.map(attend, (query_rows, key_rows, value_rows, pair_lengths))  14.4 us
  transfers between devices with their start and end apart: 23, of which 11 were waited for; matrix products, arithmetic and copies ran while one was open for 49% of the time, Pallas kernels for 0%

profile of v1, /device:TPU:0, one launch (start us, length us, event | category | flops | bytes accessed | tf_op | source)
XLA Modules:
  0.0 438.5 jit_solution(4408698091943829796)
XLA Ops:
  23.5 9.3 %collective-permute-done.2 = bf16[208,384]{1,0:T(8,128)(2,1)S(1)} collective-permute-done((bf16[208,384]{1,0:T(8,128)(2,1)S(1)}, bf16[208,384]{1,0:T(8,128)(2,1)S(1)}, u32[]{:S(2)}, u32[]{:S(2)}) %collective-permute-start.2) | collective-permute-done | bytes 159776 | tf_op jit(solution)/shard_map/ppermute | solution.py:40
  35.9 7.0 %collective-permute-done.4 = bf16[4,96,384]{2,1,0:T(8,128)(2,1)S(1)} collective-permute-done((bf16[4,96,384]{2,1,0:T(8,128)(2,1)S(1)}, bf16[4,96,384]{2,1,0:T(8,128)(2,1)S(1)}, u32[]{:S(2)}, u32[]{:S(2)}) %collective-permute-start.4) | collective-permute-done | bytes 294944 | tf_op jit(solution)/shard_map/ppermute | solution.py:40
  46.2 18.1 %collective-permute-done.6 = bf16[8,96,384]{2,1,0:T(8,128)(2,1)} collective-permute-done((bf16[8,96,384]{2,1,0:T(8,128)(2,1)S(1)}, bf16[8,96,384]{2,1,0:T(8,128)(2,1)}, u32[]{:S(2)}, u32[]{:S(2)}) %collective-permute-start.6) | collective-permute-done | bytes 589856 | tf_op jit(solution)/shard_map/ppermute | solution.py:40
  109.2 23.2 %while.26 = (s32[]{:T(128)}, bf16[2,512,768]{2,1,0:T(8,128)(2,1)}, f32[2,12,512]{2,1,0:T(8,128)S(1)}, bf16[2,512,768]{1,2,0:T(8,128)(2,1)S(1)}, s32[2,8]{1,0:T(2...) while((s32[]{:T(128)}, bf16[2,512,768]{2,1,0:T(8,128)(2,1)}, ...), condition=%wide.region_5.6_spmd, body=%wide.region_0.5_spmd.sunk | while | flops 843716160 | bytes 50033424 | solution.py:323
  141.4 4.8 %slice.202 = bf16[768,3072]{1,0:T(8,128)(2,1)} slice(bf16[768,6144]{1,0:T(8,128)(2,1)} %all-gather.2.cloned.1.call-done), slice={[0:768], [3072:6144]} | slice | bytes 9437184 | tf_op jit(solution)/shard_map/slice | solution.py:315
  146.2 6.7 %copy.178 = bf16[768,3072]{0,1:T(8,128)(2,1)} copy(bf16[768,3072]{1,0:T(8,128)(2,1)} %slice.202) | data formatting | bytes 9437184 | tf_op jit(solution)/shard_map/slice | solution.py:315
  152.9 12.5 %multiply_convert_fusion.3 = (bf16[1024,3072]{1,0:T(8,128)(2,1)S(1)}, f32[1024,3072]{1,0:T(8,128)}) fusion(f32[3072]{0:T(1024)S(1)} %copy-done.37, bf16[768,6144]{1,0:T(8,128)(2,1)} %all-gather.2.cloned.1.call-done, f32[1024,768]{1,0:T(8,128)} %copy-done.5, f32[768]{0:T(1024)S(1)} %copy-done.48, f32[768]{0:T(1024)S(1)} %copy-done.45, ...), kind=kOutput, calls=%fused_computation.53 | convolution fusion | flops 4854644736 | bytes 26765312 | tf_op jit(solution)/shard_map/dot_general | solution.py:163
  165.4 5.4 %fusion.84 = (f32[1024]{0:T(1024)S(1)}, f32[1024,768]{1,0:T(8,128)S(1)}) fusion(f32[768]{0:T(1024)S(1)} %copy-done.51, bf16[768,4,768]{0,2,1:T(8,128)(2,1)S(1)} %bitcast.355, bf16[128,4,8,768]{3,2,1,0:T(8,128)(2,1)S(1)} %bitcast.411, f32[768]{0:T(1024)S(1)} %copy-done.48, f32[768]{0:T(1024)S(1)} %copy-done.45, f32[1024]{0:T(1024)S(1)} %add_rsqrt_fusion.1, ...), kind=kOutput, calls=%fused_computation.225 | convolution fusion | flops 4837342208 | bytes 17323008 | tf_op jit(solution)/shard_map/tgi,ign->tn/dot_general | solution.py:335
  176.9 8.1 %fusion.52 = f32[768,4,1024]{2,0,1:T(8,128)} fusion(bf16[768,4,768]{0,2,1:T(8,128)(2,1)S(1)} %bitcast.356, f32[1024,768]{1,0:T(8,128)S(1)} %get-tuple-element.277), kind=kOutput, calls=%fused_computation.117 | convolution fusion | flops 4832624640 | bytes 20447232 | tf_op jit(solution)/shard_map/tn,ign->tgi/dot_general | solution.py:347
  185.0 7.4 %fusion.41 = bf16[768,4,768]{2,0,1:T(8,128)(2,1)} fusion(bf16[128,4,8,768]{3,2,1,0:T(8,128)(2,1)S(1)} %bitcast.412, f32[1024,768]{1,0:T(8,128)S(1)} %get-tuple-element.277), kind=kOutput, calls=%fused_computation.103 | convolution fusion | flops 4834983936 | bytes 14155776 | tf_op jit(solution)/shard_map/tgi,tn->ign/dot_general | solution.py:346
  192.4 12.6 %copy.222 = f32[1024,3072]{1,0:T(8,128)} copy(f32[1024,3072]{0,1:T(8,128)} %bitcast.347) | data formatting | bytes 25165824 | tf_op jit(solution)/shard_map/reshape | solution.py:349
  205.0 11.6 %convert_reduce_fusion.2 = (f32[3072]{0:T(1024)}, bf16[1024,3072]{1,0:T(8,128)(2,1)S(1)}) fusion(f32[1024,3072]{1,0:T(8,128)} %copy.222, f32[1024,3072]{1,0:T(8,128)} %get-tuple-element.323, f32[3072]{0:T(1024)S(1)} %copy-done.37), kind=kLoop, calls=%fused_computation.52 | loop fusion | flops 40891392 | bytes 31481856 | tf_op jit(solution)/shard_map/reduce_sum | solution.py:350
  216.6 7.8 %convolution_convert_fusion = bf16[768,3072]{1,0:T(8,128)(2,1)} fusion(bf16[1024,3072]{1,0:T(8,128)(2,1)S(1)} %get-tuple-element.275, f32[1024,768]{1,0:T(8,128)S(1)} %copy-done.7, f32[768]{0:T(1024)S(1)} %copy-done.48, f32[768]{0:T(1024)S(1)} %copy-done.45, f32[1024]{0:T(1024)S(1)} %add_rsqrt_fusion.1, f32[1024]{0:T(1024)S(1)} %broadcast_multiply_fusion.4), kind=kOutput, calls=%fused_computation.68 | convolution fusion | flops 4838129664 | bytes 14170112 | tf_op jit(solution)/shard_map/ta,tb->ab/dot_general | solution.py:167
  224.4 6.7 %copy.224 = bf16[768,3072]{1,0:T(8,128)(2,1)} copy(bf16[768,3072]{0,1:T(8,128)(2,1)} %bitcast.357) | data formatting | bytes 9437184 | tf_op jit(solution)/shard_map/reshape | solution.py:352
  231.1 9.0 %pad_maximum_fusion = bf16[768,6144]{1,0:T(8,128)(2,1)} fusion(bf16[768,3072]{1,0:T(8,128)(2,1)} %copy.224, bf16[768,3072]{1,0:T(8,128)(2,1)} %convolution_convert_fusion), kind=kLoop, calls=%fused_computation.58 | loop fusion | flops 18874368 | bytes 18874368 | tf_op jit(solution)/shard_map/concatenate | solution.py:352
  240.2 11.6 %multiply_reduce_fusion.1 = (f32[768]{0:T(1024)}, f32[1024]{0:T(1024)S(1)}, f32[1024]{0:T(1024)S(1)}, f32[768]{0:T(1024)}, f32[1024,768]{1,0:T(8,128)S(1)}) fusion(f32[1024,768]{1,0:T(8,128)} %copy-done.5, f32[1024]{0:T(1024)S(1)} %add_rsqrt_fusion.1, f32[1024]{0:T(1024)S(1)} %broadcast_multiply_fusion.4, f32[768]{0:T(1024)S(1)} %copy-done.45, ...), kind=kOutput, calls=%fused_computation.87 | convolution fusion | flops 4839698432 | bytes 20472832 | tf_op jit(solution)/shard_map/tb,ab->ta/dot_general | solution.py:171
  256.0 83.2 %while.27 = (s32[]{:T(128)}, bf16[2,512,768]{1,2,0:T(8,128)(2,1)}, bf16[2,512,768]{1,2,0:T(8,128)(2,1)}, bf16[2,512,768]{1,2,0:T(8,128)(2,1)}, bf16[2,512,768]{1...) while((s32[]{:T(128)}, bf16[2,512,768]{1,2,0:T(8,128)(2,1)}, ...), condition=%wide.region_18.19_spmd, body=%wide.region_14.18_spmd.sunk | while | flops 2062685696 | bytes 178959856 | solution.py:362
  259.1 6.7 %fusion.168 = f32[12,512,512]{1,2,0:T(8,128)} fusion(bf16[512,12,64]{0,2,1:T(8,128)(2,1)S(1)} %bitcast.329, bf16[512,12,64]{0,2,1:T(8,128)(2,1)S(1)} %bitcast.327), kind=kOutput, calls=%fused_computation.226.clone.1 | convolution fusion | flops 402653184 | bytes 14155776 | tf_op jit(solution)/shard_map/while/body/eval_jaxpr/qhd,khd->hqk/dot_general | solution.py:202
  269.0 11.5 %multiply_reduce_fusion.7 = (f32[12,512]{1,0:T(8,128)S(1)}, f32[12,512,512]{1,2,0:T(8,128)}) fusion(f32[12,512,512]{1,2,0:T(8,128)} %fusion.168, f32[12,512]{1,0:T(8,128)S(1)} %dynamic-slice_bitcast_fusion.10, pred[512,512]{0,1:T(8,128)(4,1)S(1)} %broadcast_compare_fusion.5, bf16[512,12,64]{0,2,1:T(8,128)(2,1)S(1)} %bitcast.332, ...), kind=kOutput, calls=%fused_computation.22.clone.1 | convolution fusion | flops 418375680 | bytes 27049984 | tf_op jit(solution)/shard_map/while/body/eval_jaxpr/qhd,khd->hqk/dot_general | solution.py:238
  282.8 7.2 %multiply_convert_fusion.7 = bf16[12,512,512]{1,2,0:T(8,128)(2,1)S(1)} fusion(f32[12,512,512]{1,2,0:T(8,128)} %get-tuple-element.445, f32[12,512,512]{1,2,0:T(8,128)S(1)} %bitcast.326, f32[12,512]{1,0:T(8,128)S(1)} %get-tuple-element.446, f32[12,512]{1,0:T(8,128)S(1)} %dynamic-slice_bitcast_fusion.10, pred[512,512]{0,1:T(8,128)(4,1)S(1)} %broadcast_compare_fusion.5), kind=kLoop, calls=%fused_computation.21.clone.1 | loop fusion | flops 18874368 | bytes 31768576 | tf_op jit(solution)/shard_map/while/body/eval_jaxpr/convert_element_type | solution.py:242
  301.1 6.4 %fusion.168 = f32[12,512,512]{1,2,0:T(8,128)} fusion(bf16[512,12,64]{0,2,1:T(8,128)(2,1)S(1)} %bitcast.329, bf16[512,12,64]{0,2,1:T(8,128)(2,1)S(1)} %bitcast.327), kind=kOutput, calls=%fused_computation.226.clone.1 | convolution fusion | flops 402653184 | bytes 14155776 | tf_op jit(solution)/shard_map/while/body/eval_jaxpr/qhd,khd->hqk/dot_general | solution.py:202
  310.7 11.1 %multiply_reduce_fusion.7 = (f32[12,512]{1,0:T(8,128)S(1)}, f32[12,512,512]{1,2,0:T(8,128)}) fusion(f32[12,512,512]{1,2,0:T(8,128)} %fusion.168, f32[12,512]{1,0:T(8,128)S(1)} %dynamic-slice_bitcast_fusion.10, pred[512,512]{0,1:T(8,128)(4,1)S(1)} %broadcast_compare_fusion.5, bf16[512,12,64]{0,2,1:T(8,128)(2,1)S(1)} %bitcast.332, ...), kind=kOutput, calls=%fused_computation.22.clone.1 | convolution fusion | flops 418375680 | bytes 27049984 | tf_op jit(solution)/shard_map/while/body/eval_jaxpr/qhd,khd->hqk/dot_general | solution.py:238
  323.7 7.1 %multiply_convert_fusion.7 = bf16[12,512,512]{1,2,0:T(8,128)(2,1)S(1)} fusion(f32[12,512,512]{1,2,0:T(8,128)} %get-tuple-element.445, f32[12,512,512]{1,2,0:T(8,128)S(1)} %bitcast.326, f32[12,512]{1,0:T(8,128)S(1)} %get-tuple-element.446, f32[12,512]{1,0:T(8,128)S(1)} %dynamic-slice_bitcast_fusion.10, pred[512,512]{0,1:T(8,128)(4,1)S(1)} %broadcast_compare_fusion.5), kind=kLoop, calls=%fused_computation.21.clone.1 | loop fusion | flops 18874368 | bytes 31768576 | tf_op jit(solution)/shard_map/while/body/eval_jaxpr/convert_element_type | solution.py:242
  401.5 5.2 %collective-permute-done.15 = bf16[4,96,384]{2,1,0:T(8,128)(2,1)S(1)} collective-permute-done((bf16[4,96,384]{2,1,0:T(8,128)(2,1)S(1)}, bf16[4,96,384]{2,1,0:T(8,128)(2,1)S(1)}, u32[]{:S(2)}, u32[]{:S(2)}) %collective-permute-start.15) | collective-permute-done | bytes 294944 | tf_op jit(solution)/shard_map/ppermute | solution.py:40
  (401 shorter events, 228.6 us)
Async XLA Ops:
  7.3 134.1 %all-gather.2.cloned.1.call-start = ((), (), s32[]{:S(2)}) async-start(), calls=%async_computation.1 | async-start | bytes 9732096 | tf_op jit(solution)/shard_map/all_gather | solution.py:290
  11.8 412.7 %reduce-scatter.2.cloned.1.call-start = ((), (), s32[]{:S(2)}) async-start(), calls=%async_computation.2 | async-start | bytes 9732096 | tf_op jit(solution)/shard_map/reduce_scatter | solution.py:353
  12.0 1.4 collective-permute-start
  13.5 10.0 %collective-permute-start.1 = (bf16[208,384]{1,0:T(8,128)(2,1)S(1)}, bf16[208,384]{1,0:T(8,128)(2,1)S(1)}, u32[]{:S(2)}, u32[]{:S(2)}) collective-permute-start(bf16[208,384]{1,0:T(8,128)(2,1)S(1)} %fusion.59), channel_id=1, source_target_pairs={{0,8},{1,9},{2,10},{3,11},{4,12},{5,13},{6,14},{7,15},{8,16},{9,17... | collective-permute-start | bytes 479240 | tf_op jit(solution)/shard_map/ppermute | solution.py:40
  16.5 16.3 %collective-permute-start.2 = (bf16[208,384]{1,0:T(8,128)(2,1)S(1)}, bf16[208,384]{1,0:T(8,128)(2,1)S(1)}, u32[]{:S(2)}, u32[]{:S(2)}) collective-permute-start(bf16[208,384]{1,0:T(8,128)(2,1)S(1)} %fusion.59), channel_id=1, source_target_pairs={{0,16},{1,17},{2,18},{3,19},{4,20},{5,21},{6,22},{7,23},{8,24},{9,... | collective-permute-start | bytes 479240 | tf_op jit(solution)/shard_map/ppermute | solution.py:40
  19.1 13.7 %collective-permute-start.3 = (bf16[208,384]{1,0:T(8,128)(2,1)S(1)}, bf16[208,384]{1,0:T(8,128)(2,1)S(1)}, u32[]{:S(2)}, u32[]{:S(2)}) collective-permute-start(bf16[208,384]{1,0:T(8,128)(2,1)S(1)} %fusion.59), channel_id=1, source_target_pairs={{0,24},{1,25},{2,26},{3,27},{4,28},{5,29},{6,30},{7,31},{8,0},{9,1... | collective-permute-start | bytes 479240 | tf_op jit(solution)/shard_map/ppermute | solution.py:40
  32.8 10.0 %collective-permute-start.5 = (bf16[4,112,384]{2,1,0:T(8,128)(2,1)S(1)}, bf16[4,112,384]{2,1,0:T(8,128)(2,1)S(1)}, u32[]{:S(2)}, u32[]{:S(2)}) collective-permute-start(bf16[4,112,384]{2,1,0:T(8,128)(2,1)S(1)} %pad_maximum_fusion.6), channel_id=1, source_target_pairs={{0,4},{1,5},{2,6},{3,7},{4,0},{5,1},{6,2},{7,3},{8,12},{9,13},{10,... | collective-permute-start | bytes 1032200 | tf_op jit(solution)/shard_map/ppermute | solution.py:40
  34.5 8.4 %collective-permute-start.4 = (bf16[4,96,384]{2,1,0:T(8,128)(2,1)S(1)}, bf16[4,96,384]{2,1,0:T(8,128)(2,1)S(1)}, u32[]{:S(2)}, u32[]{:S(2)}) collective-permute-start(bf16[4,96,384]{2,1,0:T(8,128)(2,1)S(1)} %pad_maximum_fusion.9), channel_id=1, source_target_pairs={{0,2},{1,3},{2,0},{3,1},{4,6},{5,7},{6,4},{7,5},{8,10},{9,11},{10,... | collective-permute-start | bytes 884744 | tf_op jit(solution)/shard_map/ppermute | solution.py:40
  43.0 24.5 %collective-permute-start.7 = (bf16[8,112,384]{2,1,0:T(8,128)(2,1)S(1)}, bf16[8,112,384]{2,1,0:T(8,128)(2,1)}, u32[]{:S(2)}, u32[]{:S(2)}) collective-permute-start(bf16[8,112,384]{2,1,0:T(8,128)(2,1)S(1)} %constant_dynamic-update-slice_fusion.6), channel_id=1, source_target_pairs={{0,2},{1,3},{2,0},{3,1},{4,6},{5,7},{6,4},{7,5},{8,10},{9,11},{10,... | collective-permute-start | bytes 2064392 | tf_op jit(solution)/shard_map/ppermute | solution.py:40
  44.6 22.9 %collective-permute-start.9 = (bf16[8,112,384]{2,1,0:T(8,128)(2,1)S(1)}, bf16[8,112,384]{2,1,0:T(8,128)(2,1)S(1)}, u32[]{:S(2)}, u32[]{:S(2)}) collective-permute-start(bf16[8,112,384]{2,1,0:T(8,128)(2,1)S(1)} %constant_dynamic-update-slice_fusion.6), channel_id=1, source_target_pairs={{0,1},{1,0},{2,3},{3,2},{4,5},{5,4},{6,7},{7,6},{8,9},{9,8},{10,11... | collective-permute-start | bytes 2064392 | tf_op jit(solution)/shard_map/ppermute | solution.py:40
  44.7 19.6 %collective-permute-start.6 = (bf16[8,96,384]{2,1,0:T(8,128)(2,1)S(1)}, bf16[8,96,384]{2,1,0:T(8,128)(2,1)}, u32[]{:S(2)}, u32[]{:S(2)}) collective-permute-start(bf16[8,96,384]{2,1,0:T(8,128)(2,1)S(1)} %constant_dynamic-update-slice_fusion.4), channel_id=1, source_target_pairs={{0,4},{1,5},{2,6},{3,7},{4,0},{5,1},{6,2},{7,3},{8,12},{9,13},{10,... | collective-permute-start | bytes 1769480 | tf_op jit(solution)/shard_map/ppermute | solution.py:40
  46.0 18.3 %collective-permute-start.8 = (bf16[8,96,384]{2,1,0:T(8,128)(2,1)S(1)}, bf16[8,96,384]{2,1,0:T(8,128)(2,1)S(1)}, u32[]{:S(2)}, u32[]{:S(2)}) collective-permute-start(bf16[8,96,384]{2,1,0:T(8,128)(2,1)S(1)} %constant_dynamic-update-slice_fusion.4), channel_id=1, source_target_pairs={{0,1},{1,0},{2,3},{3,2},{4,5},{5,4},{6,7},{7,6},{8,9},{9,8},{10,11... | collective-permute-start | bytes 1769480 | tf_op jit(solution)/shard_map/ppermute | solution.py:40
  67.4 7.7 %collective-permute-start.11 = (bf16[8,112,384]{2,1,0:T(8,128)(2,1)}, bf16[8,112,384]{2,1,0:T(8,128)(2,1)}, u32[]{:S(2)}, u32[]{:S(2)}) collective-permute-start(bf16[8,112,384]{2,1,0:T(8,128)(2,1)} %collective-permute-done.7), channel_id=1, source_target_pairs={{0,1},{1,0},{2,3},{3,2},{4,5},{5,4},{6,7},{7,6},{8,9},{9,8},{10,11... | collective-permute-start | bytes 2064392 | tf_op jit(solution)/shard_map/ppermute | solution.py:40
  67.4 9.3 %collective-permute-start.10 = (bf16[8,96,384]{2,1,0:T(8,128)(2,1)}, bf16[8,96,384]{2,1,0:T(8,128)(2,1)}, u32[]{:S(2)}, u32[]{:S(2)}) collective-permute-start(bf16[8,96,384]{2,1,0:T(8,128)(2,1)} %collective-permute-done.6), channel_id=1, source_target_pairs={{0,1},{1,0},{2,3},{3,2},{4,5},{5,4},{6,7},{7,6},{8,9},{9,8},{10,11... | collective-permute-start | bytes 1769480 | tf_op jit(solution)/shard_map/ppermute | solution.py:40
  366.3 5.0 %collective-permute-start.12 = (bf16[16,208,384]{2,1,0:T(8,128)(2,1)S(1)}, bf16[16,208,384]{2,1,0:T(8,128)(2,1)}, u32[]{:S(2)}, u32[]{:S(2)}) collective-permute-start(bf16[16,208,384]{2,1,0:T(8,128)(2,1)S(1)} %dynamic-slice_convert_fusion), channel_id=1, source_target_pairs={{0,1},{1,0},{2,3},{3,2},{4,5},{5,4},{6,7},{7,6},{8,9},{9,8},{10,11... | collective-permute-start | bytes 7667720 | tf_op jit(solution)/shard_map/ppermute | solution.py:40
  377.4 18.3 %collective-permute-start.14 = (bf16[4,2,112,384]{3,2,1,0:T(8,128)(2,1)}, bf16[4,2,112,384]{3,2,1,0:T(8,128)(2,1)S(1)}, u32[]{:S(2)}, u32[]{:S(2)}) collective-permute-start(bf16[4,2,112,384]{3,2,1,0:T(8,128)(2,1)} %dynamic-slice_bitcast_fusion.1), channel_id=1, source_target_pairs={{0,2},{1,3},{2,0},{3,1},{4,6},{5,7},{6,4},{7,5},{8,10},{9,11},{10,... | collective-permute-start | bytes 2064392 | tf_op jit(solution)/shard_map/ppermute | solution.py:40
  380.0 15.7 %collective-permute-start.13 = (bf16[4,2,96,384]{3,2,0,1:T(8,128)(2,1)}, bf16[4,2,96,384]{3,2,0,1:T(8,128)(2,1)}, u32[]{:S(2)}, u32[]{:S(2)}) collective-permute-start(bf16[4,2,96,384]{3,2,0,1:T(8,128)(2,1)} %dynamic-slice_bitcast_fusion.2), channel_id=1, source_target_pairs={{0,4},{1,5},{2,6},{3,7},{4,0},{5,1},{6,2},{7,3},{8,12},{9,13},{10,... | collective-permute-start | bytes 1769480 | tf_op jit(solution)/shard_map/ppermute | solution.py:40
  396.0 10.7 %collective-permute-start.16 = (bf16[4,112,384]{2,1,0:T(8,128)(2,1)S(1)}, bf16[4,112,384]{2,1,0:T(8,128)(2,1)S(1)}, u32[]{:S(2)}, u32[]{:S(2)}) collective-permute-start(bf16[4,112,384]{2,1,0:T(8,128)(2,1)S(1)} %dynamic-slice_bitcast_fusion.3), channel_id=1, source_target_pairs={{0,4},{1,5},{2,6},{3,7},{4,0},{5,1},{6,2},{7,3},{8,12},{9,13},{10,... | collective-permute-start | bytes 1032200 | tf_op jit(solution)/shard_map/ppermute | solution.py:40
  398.6 8.1 %collective-permute-start.15 = (bf16[4,96,384]{2,1,0:T(8,128)(2,1)S(1)}, bf16[4,96,384]{2,1,0:T(8,128)(2,1)S(1)}, u32[]{:S(2)}, u32[]{:S(2)}) collective-permute-start(bf16[4,96,384]{2,1,0:T(8,128)(2,1)S(1)} %dynamic-slice_bitcast_fusion.4), channel_id=1, source_target_pairs={{0,2},{1,3},{2,0},{3,1},{4,6},{5,7},{6,4},{7,5},{8,10},{9,11},{10,... | collective-permute-start | bytes 884744 | tf_op jit(solution)/shard_map/ppermute | solution.py:40
  400.0 14.7 %copy-start.21 = (bf16[1,16,48,768]{3,2,0,1:T(8,128)(2,1)S(1)}, bf16[1,16,48,768]{3,2,0,1:T(8,128)(2,1)}, u32[]{:S(2)}) copy-start(bf16[1,16,48,768]{3,2,0,1:T(8,128)(2,1)} %copy-done.20) | copy-start | bytes 3538948
  407.0 11.1 %collective-permute-start.17 = (bf16[208,384]{1,0:T(8,128)(2,1)S(1)}, bf16[208,384]{1,0:T(8,128)(2,1)S(1)}, u32[]{:S(2)}, u32[]{:S(2)}) collective-permute-start(bf16[208,384]{1,0:T(8,128)(2,1)S(1)} %get-tuple-element.295), channel_id=1, source_target_pairs={{0,8},{1,9},{2,10},{3,11},{4,12},{5,13},{6,14},{7,15},{8,16},{9,17... | collective-permute-start | bytes 479240 | tf_op jit(solution)/shard_map/ppermute | solution.py:40
  411.4 11.0 %collective-permute-start.18 = (bf16[208,384]{1,0:T(8,128)(2,1)S(1)}, bf16[208,384]{1,0:T(8,128)(2,1)S(1)}, u32[]{:S(2)}, u32[]{:S(2)}) collective-permute-start(bf16[208,384]{1,0:T(8,128)(2,1)S(1)} %get-tuple-element.294), channel_id=1, source_target_pairs={{0,16},{1,17},{2,18},{3,19},{4,20},{5,21},{6,22},{7,23},{8,24},{9,... | collective-permute-start | bytes 479240 | tf_op jit(solution)/shard_map/ppermute | solution.py:40
  413.6 8.8 %collective-permute-start.19 = (bf16[208,384]{1,0:T(8,128)(2,1)S(1)}, bf16[208,384]{1,0:T(8,128)(2,1)S(1)}, u32[]{:S(2)}, u32[]{:S(2)}) collective-permute-start(bf16[208,384]{1,0:T(8,128)(2,1)S(1)} %get-tuple-element.293), channel_id=1, source_target_pairs={{0,24},{1,25},{2,26},{3,27},{4,28},{5,29},{6,30},{7,31},{8,0},{9,1... | collective-permute-start | bytes 479240 | tf_op jit(solution)/shard_map/ppermute | solution.py:40
  422.5 1.3 collective-permute-start.20
  (74 other events, 400.0 us)
Sparse Core Ops, SparseCore 0:
  11.9 95.9 all-gather.1
  240.3 139.4 reduce-scatter.1

commit v2 on v1

v2 whole, which is shorter than its diff:
```python
import functools

import jax
import jax.numpy as jnp
from jax import lax
from jax.experimental import pallas as pl
from jax.experimental.pallas import tpu as pltpu
from jax.sharding import PartitionSpec as P

EPSILON = 1e-06
SQRT_HALF = 0.7071067811865476
INV_ROOT = 0.3989422804014327
MOST = 128
HALF = 64
NEVER = -1e30
MEGA = 1024 * 1024

AXES = ("dp", "shard")
f32 = jnp.float32
bf16 = jnp.bfloat16
cat = jnp.concatenate


def moves(move):
    pairs = []
    for index in range(32):
        z, y, x, core = index // 8, (index // 4) % 2, (index // 2) % 2, index % 2
        z, y, x, core = move(z, y, x, core)
        pairs.append((index, z * 8 + y * 4 + x * 2 + core))
    return pairs


MOVES = {
    "core": moves(lambda z, y, x, core: (z, y, x, 1 - core)),
    "x": moves(lambda z, y, x, core: (z, y, 1 - x, core)),
    "y": moves(lambda z, y, x, core: (z, 1 - y, x, core)),
    "z1": moves(lambda z, y, x, core: ((z + 1) % 4, y, x, core)),
    "z2": moves(lambda z, y, x, core: ((z + 2) % 4, y, x, core)),
    "z3": moves(lambda z, y, x, core: ((z + 3) % 4, y, x, core)),
}


def send(values, move):
    return lax.ppermute(values, AXES, MOVES[move])


def place():
    major, minor = lax.axis_index("dp"), lax.axis_index("shard")
    return major // 2, major % 2, minor // 2, minor % 2


def phase(*values):
    return lax.optimization_barrier(values)


def add(*terms):
    total = terms[0].astype(f32)
    for term in terms[1:]:
        total = total + term.astype(f32)
    return total


def gather_blocks(block, split):
    one, two, three = send(block, "z1"), send(block, "z2"), send(block, "z3")
    one, two, three = phase(one, two, three)
    line = jnp.stack([block, one, two, three])
    first, second = line[:, :split], line[:, split:]
    first_x, second_y = send(first, "x"), send(second, "y")
    first_x, second_y, first, second = phase(first_x, second_y, first, second)
    first, second = cat([first, first_x]), cat([second, second_y])
    first_y, second_x = send(first, "y"), send(second, "x")
    other_first, other_second = send(first, "core"), send(second, "core")
    first, first_y, second, second_x, other_first, other_second = phase(
        first, first_y, second, second_x, other_first, other_second
    )
    other_first_y, other_second_x = send(first_y, "core"), send(second_x, "core")
    return first, first_y, second, second_x, other_first, other_first_y, other_second, other_second_x


def scatter_blocks(keep, away, split):
    z, y, x, core = place()
    got, keep = phase(send(away, "core"), keep)
    shape = (4, 2, 2, *keep.shape[1:])
    keep, got = keep.reshape(shape), got.reshape(shape)

    def pick(values, index, axis):
        return lax.dynamic_index_in_dim(values, index, axis, False)

    def part(index, axis, rows):
        return add(pick(keep, index, axis)[:, :, rows], pick(got, index, axis)[:, :, rows]).astype(bf16)

    top, rest = slice(0, split), slice(split, None)
    got_first = send(part(1 - y, 1, top), "y")
    got_second = send(part(1 - x, 2, rest), "x")
    first, second = part(y, 1, top), part(x, 2, rest)
    got_first, got_second, first, second = phase(got_first, got_second, first, second)

    def both(one, two, index):
        return add(pick(one, index, 1), pick(two, index, 1)).astype(bf16)

    got_first_x = send(both(first, got_first, 1 - x), "x")
    got_second_y = send(both(second, got_second, 1 - y), "y")
    first, second = both(first, got_first, x), both(second, got_second, y)
    got_first_x, got_second_y, first, second = phase(got_first_x, got_second_y, first, second)
    line = cat([add(first, got_first_x), add(second, got_second_y)], 1)
    low = line.astype(bf16)
    one = send(pick(low, (z + 1) % 4, 0), "z1")
    two = send(pick(low, (z + 2) % 4, 0), "z2")
    three = send(pick(low, (z + 3) % 4, 0), "z3")
    mine = pick(line, z, 0)
    one, two, three, mine = phase(one, two, three, mine)
    return add(mine, one, two, three)


def gather_attention(matrices, vector):
    z, y, x, core = place()
    count, rows, width = matrices.shape
    half = width // 2
    mine = lax.dynamic_slice_in_dim(matrices, core * half, half, 2)
    got = send(lax.dynamic_slice_in_dim(matrices, (1 - core) * half, half, 2), "core")
    pair = jnp.where(core == 0, cat([mine, got], 1), cat([got, mine], 1))
    vector_rows = jnp.pad(vector[None], ((0, 15), (0, half - vector.shape[0])))
    block = cat([pair.reshape(count * 2 * rows, half), vector_rows])
    (block,) = phase(block)
    return gather_blocks(block, count * rows)


def scatter_attention(keep, away, count, rows, entries):
    z, y, x, core = place()
    half = keep.shape[2]
    line = scatter_blocks(keep, away, count * rows)
    size = count * 2 * rows
    mine = line[:size].reshape(count, 2, rows, half)
    kept = lax.dynamic_index_in_dim(mine, core, 1, False)
    got = send(lax.dynamic_index_in_dim(mine, 1 - core, 1, False).astype(bf16), "core").astype(f32)
    whole = jnp.where(core == 0, cat([kept, got], 2), cat([got, kept], 2))
    return whole, line[size, :entries]


def gather_attention_any(matrices, vector):
    mats = lax.all_gather(matrices, AXES, axis=1, tiled=True)
    return mats, lax.all_gather(vector, AXES, axis=0, tiled=False)


def scatter_attention_any(matrices, vectors):
    mats = lax.psum_scatter(matrices.astype(bf16), AXES, scatter_dimension=1, tiled=True)
    return mats.astype(f32), lax.psum_scatter(vectors, AXES, scatter_dimension=0, tiled=False)


def dot(left, right):
    return lax.dot_general(left, right, (((1,), (0,)), ((), ())), preferred_element_type=f32)


def dot_nt(left, right):
    return lax.dot_general(left, right, (((1,), (1,)), ((), ())), preferred_element_type=f32)


def dot_tn(left, right):
    return lax.dot_general(left, right, (((0,), (0,)), ((), ())), preferred_element_type=f32)


def mean(values):
    return jnp.sum(values, axis=1, keepdims=True) * (1.0 / values.shape[1])


def spans(length, block):
    return [(start, max(0, start - MOST), min(length, start + block + MOST)) for start in range(0, length, block)]


def make_marks(lengths, row, marks):
    length, count = marks.shape[1], lengths.shape[1]
    position = lax.broadcasted_iota(jnp.int32, (length, 128), 0)
    lane = lax.broadcasted_iota(jnp.int32, (length, 128), 1)
    number, end = jnp.zeros((length, 128), jnp.int32), jnp.int32(0)
    for pair in range(count):
        end = end + lengths[row, pair]
        number = number + (position >= end).astype(jnp.int32)
    for head in (0, 1):
        at = lane - HALF * (1 - head)
        used = (at >= 0) & (at < count)
        marks[head] = jnp.where(used & (number == at), 1.0, 0.0).astype(bf16)
        marks[2 + head] = jnp.where(used & (number != at), NEVER, 0.0).astype(bf16)


def lanes(head, value=1.0):
    lane = lax.broadcasted_iota(jnp.int32, (16, 128), 1)
    return jnp.where((lane < HALF) if head == 0 else (lane >= HALF), value, 0.0).astype(bf16)[:1]


def spread(half, width, share):
    source = lax.broadcasted_iota(jnp.int32, (half, width), 0)
    target = lax.broadcasted_iota(jnp.int32, (half, width), 1)
    return jnp.where(source % share == target % share, 1.0, 0.0).astype(bf16)


def load_weights(spot, blocks, weights, vector_blocks, sem):
    z, y, x, core = spot[0], spot[1], spot[2], spot[3]
    copies = []
    rows = 48
    half = weights.shape[2] // 2
    for index, block in enumerate(blocks):
        side = core if index < 4 else 1 - core
        columns = pl.ds(pl.multiple_of(side * half, 128), half)
        for near in (0, 1):
            for step in range(4):
                far = index % 2
                if index % 4 < 2:
                    cy, cx = jnp.bitwise_xor(y, far), jnp.bitwise_xor(x, near)
                else:
                    cy, cx = jnp.bitwise_xor(y, near), jnp.bitwise_xor(x, far)
                chip = lax.rem(z - step + 4, 4) * 4 + cy * 2 + cx
                target = pl.ds(pl.multiple_of(chip * rows, 16), rows)
                at = near * 4 + step
                for unit in (0, 1):
                    matrix = unit if index % 4 < 2 else 2 + unit
                    copies.append(
                        pltpu.make_async_copy(
                            block.at[at, pl.ds(unit * rows, rows)], weights.at[matrix, target, columns], sem
                        )
                    )
                if index % 4 >= 2:
                    copies.append(
                        pltpu.make_async_copy(
                            block.at[at, pl.ds(2 * rows, 16)], vector_blocks.at[chip * 2 + side], sem
                        )
                    )
    for copy in copies:
        copy.start()
    for copy in copies:
        copy.wait()


def spread_vectors(vector_blocks, vec, share):
    devices, _, half = vector_blocks.shape
    width = vec.shape[1]
    groups = 12
    entries = jnp.sum(vector_blocks[...].astype(f32), axis=1)
    lane = lax.broadcasted_iota(jnp.int32, (devices, half), 1)
    parts = [jnp.where(lane // share == group, entries, 0.0) for group in range(groups)]
    wide = dot(cat(parts).astype(bf16), spread(half, width, share))
    owner = lax.broadcasted_iota(jnp.int32, (devices, width), 1) // share
    device = lax.broadcasted_iota(jnp.int32, (devices, width), 0)
    for group in range(groups):
        part = wide[group * devices : (group + 1) * devices]
        vec[group : group + 1, :] = jnp.sum(jnp.where(owner == device, part, 0.0), axis=0, keepdims=True)


def attend_kernel(known, block, share, lengths, spot, x, *refs):
    if known:
        blocks, refs = refs[:8], refs[8:]
        q_out, k_out, v_out, mixed, lse, normed, inverse, w, vec, marks, vector_blocks, sem = refs
    else:
        w, vec, q_out, k_out, v_out, mixed, lse, normed, inverse, marks = refs
    row = pl.program_id(0)
    length, width = x.shape
    make_marks(lengths, row, marks)
    if known:

        @pl.when(row == 0)
        def _():
            load_weights(spot, blocks, w, vector_blocks, sem)
            spread_vectors(vector_blocks, vec, share)

    tokens = x[...]
    q_out[...] = (dot(tokens, w[0]) + vec[0:1, :]).astype(bf16)
    k_out[...] = dot(tokens, w[1]).astype(bf16)
    v_out[...] = (dot(tokens, w[2]) + vec[1:2, :]).astype(bf16)
    keep = (lanes(0), lanes(1))
    keep_scaled = (lanes(0, 0.125), lanes(1, 0.125))
    pairs, parts = width // 128, spans(length, block)

    def scores_of(pair):
        tile = pl.ds(pair * 128, 128)
        q, k, v = q_out[:, tile], k_out[:, tile], v_out[:, tile]
        qs = [q * keep_scaled[h] + marks[h] for h in (0, 1)]
        ks = [k * keep[h] + marks[2 + h] for h in (0, 1)]
        vs = [v * keep[h] + keep[1 - h] for h in (0, 1)]
        scores = [
            [dot_nt(ks[h][first:last], qs[h][start : start + block]) for h in (0, 1)] for start, first, last in parts
        ]
        return scores, vs

    upcoming = scores_of(0)
    for pair in range(pairs):
        scores, vs = upcoming
        if pair + 1 < pairs:
            upcoming = scores_of(pair + 1)
        tops = [[jnp.max(s, axis=0, keepdims=True) for s in both] for both in scores]
        probs = [[jnp.exp(s - t).astype(bf16) for s, t in zip(both, top)] for both, top in zip(scores, tops)]
        mixes = [
            [dot_tn(vs[h][first:last], probs[i][h]) for h in (0, 1)] for i, (start, first, last) in enumerate(parts)
        ]
        for i, (start, first, last) in enumerate(parts):
            out = []
            for h in (0, 1):
                mix = mixes[i][h]
                total = mix[HALF : HALF + 1] if h == 0 else mix[:1]
                lse[0, 2 * pair + h : 2 * pair + h + 1, start : start + block] = tops[i][h] + jnp.log(total)
                out.append((mix[:HALF] if h == 0 else mix[HALF:]) * (1.0 / total))
            mixed[start : start + block, pair * 128 : pair * 128 + 128] = jnp.transpose(cat(out)).astype(bf16)
    for start in range(0, length, 256):
        rows = pl.ds(start, 256)
        total = x[rows, :].astype(f32) + dot(mixed[rows, :], w[3]) + vec[2:3, :]
        centred = total - mean(total)
        inv = lax.rsqrt(mean(centred * centred) + EPSILON)
        normed[rows, :] = centred * inv
        inverse[rows, :] = jnp.broadcast_to(inv, (256, 128))


def attend_forward(known, x, gathered, lengths, spot, rows, share, block=128):
    tokens, width = x.shape
    length = tokens // rows
    shape = jax.ShapeDtypeStruct
    tile = pl.BlockSpec((length, width), lambda r, *_: (r, 0))
    fixed = [pl.BlockSpec((4, width, width), lambda r, *_: (0, 0, 0)), pl.BlockSpec((16, width), lambda r, *_: (0, 0))]
    act = shape((tokens, width), bf16)
    out_specs = [tile] * 4 + [
        pl.BlockSpec((1, 16, length), lambda r, *_: (r, 0, 0)),
        tile,
        pl.BlockSpec((length, 128), lambda r, *_: (r, 0)),
    ]
    out_shape = [act] * 4 + [shape((rows, 16, length), f32), shape((tokens, width), f32), shape((tokens, 128), f32)]
    scratch = [pltpu.VMEM((4, length, 128), bf16)]
    if known:
        in_specs = [tile] + [pl.BlockSpec(memory_space=pl.ANY)] * 8
        out_specs, out_shape = out_specs + fixed, out_shape + [shape((4, width, width), bf16), shape((16, width), f32)]
        scratch += [pltpu.VMEM((32, 16, width // 2), bf16), pltpu.SemaphoreType.DMA]
    else:
        in_specs = [tile] + fixed
    return pl.pallas_call(
        functools.partial(attend_kernel, known, block, share),
        grid_spec=pltpu.PrefetchScalarGridSpec(
            num_scalar_prefetch=2, grid=(rows,), in_specs=in_specs, out_specs=out_specs, scratch_shapes=scratch
        ),
        out_shape=out_shape,
        compiler_params=pltpu.CompilerParams(vmem_limit_bytes=60 * MEGA),
        cost_estimate=pl.CostEstimate(flops=10 * 10**9, bytes_accessed=2 * 10**7, transcendentals=4 * 10**6),
        name="attend",
    )(lengths, spot, x, *gathered)


def back_kernel(block, lengths, q_in, k_in, v_in, mixed, lse, grad, dq_out, dk_out, dv_out, marks):
    row = pl.program_id(0)
    length, width = q_in.shape
    make_marks(lengths, row, marks)
    keep = (lanes(0), lanes(1))
    keep_scaled = (lanes(0, 0.125), lanes(1, 0.125))
    head_of = lax.broadcasted_iota(jnp.int32, (16, 128), 1) // HALF
    picker = jnp.where(lax.broadcasted_iota(jnp.int32, (16, 128), 0) == head_of, 1.0, 0.0).astype(bf16)
    pairs, parts = width // 128, spans(length, block)

    def products_of(pair):
        tile = pl.ds(pair * 128, 128)
        q, k, v, g = q_in[:, tile], k_in[:, tile], v_in[:, tile], grad[:, tile]
        product = g.astype(f32) * mixed[:, tile].astype(f32)
        high = product.astype(bf16)
        centre = dot_nt(picker, high) + dot_nt(picker, (product - high.astype(f32)).astype(bf16))
        qz = [q * keep_scaled[h] for h in (0, 1)]
        kz = [k * keep[h] for h in (0, 1)]
        vz = [v * keep[h] for h in (0, 1)]
        gz = [g * keep[h] for h in (0, 1)]
        qs = [qz[h] + marks[h] for h in (0, 1)]
        ks = [kz[h] + marks[2 + h] for h in (0, 1)]
        scores = [
            [dot_nt(ks[h][start : start + block], qs[h][first:last]) for h in (0, 1)] for start, first, last in parts
        ]
        slopes = [
            [dot_nt(vz[h][start : start + block], g[first:last]) for h in (0, 1)] for start, first, last in parts
        ]
        return scores, slopes, centre, qz, kz, gz

    upcoming = products_of(0)
    for pair in range(pairs):
        scores, slopes, centre, qz, kz, gz = upcoming
        if pair + 1 < pairs:
            upcoming = products_of(pair + 1)
        probs, grads = [], []
        for i, (start, first, last) in enumerate(parts):
            prob = [jnp.exp(scores[i][h] - lse[0, 2 * pair + h : 2 * pair + h + 1, first:last]) for h in (0, 1)]
            probs.append([p.astype(bf16) for p in prob])
            grads.append([(prob[h] * (slopes[i][h] - centre[h : h + 1, first:last])).astype(bf16) for h in (0, 1)])
        columns = slice(pair * 128, pair * 128 + 128)
        to_values = [
            sum(dot(probs[i][h], gz[h][first:last]) for h in (0, 1)) for i, (start, first, last) in enumerate(parts)
        ]
        to_keys = [
            sum(dot(grads[i][h], qz[h][first:last]) for h in (0, 1)) for i, (start, first, last) in enumerate(parts)
        ]
        to_queries = [
            sum(dot_tn(grads[i][h], kz[h][start : start + block]) for h in (0, 1))
            for i, (start, first, last) in enumerate(parts)
        ]
        for i, (start, first, last) in enumerate(parts):
            dv_out[start : start + block, columns] = to_values[i].astype(bf16)
            dk_out[start : start + block, columns] = to_keys[i].astype(bf16)
        for at in range(0, length, MOST):
            pieces = [
                to_queries[i][at - first : at - first + MOST]
                for i, (start, first, last) in enumerate(parts)
                if first <= at < last
            ]
            dq_out[at : at + MOST, columns] = (sum(pieces) * 0.125).astype(bf16)


def attend_back(q, k, v, mixed, lse, grad, lengths, rows, block=128):
    tokens, width = q.shape
    length = tokens // rows
    tile = pl.BlockSpec((length, width), lambda r, *_: (r, 0))
    return pl.pallas_call(
        functools.partial(back_kernel, block),
        grid_spec=pltpu.PrefetchScalarGridSpec(
            num_scalar_prefetch=1,
            grid=(rows,),
            in_specs=[tile] * 4 + [pl.BlockSpec((1, 16, length), lambda r, *_: (r, 0, 0)), tile],
            out_specs=[tile] * 3,
            scratch_shapes=[pltpu.VMEM((4, length, 128), bf16)],
        ),
        out_shape=[jax.ShapeDtypeStruct((tokens, width), bf16)] * 3,
        compiler_params=pltpu.CompilerParams(vmem_limit_bytes=60 * MEGA),
        cost_estimate=pl.CostEstimate(flops=12 * 10**9, bytes_accessed=2 * 10**7, transcendentals=4 * 10**6),
        name="attend_back",
    )(lengths, q, k, v, mixed, lse, grad)


def gelu_parts(u):
    bell = jnp.exp(u * u * -0.5)
    t = 1.0 / (1.0 + (0.3275911 * SQRT_HALF) * jnp.abs(u))
    poly = t * (0.127414796 + t * (-0.142248368 + t * (0.7107068705 + t * (-0.7265760135 + t * 0.5307027145))))
    tail = poly * bell
    phi = jnp.where(u >= 0.0, 1.0 - tail, tail)
    return u * phi, phi + u * (bell * INV_ROOT)


def ffn_kernel(
    chunks, size, weights, normed, inverse, cot, mixed, out_mat, vec, layer_out, grads, first, grad_mixed, grad_out, sums,
    w, low, act, slope, total, second_low, back, ready, loaded, sent,
):
    tokens, width = normed.shape
    copies = []
    for i in range(2 * chunks):
        columns = pl.ds(i * width, width)
        copies.append(pltpu.make_async_copy(weights.at[:, columns], w.at[:, columns], loaded.at[i]))
        copies[i].start()
    gain, shift = vec[3:4, :], vec[4:5, :]
    down_add, final_gain, final_shift = vec[5:6, :], vec[6:7, :], vec[7:8, :]

    def up(g):
        return w[:, g * width : (g + 1) * width]

    def down(g):
        return w[:, (chunks + g) * width : (chunks + g + 1) * width]

    low[...] = (normed[...] * gain + shift).astype(bf16)
    sums[...] = jnp.zeros_like(sums)
    for copy in copies:
        copy.wait()

    def forward(t, _):
        rows = pl.ds(pl.multiple_of(t * size, size), size)
        inputs = low[rows, :]
        pre, added = dot(inputs, up(0)), None
        for g in range(chunks):
            upcoming = dot(inputs, up(g + 1)) if g + 1 < chunks else None
            activated, derivative = gelu_parts(pre + vec[8 + g : 9 + g, :])
            activated = activated.astype(bf16)
            act[g, rows, :] = activated
            slope[g, rows, :] = derivative.astype(bf16)
            part = dot(activated, down(g))
            added = part if added is None else added + part
            pre = upcoming
        second_sum = normed[rows, :] * gain + shift + added + down_add
        centred = second_sum - mean(second_sum)
        inv = lax.rsqrt(mean(centred * centred) + EPSILON)
        hat = centred * inv
        layer_out[rows, :] = (hat * final_gain + final_shift).astype(bf16)
        grad = cot[rows, :].astype(f32)
        scaled = grad * final_gain
        second = inv * (scaled - mean(scaled) - hat * mean(scaled * hat))
        total[rows, :] = second
        second_low[rows, :] = second.astype(bf16)
        sums[0:1, :] += jnp.sum(second, axis=0, keepdims=True)
        sums[1:2, :] += jnp.sum(grad * hat, axis=0, keepdims=True)
        sums[2:3, :] += jnp.sum(grad, axis=0, keepdims=True)
        return 0

    lax.fori_loop(0, tokens // size, forward, 0)
    pending = []
    for g in range(chunks):
        to_act = dot_nt(second_low[...], down(g))
        to_down = dot_tn(act[g], second_low[...])
        to_pre = to_act * slope[g].astype(f32)
        sums[6 + g : 7 + g, :] = jnp.sum(to_pre, axis=0, keepdims=True)
        back[...] = to_pre.astype(bf16)
        slot = g % 2
        if g >= 2:
            for copy in pending[g - 2]:
                copy.wait()
        ready[slot, 1] = to_down.astype(bf16)
        total[...] += dot_nt(back[...], up(g))
        ready[slot, 0] = dot_tn(low[...], back[...]).astype(bf16)
        out = [
            pltpu.make_async_copy(
                ready.at[slot, j], grads.at[:, pl.ds((j * chunks + g) * width, width)], sent.at[slot, j]
            )
            for j in (0, 1)
        ]
        for copy in out:
            copy.start()
        pending.append(out)

    def backward(t, _):
        rows = pl.ds(pl.multiple_of(t * size, size), size)
        middle, hat, inv = total[rows, :], normed[rows, :], inverse[rows, 0:1]
        scaled = middle * gain
        to_first = inv * (scaled - mean(scaled) - hat * mean(scaled * hat))
        first[rows, :] = to_first
        to_low = to_first.astype(bf16)
        second_low[rows, :] = to_low
        sums[3:4, :] += jnp.sum(middle * hat, axis=0, keepdims=True)
        sums[4:5, :] += jnp.sum(middle, axis=0, keepdims=True)
        sums[5:6, :] += jnp.sum(to_first, axis=0, keepdims=True)
        grad_mixed[rows, :] = dot_nt(to_low, out_mat[0]).astype(bf16)
        return 0

    lax.fori_loop(0, tokens // size, backward, 0)
    grad_out[...] = dot_tn(mixed[...], second_low[...]).astype(bf16)
    for out in pending[-2:]:
        for copy in out:
            copy.wait()


def ffn(weights, normed, inverse, cot, mixed, mats, vec, size=256):
    tokens, width = normed.shape
    chunks = weights.shape[1] // (2 * width)
    shape = jax.ShapeDtypeStruct

    def full(value):
        return pl.BlockSpec(value.shape, lambda i: (0,) * len(value.shape))

    outs = [
        shape((tokens, width), bf16),
        shape(weights.shape, bf16),
        shape((tokens, width), f32),
        shape((tokens, width), bf16),
        shape((width, width), bf16),
        shape((16, width), f32),
    ]
    out_specs = [full(out) for out in outs]
    out_specs[1] = pl.BlockSpec(memory_space=pl.ANY)
    return pl.pallas_call(
        functools.partial(ffn_kernel, chunks, size),
        grid=(1,),
        in_specs=[
            pl.BlockSpec(memory_space=pl.ANY),
            full(normed),
            full(inverse),
            full(cot),
            full(mixed),
            pl.BlockSpec((1, width, width), lambda i: (3, 0, 0)),
            full(vec),
        ],
        out_specs=out_specs,
        out_shape=outs,
        scratch_shapes=[
            pltpu.VMEM(weights.shape, bf16),
            pltpu.VMEM((tokens, width), bf16),
            pltpu.VMEM((chunks, tokens, width), bf16),
            pltpu.VMEM((chunks, tokens, width), bf16),
            pltpu.VMEM((tokens, width), f32),
            pltpu.VMEM((tokens, width), bf16),
            pltpu.VMEM((tokens, width), bf16),
            pltpu.VMEM((2, 2, width, width), bf16),
            pltpu.SemaphoreType.DMA((2 * chunks,)),
            pltpu.SemaphoreType.DMA((2, 2)),
        ],
        compiler_params=pltpu.CompilerParams(vmem_limit_bytes=63 * MEGA),
        cost_estimate=pl.CostEstimate(flops=32 * 10**9, bytes_accessed=3 * 10**7, transcendentals=6 * 10**6),
        name="ffn",
    )(weights, normed, inverse, cot, mixed, mats, vec)


def weight_kernel(share, spot, x, dq, dk, dv, grad_out, sums, keep, away):
    core = spot[3]
    tokens, width = x.shape
    half, chips, rows = width // 2, keep.shape[0], 2 * share
    natural = [jnp.sum(dq[...].astype(f32), axis=0, keepdims=True), jnp.sum(dv[...].astype(f32), axis=0, keepdims=True)]
    natural += [sums[i : i + 1, :] for i in (5, 3, 4, 0, 1, 2, 6, 7, 8, 9)]
    owner = lax.broadcasted_iota(jnp.int32, (chips, width), 1) // share
    chip = lax.broadcasted_iota(jnp.int32, (chips, width), 0)
    lane = lax.broadcasted_iota(jnp.int32, (chips, half), 1)
    table = spread(half, width, share)
    top = lax.broadcasted_iota(jnp.int32, (chips, 16, half), 1) == 0
    for side, out in ((1 - core, away), (core, keep)):
        columns = pl.ds(pl.multiple_of(side * half, 128), half)
        for unit, grad in enumerate((dq, dk, dv)):
            block = dot_tn(x[...], grad[:, columns]).astype(bf16)
            out[:, unit * rows : (unit + 1) * rows, :] = block.reshape(chips, rows, half)
        out[:, 3 * rows : 4 * rows, :] = grad_out[:, columns].reshape(chips, rows, half)
        mine = owner == 2 * chip + side
        entries = jnp.zeros((chips, half), f32)
        spreads = dot_nt(cat([jnp.where(mine, row, 0.0) for row in natural]).astype(bf16), table)
        for group in range(len(natural)):
            part = spreads[group * chips : (group + 1) * chips]
            entries = entries + jnp.where(lane // share == group, part, 0.0)
        out[:, 4 * rows :, :] = jnp.where(top, entries[:, None, :], 0.0).astype(bf16)


def weight_blocks(x, dq, dk, dv, grad_out, sums, spot, share):
    width = x.shape[1]
    blocks = jax.ShapeDtypeStruct((16, 8 * share + 16, width // 2), bf16)
    vmem = pl.BlockSpec(memory_space=pltpu.VMEM)
    return pl.pallas_call(
        functools.partial(weight_kernel, share),
        in_specs=[pl.BlockSpec(memory_space=pltpu.SMEM)] + [vmem] * 6,
        out_specs=[vmem] * 2,
        out_shape=[blocks] * 2,
        compiler_params=pltpu.CompilerParams(vmem_limit_bytes=60 * MEGA),
        cost_estimate=pl.CostEstimate(flops=4 * 10**9, bytes_accessed=10**7, transcendentals=0),
        name="weight_blocks",
    )(spot, x, dq, dk, dv, grad_out, sums)


def outer_sum(left, right):
    return jnp.einsum("ta,tb->ab", left, right, preferred_element_type=jnp.float32)


def back_product(grads, weights):
    return jnp.einsum("tb,ab->ta", grads, weights, preferred_element_type=jnp.float32)


def per_device(
    known,
    hidden,
    pair_lengths,
    cotangent,
    query_weight,
    query_bias,
    key_weight,
    value_weight,
    value_bias,
    out_weight,
    out_bias,
    attn_gain,
    attn_shift,
    up_weight,
    up_bias,
    down_weight,
    down_bias,
    final_gain,
    final_shift,
):
    rows_here, length, width = hidden.shape
    count = rows_here * length
    share = query_weight.shape[0]
    devices = width // share
    chunks = up_weight.shape[1] // width
    up_mine = (
        up_weight.reshape(share, devices, chunks, share).swapaxes(1, 2).reshape(share, chunks * width)
    )
    down_mine = down_weight.reshape(chunks, share, width).swapaxes(0, 1).reshape(share, chunks * width)
    ffn_mine = cat([up_mine, down_mine], 1)
    ffn_full = lax.all_gather(ffn_mine, AXES, axis=0, tiled=True)
    vector = cat(
        [
            query_bias,
            value_bias,
            out_bias,
            attn_gain,
            attn_shift,
            down_bias,
            final_gain,
            final_shift,
            up_bias,
        ]
    )
    matrices = jnp.stack([query_weight, key_weight, value_weight, out_weight])
    tokens = hidden.reshape(count, width)
    groups = 8 + chunks
    z, y, x, core = place()
    if known:
        spot = jnp.stack([z, y, x, core]).astype(jnp.int32)
        gathered = gather_attention(matrices, vector)
        out = attend_forward(True, tokens, gathered, pair_lengths, spot, rows_here, share)
        queries, keys_all, values_all, mixed, log_totals, first_norm, first_inverse, mats, vec = out
    else:
        spot = jnp.zeros((4,), jnp.int32)
        mats, vectors = gather_attention_any(matrices, vector)
        vec = vectors.reshape(devices, groups, share).swapaxes(0, 1).reshape(groups, width).astype(f32)
        vec = jnp.pad(vec, ((0, 16 - groups), (0, 0)))
        out = attend_forward(False, tokens, (mats, vec), pair_lengths, spot, rows_here, share)
        queries, keys_all, values_all, mixed, log_totals, first_norm, first_inverse = out
    layer_out, ffn_grads, grad_first, grad_mixed, grad_out_weight, sums = ffn(
        ffn_full, first_norm, first_inverse, cotangent.reshape(count, width), mixed, mats, vec
    )
    ffn_owned = lax.psum_scatter(ffn_grads, AXES, scatter_dimension=0, tiled=True).astype(f32)
    grad_queries, grad_keys, grad_values = attend_back(
        queries, keys_all, values_all, mixed, log_totals, grad_mixed, pair_lengths, rows_here
    )
    if known:
        keep, away = weight_blocks(tokens, grad_queries, grad_keys, grad_values, grad_out_weight, sums, spot, share)
        mats_owned, vectors_owned = scatter_attention(keep, away, 4, share, groups * share)
    else:
        mat_grads = jnp.stack(
            [
                outer_sum(tokens, grad_queries),
                outer_sum(tokens, grad_keys),
                outer_sum(tokens, grad_values),
                grad_out_weight.astype(f32),
            ]
        )
        biases = jnp.stack([jnp.sum(grad_queries.astype(f32), 0), jnp.sum(grad_values.astype(f32), 0)])
        vector_grads = cat([biases, sums[5:6], sums[3:5], sums[:3], sums[6 : 6 + chunks]])
        vector_grads = vector_grads.reshape(groups, devices, share).swapaxes(0, 1).reshape(devices, groups * share)
        mats_owned, vectors_owned = scatter_attention_any(mat_grads, vector_grads)
    grad_tokens = (
        grad_first
        + back_product(grad_queries, mats[0])
        + back_product(grad_keys, mats[1])
        + back_product(grad_values, mats[2])
    )
    own = vectors_owned.reshape(8 + chunks, share)
    up_owned = (
        ffn_owned[:, : chunks * width]
        .reshape(share, chunks, devices, share)
        .swapaxes(1, 2)
        .reshape(share, chunks * width)
    )
    down_owned = (
        ffn_owned[:, chunks * width :].reshape(share, chunks, width).swapaxes(0, 1).reshape(chunks * share, width)
    )
    return (
        layer_out.reshape(hidden.shape),
        grad_tokens.reshape(hidden.shape),
        mats_owned[0],
        own[0],
        mats_owned[1],
        mats_owned[2],
        own[1],
        mats_owned[3],
        own[2],
        own[3],
        own[4],
        up_owned,
        own[8:].reshape(chunks * share),
        down_owned,
        own[5],
        own[6],
        own[7],
    )


def solution(mesh):
    known = dict(mesh.shape) == {"dp": 8, "shard": 4}
    cube, flat, line = P(AXES, None, None), P(AXES, None), P(AXES)
    return jax.shard_map(
        lambda *args: per_device(known, *args),
        mesh=mesh,
        in_specs=(
            cube, flat, cube, flat, line, flat, flat, line, flat, line, line, line, flat, line, flat, line, line, line,
        ),
        out_specs=(
            cube, cube, flat, line, flat, flat, line, flat, line, line, line, flat, line, flat, line, line, line,
        ),
        check_vma=False,
    )
```

time: 445 us -> 332 us (0.75)
  matrix products: 140 us -> 6.15 us
  Pallas kernels: 0 us -> 108 us
  local copies, waits for them, and re-layouts: 118 us -> 17.8 us
  waiting for transfers between devices: 58.1 us -> 153 us
  other arithmetic: 76.8 us -> 2.84 us
    dot_general x27 -> x0, matrix products: 118 us -> none  [the longest x2 22.7 us: attend_back(): jnp.einsum('qhd,khd->hqk', grad_heads, split_heads(value_rows), preferred...]
    pallas_call x0 -> x4, Pallas kernels: none -> 108 us  [the longest x1 56.3 us: ffn(): pl.pallas_call(functools.partial(ffn_kernel, chunks, size), grid=(1,), in...]
    reduce_scatter x1, waiting for transfers between devices: 0.01 us -> 52.5 us  [per_device(): lax.psum_scatter(ffn_grads, AXES, scatter_dimension=0, tiled=True)]
    ppermute x21, waiting for transfers between devices: 58 us -> 85.4 us  [send(): return lax.ppermute(values, AXES, MOVES[move])]
    reduce_sum x15 -> x0, other arithmetic: 27.2 us -> none  [the longest x1 11.6 us: per_device(): grad_up_bias = jnp.sum(grad_pre.astype(jnp.float32), 0)]
    concatenate x7 -> x0, other arithmetic: 22.2 us -> none  [the longest x1 9 us: per_device(): cat([grad_up.astype(bf16), grad_down.astype(bf16).reshape(width, chunks *...]
    reshape x6 -> x0, local copies, waits for them, and re-layouts: 19.8 us -> none  [the longest x1 12.6 us: per_device(): grad_act.reshape(pre_act.shape) * (cdf_part + pre_act * density)]
    slice x18 -> x0, local copies, waits for them, and re-layouts: 19.5 us -> none  [the longest x2 11.4 us: per_device(): down_mat = ffn_full[:, chunks * width:].reshape(width, chunks, width)]
  transfers between devices with their start and end apart: 23 -> 23, of which waited for: 11 -> 16; matrix products, arithmetic and copies ran while one was open for 49% -> 4% of each run, Pallas kernels for 0% -> 16%
where the time goes in v2:
time: 332 us; the launch traced here: 327 us
  waiting for transfers between devices  153 us (46%)
  Pallas kernels  108 us (33%)
  starting transfers between devices  24.4 us (7%)
  local copies, waits for them, and re-layouts  17.8 us (5%)
  between operations  14.9 us (4%)
  matrix products  6.15 us (2%)
    ppermute x21, waiting for transfers between devices, send(): return lax.ppermute(values, AXES, MOVES[move])  85.4 us
    pallas_call x1, Pallas kernels, ffn(): pl.pallas_call(functools.partial(ffn_kernel, chunks, size), grid=(1,), in...  56.3 us
    reduce_scatter x1, waiting for transfers between devices, per_device(): lax.psum_scatter(ffn_grads, AXES, scatter_dimension=0, tiled=True)  52.5 us
    ppermute x21, starting transfers between devices, send(): return lax.ppermute(values, AXES, MOVES[move])  24.3 us
    pallas_call x1, Pallas kernels, attend_forward(): pl.pallas_call(functools.partial(attend_kernel, known, block, share), gri...  21.5 us
    pallas_call x1, Pallas kernels, attend_back(): pl.pallas_call(functools.partial(back_kernel, block), grid_spec=pltpu.Pre...  18.8 us
    all_gather x1, waiting for transfers between devices, per_device(): ffn_full = lax.all_gather(ffn_mine, AXES, axis=0, tiled=True)  15 us
    pallas_call x1, Pallas kernels, weight_blocks(): pl.pallas_call(functools.partial(weight_kernel, share), in_specs=[pl.Bloc...  11.7 us
  transfers between devices with their start and end apart: 23, of which 16 were waited for; matrix products, arithmetic and copies ran while one was open for 4% of the time, Pallas kernels for 16%

profile of v2, /device:TPU:0, one launch (start us, length us, event | category | flops | bytes accessed | tf_op | source)
XLA Modules:
  0.0 327.3 jit_solution(8785010208791976007)
XLA Ops:
  7.2 2.1 reshape.122
  13.5 3.0 collective-permute-start.1
  16.5 2.6 collective-permute-start.2
  20.4 3.1 collective-permute-done.1
  23.5 9.3 %collective-permute-done.2 = bf16[208,384]{1,0:T(8,128)(2,1)S(1)} collective-permute-done((bf16[208,384]{1,0:T(8,128)(2,1)S(1)}, bf16[208,384]{1,0:T(8,128)(2,1)S(1)}, u32[]{:S(2)}, u32[]{:S(2)}) %collective-permute-start.2) | collective-permute-done | bytes 159776 | tf_op jit(solution)/shard_map/ppermute | solution.py:44
  35.9 7.0 %collective-permute-done.4 = bf16[4,96,384]{2,1,0:T(8,128)(2,1)S(1)} collective-permute-done((bf16[4,96,384]{2,1,0:T(8,128)(2,1)S(1)}, bf16[4,96,384]{2,1,0:T(8,128)(2,1)S(1)}, u32[]{:S(2)}, u32[]{:S(2)}) %collective-permute-start.4) | collective-permute-done | bytes 294944 | tf_op jit(solution)/shard_map/ppermute | solution.py:44
  46.2 18.1 %collective-permute-done.6.refs_1_ = bf16[8,96,384]{2,1,0:T(8,128)(2,1)} collective-permute-done((bf16[8,96,384]{2,1,0:T(8,128)(2,1)S(1)}, bf16[8,96,384]{2,1,0:T(8,128)(2,1)}, u32[]{:S(2)}, u32[]{:S(2)}) %collective-permute-start.6) | collective-permute-done | bytes 589856 | tf_op jit(solution)/shard_map/ppermute | solution.py:44
  64.3 3.1 collective-permute-done.7.refs_3_
  68.5 2.2 collective-permute-done.10.refs_5_
  71.6 21.5 %attend.1 = (bf16[1024,768]{1,0:T(8,128)(2,1)}, bf16[1024,768]{1,0:T(8,128)(2,1)}, bf16[1024,768]{1,0:T(8,128)(2,1)}, bf16[1024,768]{1,0:T(8,128)(2,1)}, f32[2,1...) custom-call(s32[2,8]{1,0:T(2,128)} %lengths.3, ...), custom_call_target="tpu_custom_call" | custom-call | flops 10000000000 | bytes 20000000 | tf_op jit(solution)/shard_map/attend/pallas_call | solution.py:330
  93.1 15.0 %all-gather.2.cloned.1.call-done.weights = bf16[768,6144]{1,0:T(8,128)(2,1)} async-done(((bf16[24,6144]{1,0:T(8,128)(2,1)}), bf16[768,6144]{1,0:T(8,128)(2,1)}) %all-gather.2.cloned.1.call-update) | async-done | bytes 9437200 | tf_op jit(solution)/shard_map/all_gather | solution.py:662
  108.1 56.3 %ffn.1 = (bf16[1024,768]{1,0:T(8,128)(2,1)}, bf16[768,6144]{1,0:T(8,128)(2,1)}, f32[1024,768]{1,0:T(8,128)}, bf16[1024,768]{1,0:T(8,128)(2,1)}, bf16[768,768]{1,0:T(8,128)(2,1)}, /*index=5*/f32[16,768]{1,0:T(8,128)}) custom-call(bf16[768,6144]{1,0:T(8,128)(2,1)} %all-gather.2.cloned.1.call-done.weights, f32[1024,768]{1,0:T(8,128)} %get-tuple-element.77.normed, ...), custom_call_target="tpu_custom_call" | custom-call | flops 32000000000 | bytes 30000000 | tf_op jit(solution)/shard_map/ffn/pallas_call | solution.py:550
  164.5 18.8 %attend_back.1 = (bf16[1024,768]{1,0:T(8,128)(2,1)}, bf16[1024,768]{1,0:T(8,128)(2,1)}, bf16[1024,768]{1,0:T(8,128)(2,1)}) custom-call(s32[2,8]{1,0:T(2,128)} %lengths.3, bf16[1024,768]{1,0:T(8,128)(2,1)} %get-tuple-element.84.q_in, bf16[1024,768]{1,0:T(8,128)(2,1)} %get-tuple-element.85.k_in, bf16[1024,768]{1,0:T(8,128)(2,1)} %get-tuple-element.86.v_in, ...), custom_call_target="tpu_custom_call" | custom-call | flops 12000000000 | bytes 20000000 | tf_op jit(solution)/shard_map/attend_back/pallas_call | solution.py:409
  183.3 11.7 %weight_blocks.1 = (bf16[16,208,384]{2,1,0:T(8,128)(2,1)}, bf16[16,208,384]{2,1,0:T(8,128)(2,1)}) custom-call(s32[4]{0:T(128)} %pad_add_fusion.spot, bf16[1024,768]{1,0:T(8,128)(2,1)} %bitcast.157, bf16[1024,768]{1,0:T(8,128)(2,1)} %get-tuple-element.89.dq, bf16[1024,768]{1,0:T(8,128)(2,1)} %get-tuple-element.90.dk, bf16[1024,768]{1,0:T(8,128)(2,1)} %get-tuple-element.91.dv, ...), custom_call_target="tpu_custom_call" | custom-call | flops 4000000000 | bytes 10000000 | tf_op jit(solution)/shard_map/weight_blocks/pallas_call | solution.py:612
  195.2 4.8 %collective-permute-done.12 = bf16[16,208,384]{2,1,0:T(8,128)(2,1)S(1)} collective-permute-done((bf16[16,208,384]{2,1,0:T(8,128)(2,1)}, bf16[16,208,384]{2,1,0:T(8,128)(2,1)S(1)}, u32[]{:S(2)}, u32[]{:S(2)}) %collective-permute-start.12) | collective-permute-done | bytes 2555936 | tf_op jit(solution)/shard_map/ppermute | solution.py:44
  200.0 2.5 dynamic-slice_bitcast_fusion
  208.4 14.0 %collective-permute-done.13 = bf16[4,2,96,384]{3,2,1,0:T(8,128)(2,1)S(1)} collective-permute-done((bf16[4,2,96,384]{3,2,1,0:T(8,128)(2,1)S(1)}, bf16[4,2,96,384]{3,2,1,0:T(8,128)(2,1)S(1)}, u32[]{:S(2)}, u32[]{:S(2)}) %collective-permute-start.13) | collective-permute-done | bytes 589856 | tf_op jit(solution)/shard_map/ppermute | solution.py:44
  227.0 8.2 %collective-permute-done.15 = bf16[4,96,384]{2,1,0:T(8,128)(2,1)S(1)} collective-permute-done((bf16[4,96,384]{2,1,0:T(8,128)(2,1)S(1)}, bf16[4,96,384]{2,1,0:T(8,128)(2,1)S(1)}, u32[]{:S(2)}, u32[]{:S(2)}) %collective-permute-start.15) | collective-permute-done | bytes 294944 | tf_op jit(solution)/shard_map/ppermute | solution.py:44
  239.7 2.0 collective-permute-start.19
  241.7 3.3 %add_add_fusion = f32[1024,768]{1,0:T(8,128)} fusion(f32[1024,768]{1,0:T(8,128)S(1)} %fusion.2, f32[1024,768]{1,0:T(8,128)S(1)} %copy-done.1, f32[1024,768]{1,0:T(8,128)S(1)} %fusion.4, bf16[1024,768]{1,0:T(8,128)(2,1)S(1)} %copy-done.2, bf16[4,768,768]{2,1,0:T(8,128)(2,1)S(1)} %bitcast.149), kind=kOutput, calls=%fused_computation | convolution fusion | flops 1210318848 | bytes 15335424 | tf_op jit(solution)/shard_map/tb,ab->ta/dot_general | solution.py:628
  245.1 4.1 %collective-permute-done.17 = bf16[208,384]{1,0:T(8,128)(2,1)S(1)} collective-permute-done((bf16[208,384]{1,0:T(8,128)(2,1)S(1)}, bf16[208,384]{1,0:T(8,128)(2,1)S(1)}, u32[]{:S(2)}, u32[]{:S(2)}) %collective-permute-start.17) | collective-permute-done | bytes 159776 | tf_op jit(solution)/shard_map/ppermute | solution.py:44
  249.2 9.5 %collective-permute-done.18 = bf16[208,384]{1,0:T(8,128)(2,1)S(1)} collective-permute-done((bf16[208,384]{1,0:T(8,128)(2,1)S(1)}, bf16[208,384]{1,0:T(8,128)(2,1)S(1)}, u32[]{:S(2)}, u32[]{:S(2)}) %collective-permute-start.18) | collective-permute-done | bytes 159776 | tf_op jit(solution)/shard_map/ppermute | solution.py:44
  260.9 52.5 %reduce-scatter.2.cloned.1.call-done = bf16[24,6144]{1,0:T(8,128)(2,1)} async-done(((bf16[768,6144]{1,0:T(8,128)(2,1)}), bf16[24,6144]{1,0:T(8,128)(2,1)}) %reduce-scatter.2.cloned.1.call-update) | async-done | bytes 294928 | tf_op jit(solution)/shard_map/reduce_scatter | solution.py:695
  316.8 2.6 reshape.134
  (135 shorter events, 35.3 us)
Async XLA Ops:
  7.2 100.9 %all-gather.2.cloned.1.call-start = ((), (), s32[]{:S(2)}) async-start(), calls=%async_computation.1 | async-start | bytes 9732096 | tf_op jit(solution)/shard_map/all_gather | solution.py:662
  11.8 301.6 %reduce-scatter.2.cloned.1.call-start = ((), (), s32[]{:S(2)}) async-start(), calls=%async_computation.2 | async-start | bytes 9732096 | tf_op jit(solution)/shard_map/reduce_scatter | solution.py:695
  12.0 1.4 collective-permute-start
  13.5 10.0 %collective-permute-start.1 = (bf16[208,384]{1,0:T(8,128)(2,1)S(1)}, bf16[208,384]{1,0:T(8,128)(2,1)S(1)}, u32[]{:S(2)}, u32[]{:S(2)}) collective-permute-start(bf16[208,384]{1,0:T(8,128)(2,1)S(1)} %fusion.18), channel_id=1, source_target_pairs={{0,8},{1,9},{2,10},{3,11},{4,12},{5,13},{6,14},{7,15},{8,16},{9,17... | collective-permute-start | bytes 479240 | tf_op jit(solution)/shard_map/ppermute | solution.py:44
  16.5 16.3 %collective-permute-start.2 = (bf16[208,384]{1,0:T(8,128)(2,1)S(1)}, bf16[208,384]{1,0:T(8,128)(2,1)S(1)}, u32[]{:S(2)}, u32[]{:S(2)}) collective-permute-start(bf16[208,384]{1,0:T(8,128)(2,1)S(1)} %fusion.18), channel_id=1, source_target_pairs={{0,16},{1,17},{2,18},{3,19},{4,20},{5,21},{6,22},{7,23},{8,24},{9,... | collective-permute-start | bytes 479240 | tf_op jit(solution)/shard_map/ppermute | solution.py:44
  19.1 13.7 %collective-permute-start.3 = (bf16[208,384]{1,0:T(8,128)(2,1)S(1)}, bf16[208,384]{1,0:T(8,128)(2,1)S(1)}, u32[]{:S(2)}, u32[]{:S(2)}) collective-permute-start(bf16[208,384]{1,0:T(8,128)(2,1)S(1)} %fusion.18), channel_id=1, source_target_pairs={{0,24},{1,25},{2,26},{3,27},{4,28},{5,29},{6,30},{7,31},{8,0},{9,1... | collective-permute-start | bytes 479240 | tf_op jit(solution)/shard_map/ppermute | solution.py:44
  32.8 10.0 %collective-permute-start.5 = (bf16[4,112,384]{2,1,0:T(8,128)(2,1)S(1)}, bf16[4,112,384]{2,1,0:T(8,128)(2,1)S(1)}, u32[]{:S(2)}, u32[]{:S(2)}) collective-permute-start(bf16[4,112,384]{2,1,0:T(8,128)(2,1)S(1)} %pad_maximum_fusion.1), channel_id=1, source_target_pairs={{0,4},{1,5},{2,6},{3,7},{4,0},{5,1},{6,2},{7,3},{8,12},{9,13},{10,... | collective-permute-start | bytes 1032200 | tf_op jit(solution)/shard_map/ppermute | solution.py:44
  34.5 8.4 %collective-permute-start.4 = (bf16[4,96,384]{2,1,0:T(8,128)(2,1)S(1)}, bf16[4,96,384]{2,1,0:T(8,128)(2,1)S(1)}, u32[]{:S(2)}, u32[]{:S(2)}) collective-permute-start(bf16[4,96,384]{2,1,0:T(8,128)(2,1)S(1)} %pad_maximum_fusion.4), channel_id=1, source_target_pairs={{0,2},{1,3},{2,0},{3,1},{4,6},{5,7},{6,4},{7,5},{8,10},{9,11},{10,... | collective-permute-start | bytes 884744 | tf_op jit(solution)/shard_map/ppermute | solution.py:44
  43.0 27.8 %copy-start.3 = (bf16[8,112,384]{2,1,0:T(8,128)(2,1)}, bf16[8,112,384]{2,1,0:T(8,128)(2,1)S(1)}, u32[]{:S(2)}) copy-start(bf16[8,112,384]{2,1,0:T(8,128)(2,1)S(1)} %constant_dynamic-update-slice_fusion.2.refs_2_) | copy-start | bytes 2064388
  43.0 24.4 %collective-permute-start.7 = (bf16[8,112,384]{2,1,0:T(8,128)(2,1)S(1)}, bf16[8,112,384]{2,1,0:T(8,128)(2,1)S(1)}, u32[]{:S(2)}, u32[]{:S(2)}) collective-permute-start(bf16[8,112,384]{2,1,0:T(8,128)(2,1)S(1)} %constant_dynamic-update-slice_fusion.2.refs_2_), channel_id=1, source_target_pairs={{0,2},{1,3},{2,0},{3,1},{4,6},{5,7},{6,4},{7,5},{8,10},{9,11},{10,... | collective-permute-start | bytes 2064392 | tf_op jit(solution)/shard_map/ppermute | solution.py:44
  44.6 22.8 %collective-permute-start.9 = (bf16[8,112,384]{2,1,0:T(8,128)(2,1)S(1)}, bf16[8,112,384]{2,1,0:T(8,128)(2,1)S(1)}, u32[]{:S(2)}, u32[]{:S(2)}) collective-permute-start(bf16[8,112,384]{2,1,0:T(8,128)(2,1)S(1)} %constant_dynamic-update-slice_fusion.2.refs_2_), channel_id=1, source_target_pairs={{0,1},{1,0},{2,3},{3,2},{4,5},{5,4},{6,7},{7,6},{8,9},{9,8},{10,11... | collective-permute-start | bytes 2064392 | tf_op jit(solution)/shard_map/ppermute | solution.py:44
  44.7 19.6 %collective-permute-start.6 = (bf16[8,96,384]{2,1,0:T(8,128)(2,1)S(1)}, bf16[8,96,384]{2,1,0:T(8,128)(2,1)}, u32[]{:S(2)}, u32[]{:S(2)}) collective-permute-start(bf16[8,96,384]{2,1,0:T(8,128)(2,1)S(1)} %constant_dynamic-update-slice_fusion.refs_0_), channel_id=1, source_target_pairs={{0,4},{1,5},{2,6},{3,7},{4,0},{5,1},{6,2},{7,3},{8,12},{9,13},{10,... | collective-permute-start | bytes 1769480 | tf_op jit(solution)/shard_map/ppermute | solution.py:44
  46.0 18.3 %collective-permute-start.8 = (bf16[8,96,384]{2,1,0:T(8,128)(2,1)S(1)}, bf16[8,96,384]{2,1,0:T(8,128)(2,1)S(1)}, u32[]{:S(2)}, u32[]{:S(2)}) collective-permute-start(bf16[8,96,384]{2,1,0:T(8,128)(2,1)S(1)} %constant_dynamic-update-slice_fusion.refs_0_), channel_id=1, source_target_pairs={{0,1},{1,0},{2,3},{3,2},{4,5},{5,4},{6,7},{7,6},{8,9},{9,8},{10,11... | collective-permute-start | bytes 1769480 | tf_op jit(solution)/shard_map/ppermute | solution.py:44
  67.4 3.4 %collective-permute-start.11 = (bf16[8,112,384]{2,1,0:T(8,128)(2,1)S(1)}, bf16[8,112,384]{2,1,0:T(8,128)(2,1)S(1)}, u32[]{:S(2)}, u32[]{:S(2)}) collective-permute-start(bf16[8,112,384]{2,1,0:T(8,128)(2,1)S(1)} %collective-permute-done.7.refs_3_), channel_id=1, source_target_pairs={{0,1},{1,0},{2,3},{3,2},{4,5},{5,4},{6,7},{7,6},{8,9},{9,8},{10,11... | collective-permute-start | bytes 2064392 | tf_op jit(solution)/shard_map/ppermute | solution.py:44
  67.5 3.3 %collective-permute-start.10 = (bf16[8,96,384]{2,1,0:T(8,128)(2,1)}, bf16[8,96,384]{2,1,0:T(8,128)(2,1)}, u32[]{:S(2)}, u32[]{:S(2)}) collective-permute-start(bf16[8,96,384]{2,1,0:T(8,128)(2,1)} %collective-permute-done.6.refs_1_), channel_id=1, source_target_pairs={{0,1},{1,0},{2,3},{3,2},{4,5},{5,4},{6,7},{7,6},{8,9},{9,8},{10,11... | collective-permute-start | bytes 1769480 | tf_op jit(solution)/shard_map/ppermute | solution.py:44
  195.0 5.0 %collective-permute-start.12 = (bf16[16,208,384]{2,1,0:T(8,128)(2,1)}, bf16[16,208,384]{2,1,0:T(8,128)(2,1)S(1)}, u32[]{:S(2)}, u32[]{:S(2)}) collective-permute-start(bf16[16,208,384]{2,1,0:T(8,128)(2,1)} %get-tuple-element.94), channel_id=1, source_target_pairs={{0,1},{1,0},{2,3},{3,2},{4,5},{5,4},{6,7},{7,6},{8,9},{9,8},{10,11... | collective-permute-start | bytes 7667720 | tf_op jit(solution)/shard_map/ppermute | solution.py:44
  202.7 19.9 %collective-permute-start.14 = (bf16[4,2,112,384]{3,2,1,0:T(8,128)(2,1)S(1)}, bf16[4,2,112,384]{3,2,1,0:T(8,128)(2,1)S(1)}, u32[]{:S(2)}, u32[]{:S(2)}) collective-permute-start(bf16[4,2,112,384]{3,2,1,0:T(8,128)(2,1)S(1)} %add_convert_fusion.1), channel_id=1, source_target_pairs={{0,2},{1,3},{2,0},{3,1},{4,6},{5,7},{6,4},{7,5},{8,10},{9,11},{10,... | collective-permute-start | bytes 2064392 | tf_op jit(solution)/shard_map/ppermute | solution.py:44
  205.3 17.1 %collective-permute-start.13 = (bf16[4,2,96,384]{3,2,1,0:T(8,128)(2,1)S(1)}, bf16[4,2,96,384]{3,2,1,0:T(8,128)(2,1)S(1)}, u32[]{:S(2)}, u32[]{:S(2)}) collective-permute-start(bf16[4,2,96,384]{3,2,1,0:T(8,128)(2,1)S(1)} %add_convert_fusion.3), channel_id=1, source_target_pairs={{0,4},{1,5},{2,6},{3,7},{4,0},{5,1},{6,2},{7,3},{8,12},{9,13},{10,... | collective-permute-start | bytes 1769480 | tf_op jit(solution)/shard_map/ppermute | solution.py:44
  222.7 13.7 %collective-permute-start.16 = (bf16[4,112,384]{2,1,0:T(8,128)(2,1)S(1)}, bf16[4,112,384]{2,1,0:T(8,128)(2,1)S(1)}, u32[]{:S(2)}, u32[]{:S(2)}) collective-permute-start(bf16[4,112,384]{2,1,0:T(8,128)(2,1)S(1)} %fusion.11), channel_id=1, source_target_pairs={{0,4},{1,5},{2,6},{3,7},{4,0},{5,1},{6,2},{7,3},{8,12},{9,13},{10,... | collective-permute-start | bytes 1032200 | tf_op jit(solution)/shard_map/ppermute | solution.py:44
  224.3 10.9 %collective-permute-start.15 = (bf16[4,96,384]{2,1,0:T(8,128)(2,1)S(1)}, bf16[4,96,384]{2,1,0:T(8,128)(2,1)S(1)}, u32[]{:S(2)}, u32[]{:S(2)}) collective-permute-start(bf16[4,96,384]{2,1,0:T(8,128)(2,1)S(1)} %fusion.16), channel_id=1, source_target_pairs={{0,2},{1,3},{2,0},{3,1},{4,6},{5,7},{6,4},{7,5},{8,10},{9,11},{10,... | collective-permute-start | bytes 884744 | tf_op jit(solution)/shard_map/ppermute | solution.py:44
  236.7 12.4 %collective-permute-start.17 = (bf16[208,384]{1,0:T(8,128)(2,1)S(1)}, bf16[208,384]{1,0:T(8,128)(2,1)S(1)}, u32[]{:S(2)}, u32[]{:S(2)}) collective-permute-start(bf16[208,384]{1,0:T(8,128)(2,1)S(1)} %get-tuple-element.121), channel_id=1, source_target_pairs={{0,8},{1,9},{2,10},{3,11},{4,12},{5,13},{6,14},{7,15},{8,16},{9,17... | collective-permute-start | bytes 479240 | tf_op jit(solution)/shard_map/ppermute | solution.py:44
  238.2 20.4 %collective-permute-start.18 = (bf16[208,384]{1,0:T(8,128)(2,1)S(1)}, bf16[208,384]{1,0:T(8,128)(2,1)S(1)}, u32[]{:S(2)}, u32[]{:S(2)}) collective-permute-start(bf16[208,384]{1,0:T(8,128)(2,1)S(1)} %get-tuple-element.120), channel_id=1, source_target_pairs={{0,16},{1,17},{2,18},{3,19},{4,20},{5,21},{6,22},{7,23},{8,24},{9,... | collective-permute-start | bytes 479240 | tf_op jit(solution)/shard_map/ppermute | solution.py:44
  239.7 19.0 %collective-permute-start.19 = (bf16[208,384]{1,0:T(8,128)(2,1)S(1)}, bf16[208,384]{1,0:T(8,128)(2,1)S(1)}, u32[]{:S(2)}, u32[]{:S(2)}) collective-permute-start(bf16[208,384]{1,0:T(8,128)(2,1)S(1)} %get-tuple-element.119), channel_id=1, source_target_pairs={{0,24},{1,25},{2,26},{3,27},{4,28},{5,29},{6,30},{7,31},{8,0},{9,1... | collective-permute-start | bytes 479240 | tf_op jit(solution)/shard_map/ppermute | solution.py:44
  258.8 1.3 collective-permute-start.20
  (26 other events, 118.9 us)
Sparse Core Ops, SparseCore 0:
  12.0 96.0 all-gather.1
  164.6 148.7 reduce-scatter.1

commit v3 on v2

--- a/solution.py
+++ b/solution.py
@@ -5,6 +5,7 @@
 from jax import lax
 from jax.experimental import pallas as pl
 from jax.experimental.pallas import tpu as pltpu
+from jax.sharding import Mesh
 from jax.sharding import PartitionSpec as P
 
 EPSILON = 1e-06
@@ -16,6 +17,7 @@
 MEGA = 1024 * 1024
 
 AXES = ("dp", "shard")
+CHIPS = ("z", "y", "x", "core")
 f32 = jnp.float32
 bf16 = jnp.bfloat16
 cat = jnp.concatenate
@@ -41,12 +43,11 @@
 
 
 def send(values, move):
-    return lax.ppermute(values, AXES, MOVES[move])
+    return lax.ppermute(values, CHIPS, MOVES[move])
 
 
 def place():
-    major, minor = lax.axis_index("dp"), lax.axis_index("shard")
-    return major // 2, major % 2, minor // 2, minor % 2
+    return tuple(lax.axis_index(axis) for axis in CHIPS)
 
 
 def phase(*values):
@@ -77,39 +78,19 @@
     return first, first_y, second, second_x, other_first, other_first_y, other_second, other_second_x
 
 
-def scatter_blocks(keep, away, split):
+def pick(values, index, axis):
+    return lax.dynamic_index_in_dim(values, index, axis, False)
+
+
+def send_line(parts):
+    return tuple(send(part, move) for part, move in zip(parts, ("z1", "z2", "z3")))
+
+
+def halves_of(mine):
     z, y, x, core = place()
-    got, keep = phase(send(away, "core"), keep)
-    shape = (4, 2, 2, *keep.shape[1:])
-    keep, got = keep.reshape(shape), got.reshape(shape)
-
-    def pick(values, index, axis):
-        return lax.dynamic_index_in_dim(values, index, axis, False)
-
-    def part(index, axis, rows):
-        return add(pick(keep, index, axis)[:, :, rows], pick(got, index, axis)[:, :, rows]).astype(bf16)
-
-    top, rest = slice(0, split), slice(split, None)
-    got_first = send(part(1 - y, 1, top), "y")
-    got_second = send(part(1 - x, 2, rest), "x")
-    first, second = part(y, 1, top), part(x, 2, rest)
-    got_first, got_second, first, second = phase(got_first, got_second, first, second)
-
-    def both(one, two, index):
-        return add(pick(one, index, 1), pick(two, index, 1)).astype(bf16)
-
-    got_first_x = send(both(first, got_first, 1 - x), "x")
-    got_second_y = send(both(second, got_second, 1 - y), "y")
-    first, second = both(first, got_first, x), both(second, got_second, y)
-    got_first_x, got_second_y, first, second = phase(got_first_x, got_second_y, first, second)
-    line = cat([add(first, got_first_x), add(second, got_second_y)], 1)
-    low = line.astype(bf16)
-    one = send(pick(low, (z + 1) % 4, 0), "z1")
-    two = send(pick(low, (z + 2) % 4, 0), "z2")
-    three = send(pick(low, (z + 3) % 4, 0), "z3")
-    mine = pick(line, z, 0)
-    one, two, three, mine = phase(one, two, three, mine)
-    return add(mine, one, two, three)
+    kept = pick(mine, core, 1)
+    got = send(pick(mine, 1 - core, 1).astype(bf16), "core").astype(f32)
+    return jnp.where(core == 0, cat([kept, got], 2), cat([got, kept], 2))
 
 
 def gather_attention(matrices, vector):
@@ -123,18 +104,6 @@
     block = cat([pair.reshape(count * 2 * rows, half), vector_rows])
     (block,) = phase(block)
     return gather_blocks(block, count * rows)
-
-
-def scatter_attention(keep, away, count, rows, entries):
-    z, y, x, core = place()
-    half = keep.shape[2]
-    line = scatter_blocks(keep, away, count * rows)
-    size = count * 2 * rows
-    mine = line[:size].reshape(count, 2, rows, half)
-    kept = lax.dynamic_index_in_dim(mine, core, 1, False)
-    got = send(lax.dynamic_index_in_dim(mine, 1 - core, 1, False).astype(bf16), "core").astype(f32)
-    whole = jnp.where(core == 0, cat([kept, got], 2), cat([got, kept], 2))
-    return whole, line[size, :entries]
 
 
 def gather_attention_any(matrices, vector):
@@ -339,28 +308,38 @@
     )(lengths, spot, x, *gathered)
 
 
-def back_kernel(block, lengths, q_in, k_in, v_in, mixed, lse, grad, dq_out, dk_out, dv_out, marks):
-    row = pl.program_id(0)
-    length, width = q_in.shape
-    make_marks(lengths, row, marks)
-    keep = (lanes(0), lanes(1))
+def natural_rows(bias_rows, first_sums, second_sums):
+    rows = bias_rows + [second_sums[2:3, :], second_sums[0:1, :], second_sums[1:2, :]]
+    rows += [first_sums[i : i + 1, :] for i in (0, 1, 2)]
+    return rows + [first_sums[i : i + 1, :] for i in (3, 4, 5, 6)]
+
+
+def back_kernel(known, block, share, lengths, spot, x, q_in, k_in, v_in, mixed, lse, grad, *refs):
+    grad_out, first_sums, second_sums, dq_out, dk_out, dv_out, keep, away, marks = refs
+    tokens, width = q_in.shape
+    rows = lengths.shape[0]
+    length = tokens // rows
+    for row in range(rows):
+        make_marks(lengths, row, marks.at[row])
+    keep_lanes = (lanes(0), lanes(1))
     keep_scaled = (lanes(0, 0.125), lanes(1, 0.125))
     head_of = lax.broadcasted_iota(jnp.int32, (16, 128), 1) // HALF
     picker = jnp.where(lax.broadcasted_iota(jnp.int32, (16, 128), 0) == head_of, 1.0, 0.0).astype(bf16)
-    pairs, parts = width // 128, spans(length, block)
-
-    def products_of(pair):
-        tile = pl.ds(pair * 128, 128)
-        q, k, v, g = q_in[:, tile], k_in[:, tile], v_in[:, tile], grad[:, tile]
-        product = g.astype(f32) * mixed[:, tile].astype(f32)
+    parts = spans(length, block)
+    items = [(row, pair) for row in range(rows) for pair in range(width // 128)]
+
+    def products_of(row, pair):
+        tile = (slice(row * length, row * length + length), slice(pair * 128, pair * 128 + 128))
+        q, k, v, g = q_in[tile], k_in[tile], v_in[tile], grad[tile]
+        product = g.astype(f32) * mixed[tile].astype(f32)
         high = product.astype(bf16)
         centre = dot_nt(picker, high) + dot_nt(picker, (product - high.astype(f32)).astype(bf16))
         qz = [q * keep_scaled[h] for h in (0, 1)]
-        kz = [k * keep[h] for h in (0, 1)]
-        vz = [v * keep[h] for h in (0, 1)]
-        gz = [g * keep[h] for h in (0, 1)]
-        qs = [qz[h] + marks[h] for h in (0, 1)]
-        ks = [kz[h] + marks[2 + h] for h in (0, 1)]
+        kz = [k * keep_lanes[h] for h in (0, 1)]
+        vz = [v * keep_lanes[h] for h in (0, 1)]
+        gz = [g * keep_lanes[h] for h in (0, 1)]
+        qs = [qz[h] + marks[row, h] for h in (0, 1)]
+        ks = [kz[h] + marks[row, 2 + h] for h in (0, 1)]
         scores = [
             [dot_nt(ks[h][start : start + block], qs[h][first:last]) for h in (0, 1)] for start, first, last in parts
         ]
@@ -369,14 +348,15 @@
         ]
         return scores, slopes, centre, qz, kz, gz
 
-    upcoming = products_of(0)
-    for pair in range(pairs):
+    upcoming = products_of(*items[0])
+    for index, (row, pair) in enumerate(items):
         scores, slopes, centre, qz, kz, gz = upcoming
-        if pair + 1 < pairs:
-            upcoming = products_of(pair + 1)
+        if index + 1 < len(items):
+            upcoming = products_of(*items[index + 1])
         probs, grads = [], []
         for i, (start, first, last) in enumerate(parts):
-            prob = [jnp.exp(scores[i][h] - lse[0, 2 * pair + h : 2 * pair + h + 1, first:last]) for h in (0, 1)]
+            head = 2 * pair
+            prob = [jnp.exp(scores[i][h] - lse[row, head + h : head + h + 1, first:last]) for h in (0, 1)]
             probs.append([p.astype(bf16) for p in prob])
             grads.append([(prob[h] * (slopes[i][h] - centre[h : h + 1, first:last])).astype(bf16) for h in (0, 1)])
         columns = slice(pair * 128, pair * 128 + 128)
@@ -390,50 +370,86 @@
             sum(dot_tn(grads[i][h], kz[h][start : start + block]) for h in (0, 1))
             for i, (start, first, last) in enumerate(parts)
         ]
+        base = row * length
         for i, (start, first, last) in enumerate(parts):
-            dv_out[start : start + block, columns] = to_values[i].astype(bf16)
-            dk_out[start : start + block, columns] = to_keys[i].astype(bf16)
+            dv_out[base + start : base + start + block, columns] = to_values[i].astype(bf16)
+            dk_out[base + start : base + start + block, columns] = to_keys[i].astype(bf16)
         for at in range(0, length, MOST):
             pieces = [
                 to_queries[i][at - first : at - first + MOST]
                 for i, (start, first, last) in enumerate(parts)
                 if first <= at < last
             ]
-            dq_out[at : at + MOST, columns] = (sum(pieces) * 0.125).astype(bf16)
-
-
-def attend_back(q, k, v, mixed, lse, grad, lengths, rows, block=128):
+            dq_out[base + at : base + at + MOST, columns] = (sum(pieces) * 0.125).astype(bf16)
+    biases = [jnp.sum(out[...].astype(f32), axis=0, keepdims=True) for out in (dq_out, dv_out)]
+    if not known:
+        for unit, out in enumerate((dq_out, dk_out, dv_out)):
+            keep[unit] = dot_tn(x[...], out[...]).astype(bf16)
+        away[...] = jnp.zeros_like(away)
+        away[0:1, :] = biases[0]
+        away[1:2, :] = biases[1]
+        return
+    core = spot[3]
+    half, chips, size = width // 2, keep.shape[0], 2 * share
+    natural = natural_rows(biases, first_sums, second_sums)
+    owner = lax.broadcasted_iota(jnp.int32, (chips, width), 1) // share
+    chip = lax.broadcasted_iota(jnp.int32, (chips, width), 0)
+    lane = lax.broadcasted_iota(jnp.int32, (chips, half), 1)
+    table = spread(half, width, share)
+    top = lax.broadcasted_iota(jnp.int32, (chips, 16, half), 1) == 0
+    for side, out in ((1 - core, away), (core, keep)):
+        own = pl.ds(pl.multiple_of(side * half, 128), half)
+        for unit, out_ref in enumerate((dq_out, dk_out, dv_out)):
+            part = dot_tn(x[...], out_ref[:, own]).astype(bf16)
+            out[:, unit * size : (unit + 1) * size, :] = part.reshape(chips, size, half)
+        out[:, 3 * size : 4 * size, :] = grad_out[:, own].reshape(chips, size, half)
+        mine = owner == 2 * chip + side
+        entries = jnp.zeros((chips, half), f32)
+        spreads = dot_nt(cat([jnp.where(mine, row, 0.0) for row in natural]).astype(bf16), table)
+        for group in range(len(natural)):
+            part = spreads[group * chips : (group + 1) * chips]
+            entries = entries + jnp.where(lane // share == group, part, 0.0)
+        out[:, 4 * size :, :] = jnp.where(top, entries[:, None, :], 0.0).astype(bf16)
+
+
+def full_block(value):
+    return pl.BlockSpec(value.shape, lambda i, *_: (0,) * len(value.shape))
+
+
+def attend_back(known, share, spot, x, q, k, v, mixed, lse, grad, grad_out, first_sums, second_sums, lengths, block=128):
     tokens, width = q.shape
-    length = tokens // rows
-    tile = pl.BlockSpec((length, width), lambda r, *_: (r, 0))
+    rows = lengths.shape[0]
+    shape = jax.ShapeDtypeStruct
+    outs = [shape((tokens, width), bf16)] * 3
+    if known:
+        outs += [shape((16, 8 * share + 16, width // 2), bf16)] * 2
+    else:
+        outs += [shape((3, width, width), bf16), shape((8, width), f32)]
+    inputs = (x, q, k, v, mixed, lse, grad, grad_out, first_sums, second_sums)
     return pl.pallas_call(
-        functools.partial(back_kernel, block),
+        functools.partial(back_kernel, known, block, share),
         grid_spec=pltpu.PrefetchScalarGridSpec(
-            num_scalar_prefetch=1,
-            grid=(rows,),
-            in_specs=[tile] * 4 + [pl.BlockSpec((1, 16, length), lambda r, *_: (r, 0, 0)), tile],
-            out_specs=[tile] * 3,
-            scratch_shapes=[pltpu.VMEM((4, length, 128), bf16)],
+            num_scalar_prefetch=2,
+            grid=(1,),
+            in_specs=[full_block(value) for value in inputs],
+            out_specs=[full_block(out) for out in outs],
+            scratch_shapes=[pltpu.VMEM((rows, 4, tokens // rows, 128), bf16)],
         ),
-        out_shape=[jax.ShapeDtypeStruct((tokens, width), bf16)] * 3,
+        out_shape=outs,
         compiler_params=pltpu.CompilerParams(vmem_limit_bytes=60 * MEGA),
-        cost_estimate=pl.CostEstimate(flops=12 * 10**9, bytes_accessed=2 * 10**7, transcendentals=4 * 10**6),
+        cost_estimate=pl.CostEstimate(flops=20 * 10**9, bytes_accessed=2 * 10**7, transcendentals=4 * 10**6),
         name="attend_back",
-    )(lengths, q, k, v, mixed, lse, grad)
+    )(lengths, spot, *inputs)
 
 
 def gelu_parts(u):
-    bell = jnp.exp(u * u * -0.5)
-    t = 1.0 / (1.0 + (0.3275911 * SQRT_HALF) * jnp.abs(u))
-    poly = t * (0.127414796 + t * (-0.142248368 + t * (0.7107068705 + t * (-0.7265760135 + t * 0.5307027145))))
-    tail = poly * bell
-    phi = jnp.where(u >= 0.0, 1.0 - tail, tail)
-    return u * phi, phi + u * (bell * INV_ROOT)
+    phi = 0.5 * (1.0 + lax.erf(u * SQRT_HALF))
+    return u * phi, phi + u * (jnp.exp(u * u * -0.5) * INV_ROOT)
 
 
 def ffn_kernel(
-    chunks, size, weights, normed, inverse, cot, mixed, out_mat, vec, layer_out, grads, first, grad_mixed, grad_out, sums,
-    w, low, act, slope, total, second_low, back, ready, loaded, sent,
+    chunks, size, spot, weights, normed, cot, vec, layer_out, keep, away, total, sums,
+    w, low, act, slope, second_low, back, ready, loaded, sent,
 ):
     tokens, width = normed.shape
     copies = []
@@ -452,19 +468,23 @@
 
     low[...] = (normed[...] * gain + shift).astype(bf16)
     sums[...] = jnp.zeros_like(sums)
-    for copy in copies:
-        copy.wait()
-
-    def forward(t, _):
-        rows = pl.ds(pl.multiple_of(t * size, size), size)
+
+    def forward(t, first=False):
+        rows = pl.ds(t * size, size) if first else pl.ds(pl.multiple_of(t * size, size), size)
         inputs = low[rows, :]
+        if first:
+            copies[0].wait()
         pre, added = dot(inputs, up(0)), None
         for g in range(chunks):
+            if first and g + 1 < chunks:
+                copies[g + 1].wait()
             upcoming = dot(inputs, up(g + 1)) if g + 1 < chunks else None
             activated, derivative = gelu_parts(pre + vec[8 + g : 9 + g, :])
             activated = activated.astype(bf16)
             act[g, rows, :] = activated
             slope[g, rows, :] = derivative.astype(bf16)
+            if first:
+                copies[chunks + g].wait()
             part = dot(activated, down(g))
             added = part if added is None else added + part
             pre = upcoming
@@ -481,15 +501,19 @@
         sums[0:1, :] += jnp.sum(second, axis=0, keepdims=True)
         sums[1:2, :] += jnp.sum(grad * hat, axis=0, keepdims=True)
         sums[2:3, :] += jnp.sum(grad, axis=0, keepdims=True)
-        return 0
-
-    lax.fori_loop(0, tokens // size, forward, 0)
+
+    forward(0, True)
+
+    @pl.loop(1, tokens // size)
+    def _(t):
+        forward(t)
+
     pending = []
     for g in range(chunks):
         to_act = dot_nt(second_low[...], down(g))
         to_down = dot_tn(act[g], second_low[...])
         to_pre = to_act * slope[g].astype(f32)
-        sums[6 + g : 7 + g, :] = jnp.sum(to_pre, axis=0, keepdims=True)
+        sums[3 + g : 4 + g, :] = jnp.sum(to_pre, axis=0, keepdims=True)
         back[...] = to_pre.astype(bf16)
         slot = g % 2
         if g >= 2:
@@ -498,67 +522,35 @@
         ready[slot, 1] = to_down.astype(bf16)
         total[...] += dot_nt(back[...], up(g))
         ready[slot, 0] = dot_tn(low[...], back[...]).astype(bf16)
-        out = [
-            pltpu.make_async_copy(
-                ready.at[slot, j], grads.at[:, pl.ds((j * chunks + g) * width, width)], sent.at[slot, j]
-            )
-            for j in (0, 1)
-        ]
+        half, core = width // 2, spot[3]
+        out = []
+        for j in (0, 1):
+            for target, side in ((away, 1 - core), (keep, core)):
+                source = ready.at[slot, j, :, pl.ds(pl.multiple_of(side * half, 128), half)]
+                place_of = target.at[:, pl.ds((j * chunks + g) * half, half)]
+                out.append(pltpu.make_async_copy(source, place_of, sent.at[slot, len(out)]))
         for copy in out:
             copy.start()
         pending.append(out)
 
-    def backward(t, _):
-        rows = pl.ds(pl.multiple_of(t * size, size), size)
-        middle, hat, inv = total[rows, :], normed[rows, :], inverse[rows, 0:1]
-        scaled = middle * gain
-        to_first = inv * (scaled - mean(scaled) - hat * mean(scaled * hat))
-        first[rows, :] = to_first
-        to_low = to_first.astype(bf16)
-        second_low[rows, :] = to_low
-        sums[3:4, :] += jnp.sum(middle * hat, axis=0, keepdims=True)
-        sums[4:5, :] += jnp.sum(middle, axis=0, keepdims=True)
-        sums[5:6, :] += jnp.sum(to_first, axis=0, keepdims=True)
-        grad_mixed[rows, :] = dot_nt(to_low, out_mat[0]).astype(bf16)
-        return 0
-
-    lax.fori_loop(0, tokens // size, backward, 0)
-    grad_out[...] = dot_tn(mixed[...], second_low[...]).astype(bf16)
     for out in pending[-2:]:
         for copy in out:
             copy.wait()
 
 
-def ffn(weights, normed, inverse, cot, mixed, mats, vec, size=256):
+def ffn(weights, normed, cot, vec, spot, size=256):
     tokens, width = normed.shape
     chunks = weights.shape[1] // (2 * width)
     shape = jax.ShapeDtypeStruct
-
-    def full(value):
-        return pl.BlockSpec(value.shape, lambda i: (0,) * len(value.shape))
-
-    outs = [
-        shape((tokens, width), bf16),
-        shape(weights.shape, bf16),
-        shape((tokens, width), f32),
-        shape((tokens, width), bf16),
-        shape((width, width), bf16),
-        shape((16, width), f32),
-    ]
-    out_specs = [full(out) for out in outs]
-    out_specs[1] = pl.BlockSpec(memory_space=pl.ANY)
+    anywhere = pl.BlockSpec(memory_space=pl.ANY)
+    halves = shape((width, chunks * width), bf16)
+    outs = [shape((tokens, width), bf16)] + [halves] * 2 + [shape((tokens, width), f32), shape((8, width), f32)]
+    out_specs = [full_block(out) for out in outs]
+    out_specs[1:3] = [anywhere] * 2
     return pl.pallas_call(
         functools.partial(ffn_kernel, chunks, size),
         grid=(1,),
-        in_specs=[
-            pl.BlockSpec(memory_space=pl.ANY),
-            full(normed),
-            full(inverse),
-            full(cot),
-            full(mixed),
-            pl.BlockSpec((1, width, width), lambda i: (3, 0, 0)),
-            full(vec),
-        ],
+        in_specs=[pl.BlockSpec(memory_space=pltpu.SMEM), anywhere, full_block(normed), full_block(cot), full_block(vec)],
         out_specs=out_specs,
         out_shape=outs,
         scratch_shapes=[
@@ -566,66 +558,207 @@
             pltpu.VMEM((tokens, width), bf16),
             pltpu.VMEM((chunks, tokens, width), bf16),
             pltpu.VMEM((chunks, tokens, width), bf16),
-            pltpu.VMEM((tokens, width), f32),
             pltpu.VMEM((tokens, width), bf16),
             pltpu.VMEM((tokens, width), bf16),
             pltpu.VMEM((2, 2, width, width), bf16),
             pltpu.SemaphoreType.DMA((2 * chunks,)),
-            pltpu.SemaphoreType.DMA((2, 2)),
+            pltpu.SemaphoreType.DMA((2, 4)),
         ],
         compiler_params=pltpu.CompilerParams(vmem_limit_bytes=63 * MEGA),
         cost_estimate=pl.CostEstimate(flops=32 * 10**9, bytes_accessed=3 * 10**7, transcendentals=6 * 10**6),
         name="ffn",
-    )(weights, normed, inverse, cot, mixed, mats, vec)
-
-
-def weight_kernel(share, spot, x, dq, dk, dv, grad_out, sums, keep, away):
-    core = spot[3]
-    tokens, width = x.shape
-    half, chips, rows = width // 2, keep.shape[0], 2 * share
-    natural = [jnp.sum(dq[...].astype(f32), axis=0, keepdims=True), jnp.sum(dv[...].astype(f32), axis=0, keepdims=True)]
-    natural += [sums[i : i + 1, :] for i in (5, 3, 4, 0, 1, 2, 6, 7, 8, 9)]
-    owner = lax.broadcasted_iota(jnp.int32, (chips, width), 1) // share
-    chip = lax.broadcasted_iota(jnp.int32, (chips, width), 0)
-    lane = lax.broadcasted_iota(jnp.int32, (chips, half), 1)
-    table = spread(half, width, share)
-    top = lax.broadcasted_iota(jnp.int32, (chips, 16, half), 1) == 0
-    for side, out in ((1 - core, away), (core, keep)):
-        columns = pl.ds(pl.multiple_of(side * half, 128), half)
-        for unit, grad in enumerate((dq, dk, dv)):
-            block = dot_tn(x[...], grad[:, columns]).astype(bf16)
-            out[:, unit * rows : (unit + 1) * rows, :] = block.reshape(chips, rows, half)
-        out[:, 3 * rows : 4 * rows, :] = grad_out[:, columns].reshape(chips, rows, half)
-        mine = owner == 2 * chip + side
-        entries = jnp.zeros((chips, half), f32)
-        spreads = dot_nt(cat([jnp.where(mine, row, 0.0) for row in natural]).astype(bf16), table)
-        for group in range(len(natural)):
-            part = spreads[group * chips : (group + 1) * chips]
-            entries = entries + jnp.where(lane // share == group, part, 0.0)
-        out[:, 4 * rows :, :] = jnp.where(top, entries[:, None, :], 0.0).astype(bf16)
-
-
-def weight_blocks(x, dq, dk, dv, grad_out, sums, spot, share):
-    width = x.shape[1]
-    blocks = jax.ShapeDtypeStruct((16, 8 * share + 16, width // 2), bf16)
+    )(spot, weights, normed, cot, vec)
+
+
+def middle_kernel(grad_middle, normed, inverse, mixed, out_mat, vec, first, grad_mixed, grad_out, sums, low):
+    step = pl.program_id(0)
+    size = normed.shape[0]
+    middle, hat, inv = grad_middle[...], normed[...], inverse[:, 0:1]
+    scaled = middle * vec[3:4, :]
+    to_first = inv * (scaled - mean(scaled) - hat * mean(scaled * hat))
+    first[...] = to_first
+    to_low = to_first.astype(bf16)
+    low[pl.ds(pl.multiple_of(step * size, size), size), :] = to_low
+    grad_mixed[...] = dot_nt(to_low, out_mat[0]).astype(bf16)
+
+    @pl.when(step == 0)
+    def _():
+        sums[...] = jnp.zeros_like(sums)
+
+    sums[0:1, :] += jnp.sum(middle * hat, axis=0, keepdims=True)
+    sums[1:2, :] += jnp.sum(middle, axis=0, keepdims=True)
+    sums[2:3, :] += jnp.sum(to_first, axis=0, keepdims=True)
+
+    @pl.when(step == pl.num_programs(0) - 1)
+    def _():
+        grad_out[...] = dot_tn(mixed[...], low[...]).astype(bf16)
+
+
+def middle_back(grad_middle, normed, inverse, mixed, mats, vec, size=256):
+    tokens, width = normed.shape
+    shape = jax.ShapeDtypeStruct
+    tile = pl.BlockSpec((size, width), lambda i: (i, 0))
+    outs = [shape((tokens, width), f32), shape((tokens, width), bf16), shape((width, width), bf16), shape((8, width), f32)]
+    return pl.pallas_call(
+        middle_kernel,
+        grid=(tokens // size,),
+        in_specs=[
+            tile,
+            tile,
+            pl.BlockSpec((size, 128), lambda i: (i, 0)),
+            full_block(mixed),
+            pl.BlockSpec((1, width, width), lambda i: (3, 0, 0)),
+            full_block(vec),
+        ],
+        out_specs=[tile, tile, full_block(outs[2]), full_block(outs[3])],
+        out_shape=outs,
+        scratch_shapes=[pltpu.VMEM((tokens, width), bf16)],
+        compiler_params=pltpu.CompilerParams(vmem_limit_bytes=60 * MEGA),
+        cost_estimate=pl.CostEstimate(flops=5 * 10**9, bytes_accessed=10**7, transcendentals=0),
+        name="middle_back",
+    )(grad_middle, normed, inverse, mixed, mats, vec)
+
+
+def core_kernel(views, spot, keep, got, away_first, kept_first, away_second, kept_second):
+    _, y, x, _ = (spot[i] for i in range(4))
+    first, second = views
+    for i in (0, 1):
+        for out, index in ((away_first, 1 - y), (kept_first, y)):
+            out[0, i] = first(keep, index, i) + first(got, index, i)
+        for out, index in ((away_second, 1 - x), (kept_second, x)):
+            out[0, i] = second(keep, i, index) + second(got, i, index)
+
+
+def core_stage(keep, got, spot, split, by_rows):
+    rows, columns = keep.shape[-2:]
+    cuts = (slice(0, split), slice(split, None))
+    if by_rows:
+        sizes, cuts = ((split, columns), (rows - split, columns)), tuple((cut, slice(None)) for cut in cuts)
+    else:
+        sizes, cuts = ((rows, split), (rows, columns - split)), tuple((slice(None), cut) for cut in cuts)
+    views = (
+        lambda ref, y, x: ref[(0, pl.ds(y, 1), x, *cuts[0])][0],
+        lambda ref, y, x: ref[(0, y, pl.ds(x, 1), *cuts[1])][0],
+    )
+    block = pl.BlockSpec((1, *keep.shape[1:]), lambda i, *_: (i, 0, 0, 0, 0))
+    outs = [jax.ShapeDtypeStruct((4, 2, *size), bf16) for size in (sizes[0], sizes[0], sizes[1], sizes[1])]
+    return pl.pallas_call(
+        functools.partial(core_kernel, views),
+        grid_spec=pltpu.PrefetchScalarGridSpec(
+            num_scalar_prefetch=1,
+            grid=(4,),
+            in_specs=[block] * 2,
+            out_specs=[pl.BlockSpec((1, *out.shape[1:]), lambda i, *_: (i, 0, 0, 0)) for out in outs],
+        ),
+        out_shape=outs,
+        compiler_params=pltpu.CompilerParams(vmem_limit_bytes=40 * MEGA),
+        cost_estimate=pl.CostEstimate(flops=10**6, bytes_accessed=10**7, transcendentals=0),
+        name="core_stage",
+    )(spot, keep, got)
+
+
+def plane_kernel(spot, mine_first, got_first, mine_second, got_second, *outs):
+    _, y, x, _ = (spot[i] for i in range(4))
+    away_first, kept_first, away_second, kept_second = outs
+    pairs = ((away_first, mine_first, got_first, 1 - x), (kept_first, mine_first, got_first, x))
+    pairs += ((away_second, mine_second, got_second, 1 - y), (kept_second, mine_second, got_second, y))
+    for out, mine, got, index in pairs:
+        out[...] = mine[0, pl.ds(index, 1)] + got[0, pl.ds(index, 1)]
+
+
+def plane_stage(kept, got, spot):
+    inputs = (kept[0], got[0], kept[1], got[1])
+    outs = [jax.ShapeDtypeStruct((4, *value.shape[2:]), bf16) for value in inputs]
+    away_first, kept_first, away_second, kept_second = pl.pallas_call(
+        plane_kernel,
+        grid_spec=pltpu.PrefetchScalarGridSpec(
+            num_scalar_prefetch=1,
+            grid=(4,),
+            in_specs=[pl.BlockSpec((1, *value.shape[1:]), lambda i, *_: (i, 0, 0, 0)) for value in inputs],
+            out_specs=[pl.BlockSpec((1, *out.shape[1:]), lambda i, *_: (i, 0, 0)) for out in outs],
+        ),
+        out_shape=outs,
+        compiler_params=pltpu.CompilerParams(vmem_limit_bytes=40 * MEGA),
+        cost_estimate=pl.CostEstimate(flops=10**6, bytes_accessed=5 * 10**6, transcendentals=0),
+        name="plane_stage",
+    )(spot, *inputs)
+    return (away_first, away_second), (kept_first, kept_second)
+
+
+def line_kernel(spot, mine_first, got_first, mine_second, got_second, one, two, three, stays):
+    z = spot[0]
+    rows = mine_first.shape[1]
+    for step, out in enumerate((stays, one, two, three)):
+        index = lax.rem(z + step, 4)
+        at = (pl.ds(index, 1),)
+        for mine, got, part in ((mine_first, got_first, slice(0, rows)), (mine_second, got_second, slice(rows, None))):
+            total = mine[at][0].astype(f32) + got[at][0].astype(f32)
+            out[part, :] = total.astype(out.dtype)
+
+
+def line_stage(kept, got, spot):
+    inputs = (kept[0], got[0], kept[1], got[1])
+    size = (kept[0].shape[1] + kept[1].shape[1], kept[0].shape[2])
+    outs = [jax.ShapeDtypeStruct(size, bf16)] * 3 + [jax.ShapeDtypeStruct(size, f32)]
+    vmem = pl.BlockSpec(memory_space=pltpu.VMEM)
+    *parts, stays = pl.pallas_call(
+        line_kernel,
+        in_specs=[pl.BlockSpec(memory_space=pltpu.SMEM)] + [vmem] * 4,
+        out_specs=[vmem] * 4,
+        out_shape=outs,
+        compiler_params=pltpu.CompilerParams(vmem_limit_bytes=40 * MEGA),
+        cost_estimate=pl.CostEstimate(flops=10**6, bytes_accessed=3 * 10**6, transcendentals=0),
+        name="line_stage",
+    )(spot, *inputs)
+    return parts, stays
+
+
+def sum_kernel(mine_first, got_first, mine_second, got_second, out):
+    columns = mine_first.shape[-1]
+    out[:, :, :columns] = mine_first[...] + got_first[...]
+    out[:, :, columns:] = mine_second[...] + got_second[...]
+
+
+def line_sum(kept, got):
+    line, rows, columns = kept[0].shape
     vmem = pl.BlockSpec(memory_space=pltpu.VMEM)
     return pl.pallas_call(
-        functools.partial(weight_kernel, share),
-        in_specs=[pl.BlockSpec(memory_space=pltpu.SMEM)] + [vmem] * 6,
-        out_specs=[vmem] * 2,
-        out_shape=[blocks] * 2,
+        sum_kernel,
+        in_specs=[vmem] * 4,
+        out_specs=vmem,
+        out_shape=jax.ShapeDtypeStruct((line, rows, 2 * columns), bf16),
+        compiler_params=pltpu.CompilerParams(vmem_limit_bytes=40 * MEGA),
+        cost_estimate=pl.CostEstimate(flops=10**6, bytes_accessed=5 * 10**6, transcendentals=0),
+        name="line_sum",
+    )(kept[0], got[0], kept[1], got[1])
+
+
+def token_kernel(first, dq, dk, dv, w, out):
+    total = first[...]
+    for unit, grad in enumerate((dq, dk, dv)):
+        total = total + dot_nt(grad[...], w[unit])
+    out[...] = total
+
+
+def token_grad(first, grads, mats, size=256):
+    tokens, width = first.shape
+    tile = pl.BlockSpec((size, width), lambda i: (i, 0))
+    return pl.pallas_call(
+        token_kernel,
+        grid=(tokens // size,),
+        in_specs=[tile] * 4 + [pl.BlockSpec((3, width, width), lambda i: (0, 0, 0))],
+        out_specs=tile,
+        out_shape=jax.ShapeDtypeStruct((tokens, width), f32),
         compiler_params=pltpu.CompilerParams(vmem_limit_bytes=60 * MEGA),
         cost_estimate=pl.CostEstimate(flops=4 * 10**9, bytes_accessed=10**7, transcendentals=0),
-        name="weight_blocks",
-    )(spot, x, dq, dk, dv, grad_out, sums)
-
-
-def outer_sum(left, right):
-    return jnp.einsum("ta,tb->ab", left, right, preferred_element_type=jnp.float32)
-
-
-def back_product(grads, weights):
-    return jnp.einsum("tb,ab->ta", grads, weights, preferred_element_type=jnp.float32)
+        name="token_grad",
+    )(first, *grads, mats)
+
+
+def natural_hidden(up, down, devices):
+    share, chunks, width = up.shape
+    up = up.reshape(share, chunks, devices, share).swapaxes(1, 2).reshape(share, chunks * width)
+    return up, down.swapaxes(0, 1).reshape(chunks * share, width)
 
 
 def per_device(
@@ -659,7 +792,7 @@
     )
     down_mine = down_weight.reshape(chunks, share, width).swapaxes(0, 1).reshape(share, chunks * width)
     ffn_mine = cat([up_mine, down_mine], 1)
-    ffn_full = lax.all_gather(ffn_mine, AXES, axis=0, tiled=True)
+    ffn_full = lax.all_gather(ffn_mine, CHIPS if known else AXES, axis=0, tiled=True)
     vector = cat(
         [
             query_bias,
@@ -676,8 +809,8 @@
     matrices = jnp.stack([query_weight, key_weight, value_weight, out_weight])
     tokens = hidden.reshape(count, width)
     groups = 8 + chunks
-    z, y, x, core = place()
     if known:
+        z, y, x, core = place()
         spot = jnp.stack([z, y, x, core]).astype(jnp.int32)
         gathered = gather_attention(matrices, vector)
         out = attend_forward(True, tokens, gathered, pair_lengths, spot, rows_here, share)
@@ -689,45 +822,65 @@
         vec = jnp.pad(vec, ((0, 16 - groups), (0, 0)))
         out = attend_forward(False, tokens, (mats, vec), pair_lengths, spot, rows_here, share)
         queries, keys_all, values_all, mixed, log_totals, first_norm, first_inverse = out
-    layer_out, ffn_grads, grad_first, grad_mixed, grad_out_weight, sums = ffn(
-        ffn_full, first_norm, first_inverse, cotangent.reshape(count, width), mixed, mats, vec
+    layer_out, ffn_keep, ffn_away, grad_middle, first_sums = ffn(
+        ffn_full, first_norm, cotangent.reshape(count, width), vec, spot
     )
-    ffn_owned = lax.psum_scatter(ffn_grads, AXES, scatter_dimension=0, tiled=True).astype(f32)
-    grad_queries, grad_keys, grad_values = attend_back(
-        queries, keys_all, values_all, mixed, log_totals, grad_mixed, pair_lengths, rows_here
+    ffn_got = send(ffn_away, "core") if known else None
+    grad_first, grad_mixed, grad_out_weight, second_sums = middle_back(
+        grad_middle, first_norm, first_inverse, mixed, mats, vec
     )
+
+    def back(gradient):
+        sums = (grad_out_weight, first_sums, second_sums)
+        heads = (queries, keys_all, values_all, mixed, log_totals)
+        return attend_back(known, share, spot, tokens, *heads, gradient, *sums, pair_lengths)
+
     if known:
-        keep, away = weight_blocks(tokens, grad_queries, grad_keys, grad_values, grad_out_weight, sums, spot, share)
-        mats_owned, vectors_owned = scatter_attention(keep, away, 4, share, groups * share)
+        half = width // 2
+        grid = (4, 2, 2, 2 * share, -1)
+        ffn_got, ffn_keep, grad_mixed = phase(ffn_got, ffn_keep, grad_mixed)
+        out = core_stage(ffn_keep.reshape(grid), ffn_got.reshape(grid), spot, chunks * half, False)
+        ffn_got = send(out[0], "y"), send(out[2], "x")
+        *ffn_kept, grad_mixed = phase(out[1], out[3], grad_mixed)
+        *token_grads, keep, away = back(grad_mixed)
+        *ffn_got, keep, away = phase(*ffn_got, keep, away)
+        got = send(away, "core")
+        plane, ffn_kept = plane_stage(ffn_kept, ffn_got, spot)
+        got, *plane = phase(got, *plane)
+        ffn_got = send(plane[0], "x"), send(plane[1], "y")
+        shape = (4, 2, 2, *keep.shape[1:])
+        out = core_stage(keep.reshape(shape), got.reshape(shape), spot, 4 * share, True)
+        attn_got = send(out[0], "y"), send(out[2], "x")
+        *attn_kept, grad_first = phase(out[1], out[3], grad_first)
+        grad_tokens = token_grad(grad_first, token_grads, mats)
+        *ffn_got, grad_tokens = phase(*ffn_got, grad_tokens)
+        ffn_sum = lax.psum_scatter(line_sum(ffn_kept, ffn_got), "z", scatter_dimension=0, tiled=True)
+        attn_got = phase(*attn_got)
+        plane, attn_kept = plane_stage(attn_kept, attn_got, spot)
+        attn_got = send(plane[0], "x"), send(plane[1], "y")
+        attn_got = phase(*attn_got)
+        line, attn_mine = line_stage(attn_kept, attn_got, spot)
+        attn_line = send_line(line)
+        ffn_sum, attn_mine = phase(ffn_sum, attn_mine)
+        ffn_mine = ffn_sum[0].reshape(2, share, 2, chunks, half).transpose(2, 0, 1, 3, 4)
+        ffn_whole = halves_of(ffn_mine.reshape(2, 2, share * chunks, half)).reshape(2, share, chunks, width)
+        up_owned, down_owned = natural_hidden(ffn_whole[0], ffn_whole[1], devices)
+        attn_one, attn_two, attn_three, up_owned, down_owned = phase(*attn_line, up_owned, down_owned)
+        attn_mine = add(attn_mine, attn_one, attn_two, attn_three)
+        mats_owned = halves_of(attn_mine[: 8 * share].reshape(4, 2, share, width // 2))
+        vectors_owned = attn_mine[8 * share, : groups * share]
     else:
-        mat_grads = jnp.stack(
-            [
-                outer_sum(tokens, grad_queries),
-                outer_sum(tokens, grad_keys),
-                outer_sum(tokens, grad_values),
-                grad_out_weight.astype(f32),
-            ]
-        )
-        biases = jnp.stack([jnp.sum(grad_queries.astype(f32), 0), jnp.sum(grad_values.astype(f32), 0)])
-        vector_grads = cat([biases, sums[5:6], sums[3:5], sums[:3], sums[6 : 6 + chunks]])
+        *token_grads, mat_grads, bias_sums = back(grad_mixed)
+        grad_tokens = token_grad(grad_first, token_grads, mats)
+        ffn_grads = jnp.stack([ffn_keep, ffn_away]).reshape(2, width, 2, chunks, width // 2)
+        ffn_grads = ffn_grads.transpose(2, 1, 3, 0, 4).reshape(2, width, chunks * width)
+        ffn_whole = lax.psum_scatter(ffn_grads, AXES, scatter_dimension=1, tiled=True).astype(f32)
+        up_owned, down_owned = natural_hidden(*ffn_whole.reshape(2, share, chunks, width), devices)
+        mat_grads = cat([mat_grads, grad_out_weight[None]])
+        vector_grads = cat(natural_rows([bias_sums[0:1], bias_sums[1:2]], first_sums, second_sums))
         vector_grads = vector_grads.reshape(groups, devices, share).swapaxes(0, 1).reshape(devices, groups * share)
         mats_owned, vectors_owned = scatter_attention_any(mat_grads, vector_grads)
-    grad_tokens = (
-        grad_first
-        + back_product(grad_queries, mats[0])
-        + back_product(grad_keys, mats[1])
-        + back_product(grad_values, mats[2])
-    )
-    own = vectors_owned.reshape(8 + chunks, share)
-    up_owned = (
-        ffn_owned[:, : chunks * width]
-        .reshape(share, chunks, devices, share)
-        .swapaxes(1, 2)
-        .reshape(share, chunks * width)
-    )
-    down_owned = (
-        ffn_owned[:, chunks * width :].reshape(share, chunks, width).swapaxes(0, 1).reshape(chunks * share, width)
-    )
+    own = vectors_owned.reshape(groups, share)
     return (
         layer_out.reshape(hidden.shape),
         grad_tokens.reshape(hidden.shape),
@@ -751,7 +904,10 @@
 
 def solution(mesh):
     known = dict(mesh.shape) == {"dp": 8, "shard": 4}
-    cube, flat, line = P(AXES, None, None), P(AXES, None), P(AXES)
+    axes = AXES
+    if known:
+        mesh, axes = Mesh(mesh.devices.reshape(4, 2, 2, 2), CHIPS), CHIPS
+    cube, flat, line = P(axes, None, None), P(axes, None), P(axes)
     return jax.shard_map(
         lambda *args: per_device(known, *args),
         mesh=mesh,

time: 332 us -> 290 us (0.87)
  waiting for transfers between devices: 153 us -> 91.9 us
  Pallas kernels: 108 us -> 125 us
  matrix products: 6.15 us -> 0 us
  local copies, waits for them, and re-layouts: 17.8 us -> 23.3 us
    reduce_scatter x1, waiting for transfers between devices: 52.5 us -> 1.02 us  [per_device(): lax.psum_scatter(line_sum(ffn_kept, ffn_got), 'z', scatter_dimension=0, t...]
    pallas_call x2 -> x9, Pallas kernels: 30.5 us -> 59.2 us  [the longest x1 27 us: attend_back(): pl.pallas_call(functools.partial(back_kernel, known, block, share), grid_...]
    pallas_call x1, Pallas kernels: 56.3 us -> 46.1 us  [ffn(): pl.pallas_call(functools.partial(ffn_kernel, chunks, size), grid=(1,), in...]
    ppermute x21 -> x27, waiting for transfers between devices: 85.4 us -> 76.5 us  [send(): return lax.ppermute(values, CHIPS, MOVES[move])]
    dot_general x3 -> x0, matrix products: 6.15 us -> none  [back_product(): jnp.einsum('tb,ab->ta', grads, weights, preferred_element_type=jnp.float32)]
    unnamed x57 -> x65, local copies, waits for them, and re-layouts: 2.04 us -> 6.73 us
    ppermute x21 -> x27, starting transfers between devices: 24.3 us -> 26.1 us  [send(): return lax.ppermute(values, CHIPS, MOVES[move])]
  transfers between devices with their start and end apart: 23 -> 29, of which waited for: 16 -> 19; matrix products, arithmetic and copies ran while one was open for 4% -> 3% of each run, Pallas kernels for 16% -> 26%
where the time goes in v3:
time: 290 us; the launch traced here: 285 us
  Pallas kernels  125 us (43%)
  waiting for transfers between devices  91.9 us (32%)
  starting transfers between devices  26.2 us (9%)
  local copies, waits for them, and re-layouts  23.3 us (8%)
  between operations  15.1 us (5%)
  other arithmetic  3.18 us (1%)
    ppermute x27, waiting for transfers between devices, send(): return lax.ppermute(values, CHIPS, MOVES[move])  76.5 us
    pallas_call x1, Pallas kernels, ffn(): pl.pallas_call(functools.partial(ffn_kernel, chunks, size), grid=(1,), in...  46.1 us
    pallas_call x1, Pallas kernels, attend_back(): pl.pallas_call(functools.partial(back_kernel, known, block, share), grid_...  27 us
    ppermute x27, starting transfers between devices, send(): return lax.ppermute(values, CHIPS, MOVES[move])  26.1 us
    pallas_call x1, Pallas kernels, attend_forward(): pl.pallas_call(functools.partial(attend_kernel, known, block, share), gri...  20.1 us
    all_gather x1, waiting for transfers between devices, per_device(): lax.all_gather(ffn_mine, CHIPS if known else AXES, axis=0, tiled=True)  14.3 us
    pallas_call x1, Pallas kernels, middle_back(): pl.pallas_call(middle_kernel, grid=(tokens // size,), in_specs=[tile, til...  10.4 us
    pallas_call x1, Pallas kernels, token_grad(): pl.pallas_call(token_kernel, grid=(tokens // size,), in_specs=[tile] * 4...  8.96 us
  transfers between devices with their start and end apart: 29, of which 19 were waited for; matrix products, arithmetic and copies ran while one was open for 3% of the time, Pallas kernels for 26%

profile of v3, /device:TPU:0, one launch (start us, length us, event | category | flops | bytes accessed | tf_op | source)
XLA Modules:
  0.0 285.0 jit_solution(524421362152740989)
XLA Ops:
  8.2 2.1 reshape.116
  14.3 5.0 %collective-permute-start.3 = (bf16[208,384]{1,0:T(8,128)(2,1)S(1)}, bf16[208,384]{1,0:T(8,128)(2,1)S(1)}, u32[]{:S(2)}, u32[]{:S(2)}) collective-permute-start(bf16[208,384]{1,0:T(8,128)(2,1)S(1)} %fusion.1), channel_id=1, source_target_pairs={{0,24},{1,25},{2,26},{3,27},{4,28},{5,29},{6,30},{7,31},{8,0},{9,1... | collective-permute-start | bytes 479240 | tf_op jit(solution)/shard_map/ppermute | solution.py:46
  20.4 3.5 %collective-permute-done.3 = bf16[208,384]{1,0:T(8,128)(2,1)S(1)} collective-permute-done((bf16[208,384]{1,0:T(8,128)(2,1)S(1)}, bf16[208,384]{1,0:T(8,128)(2,1)S(1)}, u32[]{:S(2)}, u32[]{:S(2)}) %collective-permute-start.3) | collective-permute-done | bytes 159776 | tf_op jit(solution)/shard_map/ppermute | solution.py:46
  23.9 14.6 %collective-permute-done.2 = bf16[208,384]{1,0:T(8,128)(2,1)S(1)} collective-permute-done((bf16[208,384]{1,0:T(8,128)(2,1)S(1)}, bf16[208,384]{1,0:T(8,128)(2,1)S(1)}, u32[]{:S(2)}, u32[]{:S(2)}) %collective-permute-start.2) | collective-permute-done | bytes 159776 | tf_op jit(solution)/shard_map/ppermute | solution.py:46
  41.7 5.6 %collective-permute-done.4 = bf16[4,96,384]{2,1,0:T(8,128)(2,1)S(1)} collective-permute-done((bf16[4,96,384]{2,1,0:T(8,128)(2,1)S(1)}, bf16[4,96,384]{2,1,0:T(8,128)(2,1)S(1)}, u32[]{:S(2)}, u32[]{:S(2)}) %collective-permute-start.4) | collective-permute-done | bytes 294944 | tf_op jit(solution)/shard_map/ppermute | solution.py:46
  51.3 14.5 %collective-permute-done.6.refs_1_ = bf16[8,96,384]{2,1,0:T(8,128)(2,1)} collective-permute-done((bf16[8,96,384]{2,1,0:T(8,128)(2,1)S(1)}, bf16[8,96,384]{2,1,0:T(8,128)(2,1)}, u32[]{:S(2)}, u32[]{:S(2)}) %collective-permute-start.6) | collective-permute-done | bytes 589856 | tf_op jit(solution)/shard_map/ppermute | solution.py:46
  65.8 6.2 %collective-permute-done.7.refs_3_ = bf16[8,112,384]{2,1,0:T(8,128)(2,1)S(1)} collective-permute-done((bf16[8,112,384]{2,1,0:T(8,128)(2,1)S(1)}, bf16[8,112,384]{2,1,0:T(8,128)(2,1)S(1)}, u32[]{:S(2)}, u32[]{:S(2)}) %collective-permute-start.7) | collective-permute-done | bytes 688160 | tf_op jit(solution)/shard_map/ppermute | solution.py:46
  73.1 2.2 collective-permute-done.10.refs_5_
  76.2 20.1 %attend.1 = (bf16[1024,768]{1,0:T(8,128)(2,1)}, bf16[1024,768]{1,0:T(8,128)(2,1)}, bf16[1024,768]{1,0:T(8,128)(2,1)}, bf16[1024,768]{1,0:T(8,128)(2,1)}, f32[2,1...) custom-call(s32[2,8]{1,0:T(2,128)} %lengths.3, ...), custom_call_target="tpu_custom_call" | custom-call | flops 10000000000 | bytes 20000000 | tf_op jit(solution)/shard_map/attend/pallas_call | solution.py:299
  96.3 14.3 %all-gather.2.cloned.1.call-done.weights = bf16[768,6144]{1,0:T(8,128)(2,1)} async-done(((bf16[24,6144]{1,0:T(8,128)(2,1)}), bf16[768,6144]{1,0:T(8,128)(2,1)}) %all-gather.2.cloned.1.call-update) | async-done | bytes 9437200 | tf_op jit(solution)/shard_map/all_gather | solution.py:795
  110.6 46.1 %ffn.1 = (bf16[1024,768]{1,0:T(8,128)(2,1)}, bf16[768,3072]{1,0:T(8,128)(2,1)}, bf16[768,3072]{1,0:T(8,128)(2,1)}, f32[1024,768]{1,0:T(8,128)}, f32[8,768]{1,0:T(8,128)}) custom-call(s32[4]{0:T(128)} %pad_add_fusion.spot, bf16[768,6144]{1,0:T(8,128)(2,1)} %all-gather.2.cloned.1.call-done.weights, f32[1024,768]{1,0:T(8,128)} %get-tuple-element.116.normed, ...), custom_call_target="tpu_custom_call" | custom-call | flops 32000000000 | bytes 30000000 | tf_op jit(solution)/shard_map/ffn/pallas_call | solution.py:550
  157.1 10.4 %middle_back.1 = (f32[1024,768]{1,0:T(8,128)}, bf16[1024,768]{1,0:T(8,128)(2,1)}, bf16[768,768]{1,0:T(8,128)(2,1)}, f32[8,768]{1,0:T(8,128)}) custom-call(f32[1024,768]{1,0:T(8,128)} %get-tuple-element.121.grad_middle, f32[1024,768]{1,0:T(8,128)} %get-tuple-element.116.normed, f32[1024,128]{1,0:T(8,128)} %get-tuple-element.122.inverse, ...), custom_call_target="tpu_custom_call" | custom-call | flops 5000000000 | bytes 10000000 | tf_op jit(solution)/shard_map/middle_back/pallas_call | solution.py:602
  167.6 2.3 copy-done
  170.0 5.1 %core_stage.2 = (bf16[4,2,48,1536]{3,2,1,0:T(8,128)(2,1)}, bf16[4,2,48,1536]{3,2,1,0:T(8,128)(2,1)S(1)}, bf16[4,2,48,1536]{3,2,1,0:T(8,128)(2,1)}, bf16[4,2,48,1536]{3,2,1,0:T(8,128)(2,1)S(1)}) custom-call(s32[4]{0:T(128)S(1)} %copy-done.6, bf16[4,2,2,48,3072]{4,3,2,1,0:T(8,128)(2,1)S(1)} %bitcast.75, bf16[4,2,2,48,3072]{4,3,2,1,0:T(8,128)(2,1)} %bitcast.20.got), custom_call_target="tpu_custom_call" | custom-call | flops 1000000 | bytes 10000000 | tf_op jit(solution)/shard_map/core_stage/pallas_call | solution.py:645
  177.0 27.0 %attend_back.1 = (bf16[1024,768]{1,0:T(8,128)(2,1)}, bf16[1024,768]{1,0:T(8,128)(2,1)}, bf16[1024,768]{1,0:T(8,128)(2,1)}, bf16[16,208,384]{2,1,0:T(8,128)(2,1)}, bf16[16,208,384]{2,1,0:T(8,128)(2,1)}) custom-call(s32[2,8]{1,0:T(2,128)} %lengths.3, s32[4]{0:T(128)} %pad_add_fusion.spot, bf16[1024,768]{1,0:T(8,128)(2,1)} %bitcast.106, ...), custom_call_target="tpu_custom_call" | custom-call | flops 20000000000 | bytes 20000000 | tf_op jit(solution)/shard_map/attend_back/pallas_call | solution.py:429
  205.4 4.0 %plane_stage.2 = (bf16[4,48,1536]{2,1,0:T(8,128)(2,1)}, bf16[4,48,1536]{2,1,0:T(8,128)(2,1)S(1)}, bf16[4,48,1536]{2,1,0:T(8,128)(2,1)}, bf16[4,48,1536]{2,1,0:T(8,128)(2,1)S(1)}) custom-call(s32[4]{0:T(128)S(1)} %copy-done.7, bf16[4,2,48,1536]{3,2,1,0:T(8,128)(2,1)S(1)} %get-tuple-element.144.mine_first, ...), custom_call_target="tpu_custom_call" | custom-call | flops 1000000 | bytes 5000000 | tf_op jit(solution)/shard_map/plane_stage/pallas_call | solution.py:672
  215.0 9.0 %token_grad.1 = f32[1024,768]{1,0:T(8,128)} custom-call(f32[1024,768]{1,0:T(8,128)} %get-tuple-element.157.first, bf16[1024,768]{1,0:T(8,128)(2,1)} %get-tuple-element.158.dq, bf16[1024,768]{1,0:T(8,128)(2,1)} %get-tuple-element.159.dk, bf16[1024,768]{1,0:T(8,128)(2,1)} %get-tuple-element.160.dv, bf16[4,768,768]{2,1,0:T(8,128)(2,1)} %get-tuple-element.124.out_mat.w), custom_call_target="tpu_custom_call" | custom-call | flops 4000000000 | bytes 10000000 | tf_op jit(solution)/shard_map/token_grad/pallas_call | solution.py:746
  223.9 2.2 collective-permute-done.16.got_first
  230.1 13.2 %collective-permute-done.18.got_first = bf16[4,2,96,384]{3,2,1,0:T(8,128)(2,1)S(1)} collective-permute-done((bf16[4,2,96,384]{3,2,1,0:T(8,128)(2,1)S(1)}, bf16[4,2,96,384]{3,2,1,0:T(8,128)(2,1)S(1)}, u32[]{:S(2)}, u32[]{:S(2)}) %collective-permute-start.18) | collective-permute-done | bytes 589856 | tf_op jit(solution)/shard_map/ppermute | solution.py:46
  247.7 6.1 %collective-permute-done.20.got_first = bf16[4,96,384]{2,1,0:T(8,128)(2,1)S(1)} collective-permute-done((bf16[4,96,384]{2,1,0:T(8,128)(2,1)S(1)}, bf16[4,96,384]{2,1,0:T(8,128)(2,1)S(1)}, u32[]{:S(2)}, u32[]{:S(2)}) %collective-permute-start.20) | collective-permute-done | bytes 294944 | tf_op jit(solution)/shard_map/ppermute | solution.py:46
  259.7 2.6 collective-permute-start.24
  264.5 2.4 copy.46
  266.9 4.0 %reshape.129 = f32[24,3072]{1,0:T(8,128)} reshape(f32[24,32,4,24]{3,2,1,0:T(4,128)} %copy.46) | data formatting | bytes 589824 | tf_op jit(solution)/shard_map/reshape | solution.py:760
  270.9 2.5 collective-permute-done.23
  (148 shorter events, 44.8 us)
Async XLA Ops:
  7.2 103.5 %all-gather.2.cloned.1.call-start = ((), (), s32[]{:S(2)}) async-start(), calls=%async_computation.1 | async-start | bytes 9732096 | tf_op jit(solution)/shard_map/all_gather | solution.py:795
  12.7 243.2 %reduce-scatter.2.cloned.1.call-start = ((), (), s32[]{:S(2)}) async-start(), calls=%async_computation.2 | async-start | bytes 1474560 | tf_op jit(solution)/shard_map/reduce_scatter | solution.py:857
  14.3 9.6 %collective-permute-start.3 = (bf16[208,384]{1,0:T(8,128)(2,1)S(1)}, bf16[208,384]{1,0:T(8,128)(2,1)S(1)}, u32[]{:S(2)}, u32[]{:S(2)}) collective-permute-start(bf16[208,384]{1,0:T(8,128)(2,1)S(1)} %fusion.1), channel_id=1, source_target_pairs={{0,24},{1,25},{2,26},{3,27},{4,28},{5,29},{6,30},{7,31},{8,0},{9,1... | collective-permute-start | bytes 479240 | tf_op jit(solution)/shard_map/ppermute | solution.py:46
  19.3 19.1 %collective-permute-start.2 = (bf16[208,384]{1,0:T(8,128)(2,1)S(1)}, bf16[208,384]{1,0:T(8,128)(2,1)S(1)}, u32[]{:S(2)}, u32[]{:S(2)}) collective-permute-start(bf16[208,384]{1,0:T(8,128)(2,1)S(1)} %fusion.1), channel_id=1, source_target_pairs={{0,16},{1,17},{2,18},{3,19},{4,20},{5,21},{6,22},{7,23},{8,24},{9,... | collective-permute-start | bytes 479240 | tf_op jit(solution)/shard_map/ppermute | solution.py:46
  19.4 19.1 %collective-permute-start.1 = (bf16[208,384]{1,0:T(8,128)(2,1)S(1)}, bf16[208,384]{1,0:T(8,128)(2,1)S(1)}, u32[]{:S(2)}, u32[]{:S(2)}) collective-permute-start(bf16[208,384]{1,0:T(8,128)(2,1)S(1)} %fusion.1), channel_id=1, source_target_pairs={{0,8},{1,9},{2,10},{3,11},{4,12},{5,13},{6,14},{7,15},{8,16},{9,17... | collective-permute-start | bytes 479240 | tf_op jit(solution)/shard_map/ppermute | solution.py:46
  38.5 8.8 %collective-permute-start.5 = (bf16[4,112,384]{2,1,0:T(8,128)(2,1)S(1)}, bf16[4,112,384]{2,1,0:T(8,128)(2,1)S(1)}, u32[]{:S(2)}, u32[]{:S(2)}) collective-permute-start(bf16[4,112,384]{2,1,0:T(8,128)(2,1)S(1)} %pad_maximum_fusion), channel_id=1, source_target_pairs={{0,4},{1,5},{2,6},{3,7},{4,0},{5,1},{6,2},{7,3},{8,12},{9,13},{10,... | collective-permute-start | bytes 1032200 | tf_op jit(solution)/shard_map/ppermute | solution.py:46
  40.3 7.1 %collective-permute-start.4 = (bf16[4,96,384]{2,1,0:T(8,128)(2,1)S(1)}, bf16[4,96,384]{2,1,0:T(8,128)(2,1)S(1)}, u32[]{:S(2)}, u32[]{:S(2)}) collective-permute-start(bf16[4,96,384]{2,1,0:T(8,128)(2,1)S(1)} %pad_maximum_fusion.3), channel_id=1, source_target_pairs={{0,2},{1,3},{2,0},{3,1},{4,6},{5,7},{6,4},{7,5},{8,10},{9,11},{10,... | collective-permute-start | bytes 884744 | tf_op jit(solution)/shard_map/ppermute | solution.py:46
  47.5 18.3 %collective-permute-start.9 = (bf16[8,112,384]{2,1,0:T(8,128)(2,1)S(1)}, bf16[8,112,384]{2,1,0:T(8,128)(2,1)S(1)}, u32[]{:S(2)}, u32[]{:S(2)}) collective-permute-start(bf16[8,112,384]{2,1,0:T(8,128)(2,1)S(1)} %constant_dynamic-update-slice_fusion.2.refs_2_), channel_id=1, source_target_pairs={{0,1},{1,0},{2,3},{3,2},{4,5},{5,4},{6,7},{7,6},{8,9},{9,8},{10,11... | collective-permute-start | bytes 2064392 | tf_op jit(solution)/shard_map/ppermute | solution.py:46
  47.5 24.5 %collective-permute-start.7 = (bf16[8,112,384]{2,1,0:T(8,128)(2,1)S(1)}, bf16[8,112,384]{2,1,0:T(8,128)(2,1)S(1)}, u32[]{:S(2)}, u32[]{:S(2)}) collective-permute-start(bf16[8,112,384]{2,1,0:T(8,128)(2,1)S(1)} %constant_dynamic-update-slice_fusion.2.refs_2_), channel_id=1, source_target_pairs={{0,2},{1,3},{2,0},{3,1},{4,6},{5,7},{6,4},{7,5},{8,10},{9,11},{10,... | collective-permute-start | bytes 2064392 | tf_op jit(solution)/shard_map/ppermute | solution.py:46
  49.4 16.3 %collective-permute-start.6 = (bf16[8,96,384]{2,1,0:T(8,128)(2,1)S(1)}, bf16[8,96,384]{2,1,0:T(8,128)(2,1)}, u32[]{:S(2)}, u32[]{:S(2)}) collective-permute-start(bf16[8,96,384]{2,1,0:T(8,128)(2,1)S(1)} %constant_dynamic-update-slice_fusion.refs_0_), channel_id=1, source_target_pairs={{0,4},{1,5},{2,6},{3,7},{4,0},{5,1},{6,2},{7,3},{8,12},{9,13},{10,... | collective-permute-start | bytes 1769480 | tf_op jit(solution)/shard_map/ppermute | solution.py:46
  156.8 10.8 %collective-permute-start.12 = (bf16[768,3072]{1,0:T(8,128)(2,1)}, bf16[768,3072]{1,0:T(8,128)(2,1)}, u32[]{:S(2)}, u32[]{:S(2)}) collective-permute-start(bf16[768,3072]{1,0:T(8,128)(2,1)} %get-tuple-element.119), channel_id=1, source_target_pairs={{0,1},{1,0},{2,3},{3,2},{4,5},{5,4},{6,7},{7,6},{8,9},{9,8},{10,11... | collective-permute-start | bytes 14155784 | tf_op jit(solution)/shard_map/ppermute | solution.py:46
  175.0 29.0 %collective-permute-start.13 = (bf16[4,2,48,1536]{3,2,1,0:T(8,128)(2,1)}, bf16[4,2,48,1536]{3,2,1,0:T(8,128)(2,1)S(1)}, u32[]{:S(2)}, u32[]{:S(2)}) collective-permute-start(bf16[4,2,48,1536]{3,2,1,0:T(8,128)(2,1)} %get-tuple-element.128), channel_id=1, source_target_pairs={{0,4},{1,5},{2,6},{3,7},{4,0},{5,1},{6,2},{7,3},{8,12},{9,13},{10,... | collective-permute-start | bytes 3538952 | tf_op jit(solution)/shard_map/ppermute | solution.py:46
  176.5 28.2 %collective-permute-start.14 = (bf16[4,2,48,1536]{3,2,1,0:T(8,128)(2,1)}, bf16[4,2,48,1536]{3,2,1,0:T(8,128)(2,1)}, u32[]{:S(2)}, u32[]{:S(2)}) collective-permute-start(bf16[4,2,48,1536]{3,2,1,0:T(8,128)(2,1)} %get-tuple-element.129), channel_id=1, source_target_pairs={{0,2},{1,3},{2,0},{3,1},{4,6},{5,7},{6,4},{7,5},{8,10},{9,11},{10,... | collective-permute-start | bytes 3538952 | tf_op jit(solution)/shard_map/ppermute | solution.py:46
  204.6 5.7 %collective-permute-start.15 = (bf16[16,208,384]{2,1,0:T(8,128)(2,1)}, bf16[16,208,384]{2,1,0:T(8,128)(2,1)S(1)}, u32[]{:S(2)}, u32[]{:S(2)}) collective-permute-start(bf16[16,208,384]{2,1,0:T(8,128)(2,1)} %get-tuple-element.143), channel_id=1, source_target_pairs={{0,1},{1,0},{2,3},{3,2},{4,5},{5,4},{6,7},{7,6},{8,9},{9,8},{10,11... | collective-permute-start | bytes 7667720 | tf_op jit(solution)/shard_map/ppermute | solution.py:46
  210.3 15.8 %collective-permute-start.16 = (bf16[4,48,1536]{2,1,0:T(8,128)(2,1)}, bf16[4,48,1536]{2,1,0:T(8,128)(2,1)S(1)}, u32[]{:S(2)}, u32[]{:S(2)}) collective-permute-start(bf16[4,48,1536]{2,1,0:T(8,128)(2,1)} %get-tuple-element.150), channel_id=1, source_target_pairs={{0,2},{1,3},{2,0},{3,1},{4,6},{5,7},{6,4},{7,5},{8,10},{9,11},{10,... | collective-permute-start | bytes 1769480 | tf_op jit(solution)/shard_map/ppermute | solution.py:46
  211.3 15.5 %collective-permute-start.17 = (bf16[4,48,1536]{2,1,0:T(8,128)(2,1)}, bf16[4,48,1536]{2,1,0:T(8,128)(2,1)S(1)}, u32[]{:S(2)}, u32[]{:S(2)}) collective-permute-start(bf16[4,48,1536]{2,1,0:T(8,128)(2,1)} %get-tuple-element.151), channel_id=1, source_target_pairs={{0,4},{1,5},{2,6},{3,7},{4,0},{5,1},{6,2},{7,3},{8,12},{9,13},{10,... | collective-permute-start | bytes 1769480 | tf_op jit(solution)/shard_map/ppermute | solution.py:46
  228.0 16.8 %collective-permute-start.19 = (bf16[4,2,112,384]{3,2,1,0:T(8,128)(2,1)}, bf16[4,2,112,384]{3,2,1,0:T(8,128)(2,1)S(1)}, u32[]{:S(2)}, u32[]{:S(2)}) collective-permute-start(bf16[4,2,112,384]{3,2,1,0:T(8,128)(2,1)} %copy-done.10), channel_id=1, source_target_pairs={{0,2},{1,3},{2,0},{3,1},{4,6},{5,7},{6,4},{7,5},{8,10},{9,11},{10,... | collective-permute-start | bytes 2064392 | tf_op jit(solution)/shard_map/ppermute | solution.py:46
  229.1 14.2 %collective-permute-start.18 = (bf16[4,2,96,384]{3,2,1,0:T(8,128)(2,1)S(1)}, bf16[4,2,96,384]{3,2,1,0:T(8,128)(2,1)S(1)}, u32[]{:S(2)}, u32[]{:S(2)}) collective-permute-start(bf16[4,2,96,384]{3,2,1,0:T(8,128)(2,1)S(1)} %get-tuple-element.167), channel_id=1, source_target_pairs={{0,4},{1,5},{2,6},{3,7},{4,0},{5,1},{6,2},{7,3},{8,12},{9,13},{10,... | collective-permute-start | bytes 1769480 | tf_op jit(solution)/shard_map/ppermute | solution.py:46
  245.7 8.4 %collective-permute-start.21 = (bf16[4,112,384]{2,1,0:T(8,128)(2,1)S(1)}, bf16[4,112,384]{2,1,0:T(8,128)(2,1)S(1)}, u32[]{:S(2)}, u32[]{:S(2)}) collective-permute-start(bf16[4,112,384]{2,1,0:T(8,128)(2,1)S(1)} %get-tuple-element.174), channel_id=1, source_target_pairs={{0,4},{1,5},{2,6},{3,7},{4,0},{5,1},{6,2},{7,3},{8,12},{9,13},{10,... | collective-permute-start | bytes 1032200 | tf_op jit(solution)/shard_map/ppermute | solution.py:46
  246.8 7.0 %collective-permute-start.20 = (bf16[4,96,384]{2,1,0:T(8,128)(2,1)S(1)}, bf16[4,96,384]{2,1,0:T(8,128)(2,1)S(1)}, u32[]{:S(2)}, u32[]{:S(2)}) collective-permute-start(bf16[4,96,384]{2,1,0:T(8,128)(2,1)S(1)} %get-tuple-element.173), channel_id=1, source_target_pairs={{0,2},{1,3},{2,0},{3,1},{4,6},{5,7},{6,4},{7,5},{8,10},{9,11},{10,... | collective-permute-start | bytes 884744 | tf_op jit(solution)/shard_map/ppermute | solution.py:46
  257.9 4.4 %collective-permute-start.25 = (bf16[2,96,384]{2,1,0:T(8,128)(2,1)S(1)}, bf16[2,96,384]{2,1,0:T(8,128)(2,1)S(1)}, u32[]{:S(2)}, u32[]{:S(2)}) collective-permute-start(bf16[2,96,384]{2,1,0:T(8,128)(2,1)S(1)} %bitcast.98), channel_id=1, source_target_pairs={{0,1},{1,0},{2,3},{3,2},{4,5},{5,4},{6,7},{7,6},{8,9},{9,8},{10,11... | collective-permute-start | bytes 442376 | tf_op jit(solution)/shard_map/ppermute | solution.py:46
  258.0 12.9 %collective-permute-start.22 = (bf16[208,384]{1,0:T(8,128)(2,1)S(1)}, bf16[208,384]{1,0:T(8,128)(2,1)S(1)}, u32[]{:S(2)}, u32[]{:S(2)}) collective-permute-start(bf16[208,384]{1,0:T(8,128)(2,1)S(1)} %get-tuple-element.180), channel_id=1, source_target_pairs={{0,8},{1,9},{2,10},{3,11},{4,12},{5,13},{6,14},{7,15},{8,16},{9,17... | collective-permute-start | bytes 479240 | tf_op jit(solution)/shard_map/ppermute | solution.py:46
  258.5 14.8 %collective-permute-start.23 = (bf16[208,384]{1,0:T(8,128)(2,1)S(1)}, bf16[208,384]{1,0:T(8,128)(2,1)}, u32[]{:S(2)}, u32[]{:S(2)}) collective-permute-start(bf16[208,384]{1,0:T(8,128)(2,1)S(1)} %get-tuple-element.181), channel_id=1, source_target_pairs={{0,16},{1,17},{2,18},{3,19},{4,20},{5,21},{6,22},{7,23},{8,24},{9,... | collective-permute-start | bytes 479240 | tf_op jit(solution)/shard_map/ppermute | solution.py:46
  259.7 13.6 %collective-permute-start.24 = (bf16[208,384]{1,0:T(8,128)(2,1)S(1)}, bf16[208,384]{1,0:T(8,128)(2,1)}, u32[]{:S(2)}, u32[]{:S(2)}) collective-permute-start(bf16[208,384]{1,0:T(8,128)(2,1)S(1)} %get-tuple-element.182), channel_id=1, source_target_pairs={{0,24},{1,25},{2,26},{3,27},{4,28},{5,29},{6,30},{7,31},{8,0},{9,1... | collective-permute-start | bytes 479240 | tf_op jit(solution)/shard_map/ppermute | solution.py:46
  (35 other events, 212.1 us)
Sparse Core Ops, SparseCore 0:
  12.8 97.7 all-gather.1
  228.1 27.6 reduce-scatter.1
